TPU v7x, 32 devices: a whole 2x2x4 slice. The times are simulated.
32 devices in a mesh: seq: 4 (over z), ctx: 8 (over y, x, core).
Axes of the slice: x: 2, y: 2, z: 4, core: 2. Of those that a mesh axis runs over, the one named last changes fastest.
Arguments:
- tokens: bfloat16 [6144, 2048], P(('seq', 'ctx')), may hold values from -6 to 6
- block_ids: int32 [4, 16], P('seq'), may hold values from 0 to 15, as said below
- cotangent: bfloat16 [6144, 2048], P(('seq', 'ctx')), may hold values from -6 to 6
- norm1_gain: bfloat16 [2048], P('seq'), may hold values from 0.25 to 1.75
- norm1_bias: bfloat16 [2048], P('seq'), may hold values from -3 to 3
- norm2_gain: bfloat16 [2048], P('seq'), may hold values from 0.25 to 1.75
- norm2_bias: bfloat16 [2048], P('seq'), may hold values from -3 to 3
- w_qkv: bfloat16 [2048, 6144], P('seq'), may hold values from -0.125 to 0.125
- b_qkv: bfloat16 [6144], P('seq'), may hold values from -3 to 3
- w_dense: bfloat16 [2048, 2048], P('seq'), may hold values from -1 to 1
- b_dense: bfloat16 [2048], P('seq'), may hold values from -3 to 3
- w_in: bfloat16 [2048, 8192], P('seq'), may hold values from -0.125 to 0.125
- b_in: bfloat16 [8192], P('seq'), may hold values from -3 to 3
- w_out: bfloat16 [8192, 2048], P('seq'), may hold values from -0.0625 to 0.0625
- b_out: bfloat16 [2048], P('seq'), may hold values from -3 to 3
Outputs:
- output: bfloat16 [6144, 2048], P(('seq', 'ctx'))
- grad_tokens: bfloat16 [6144, 2048], P(('seq', 'ctx'))
- grad_norm1_gain: float32 [2048], P('seq')
- grad_norm1_bias: float32 [2048], P('seq')
- grad_norm2_gain: float32 [2048], P('seq')
- grad_norm2_bias: float32 [2048], P('seq')
- grad_w_qkv: float32 [2048, 6144], P('seq')
- grad_b_qkv: float32 [6144], P('seq')
- grad_w_dense: float32 [2048, 2048], P('seq')
- grad_b_dense: float32 [2048], P('seq')
- grad_w_in: float32 [2048, 8192], P('seq')
- grad_b_in: float32 [8192], P('seq')
- grad_w_out: float32 [8192, 2048], P('seq')
- grad_b_out: float32 [2048], P('seq')
Inputs may be any that keep to these rules, and one draw needn't show every extreme that they name: In each row of block_ids (one sequence), the slots 2 * j and 2 * j + 1 hold two blocks whose numbers sum to 15, and every block number appears once in the row.
All inputs are finite; a program needn't handle non-finite values.
Results may differ from a plain program's by a relative error of at most 0.011.
Values may be sent and summed in bfloat16 or wider, within the bound.
A program may use at most 408 MiB of HBM per device.

v0:
```python
from functools import partial
import math

import jax
import jax.numpy as jnp
from jax import lax
from jax.sharding import PartitionSpec as P

H = 8
HD = 256
ROT = 64
BLOCK = 96


EPSILON = 1e-05
ROT_BASE = 10000.0


def layer_norm(values, norm_gain, offset):
    center = values - jnp.mean(values, axis=-1, keepdims=True)
    spread = jnp.mean(center * center, axis=-1, keepdims=True)
    return center * lax.rsqrt(spread + EPSILON) * norm_gain + offset


def rotate(vectors, positions, rot_dims):
    half_rot = rot_dims // 2
    inverse_freq = jnp.power(ROT_BASE, -(jnp.arange(half_rot, dtype=jnp.float32) * 2.0) / rot_dims)
    angles = positions.astype(jnp.float32)[:, None] * inverse_freq[None, :]
    cosine = jnp.cos(angles)[:, None, :]
    sine_part = jnp.sin(angles)[:, None, :]
    first_half = vectors[..., :half_rot]
    second = vectors[..., half_rot:rot_dims]
    return jnp.concatenate(
        [
            first_half * cosine - second * sine_part,
            second * cosine + first_half * sine_part,
            vectors[..., rot_dims:],
        ],
        axis=-1,
    )


def masked_scores(query_part, query_pos, key_part, key_pos):
    raw_scores = jnp.einsum(
        "qhd,khd->hqk", query_part, key_part, preferred_element_type=jnp.float32
    ) * HD ** (-0.5)
    allowed = (query_pos[:, None] >= key_pos[None, :])[None]
    return (jnp.where(allowed, raw_scores, -1e30), allowed)


def softmax_grads(
    query_part, dout_part, total_part, shift_part, query_pos, key_part, value_part, key_pos
):
    scores, allowed = masked_scores(query_part, query_pos, key_part, key_pos)
    probabilities = jnp.where(allowed, jnp.exp(scores - total_part[..., None]), 0.0)
    grad_probs = jnp.einsum(
        "qhd,khd->hqk", dout_part, value_part, preferred_element_type=jnp.float32
    )
    grad_scores = (probabilities * (grad_probs - shift_part[..., None])).astype(jnp.bfloat16)
    return (probabilities, grad_scores)


def on_device(
    tokens,
    block_ids,
    cotangent,
    norm1_gain,
    norm1_bias,
    norm2_gain,
    norm2_bias,
    w_qkv,
    b_qkv,
    w_dense,
    b_dense,
    w_in,
    b_in,
    w_out,
    b_out,
):
    f32 = jnp.float32
    bf16 = jnp.bfloat16
    params = (
        lax.all_gather(norm1_gain, "seq", axis=0, tiled=True),
        lax.all_gather(norm1_bias, "seq", axis=0, tiled=True),
        lax.all_gather(norm2_gain, "seq", axis=0, tiled=True),
        lax.all_gather(norm2_bias, "seq", axis=0, tiled=True),
        lax.all_gather(w_qkv, "seq", axis=0, tiled=True),
        lax.all_gather(b_qkv, "seq", axis=0, tiled=True),
        lax.all_gather(w_dense, "seq", axis=0, tiled=True),
        lax.all_gather(b_dense, "seq", axis=0, tiled=True),
        lax.all_gather(w_in, "seq", axis=0, tiled=True),
        lax.all_gather(b_in, "seq", axis=0, tiled=True),
        lax.all_gather(w_out, "seq", axis=0, tiled=True),
        lax.all_gather(b_out, "seq", axis=0, tiled=True),
    )
    (
        full_gain1,
        full_bias1,
        full_gain2,
        full_bias2,
        full_wqkv,
        full_bqkv,
        full_wdense,
        full_bdense,
        full_win,
        full_bin,
        full_wout,
        full_bout,
    ) = params
    own_rows = tokens.shape[0]
    model_width = H * HD
    scale_attn = HD ** (-0.5)
    inputs = tokens.astype(f32)
    gain_one = full_gain1.astype(f32)
    bias_one = full_bias1.astype(f32)
    gain_two = full_gain2.astype(f32)
    bias_two = full_bias2.astype(f32)
    normed1 = layer_norm(inputs, gain_one, bias_one).astype(bf16)
    normed2 = layer_norm(inputs, gain_two, bias_two).astype(bf16)
    project = jnp.dot(normed1, full_wqkv, preferred_element_type=f32) + full_bqkv.astype(f32)
    slot_count = block_ids.shape[1]
    pos_all = jnp.repeat(block_ids[0], BLOCK) * BLOCK + jnp.tile(
        jnp.arange(BLOCK, dtype=jnp.int32), slot_count
    )
    own_pos = lax.dynamic_slice_in_dim(pos_all, lax.axis_index("ctx") * own_rows, own_rows)
    rotation = partial(rotate, positions=own_pos, rot_dims=ROT)
    query_pre = project[:, :model_width].reshape(own_rows, H, HD)
    key_pre = project[:, model_width : 2 * model_width].reshape(own_rows, H, HD)
    queries = rotation(query_pre).astype(bf16)
    keys_own = rotation(key_pre).astype(bf16).reshape(own_rows, model_width)
    values_own = project[:, 2 * model_width :].astype(bf16)
    keys_all, values_all = (
        lax.all_gather(keys_own, "ctx", axis=0, tiled=True),
        lax.all_gather(values_own, "ctx", axis=0, tiled=True),
    )
    key_rows = keys_all.shape[0]
    key_block = math.gcd(key_rows, 1024)
    block_count = key_rows // key_block
    key_blocks = keys_all.reshape(block_count, key_block, H, HD)
    value_blocks = values_all.reshape(block_count, key_block, H, HD)
    pos_blocks = pos_all.reshape(block_count, key_block)

    def stats_step(running, slices):
        run_max, run_sum = running
        key_part, pos_part = slices
        scores, allowed = masked_scores(queries, own_pos, key_part, pos_part)
        new_max = jnp.maximum(run_max, jnp.max(scores, axis=-1))
        exponent = jnp.where(allowed, jnp.exp(scores - new_max[..., None]), 0.0)
        return ((new_max, run_sum * jnp.exp(run_max - new_max) + jnp.sum(exponent, axis=-1)), None)

    initial = (jnp.full((H, own_rows), -1e30, f32), jnp.zeros((H, own_rows), f32))
    (run_max, run_sum), unused = lax.scan(stats_step, initial, (key_blocks, pos_blocks))
    log_total = run_max + jnp.log(run_sum)

    def output_step(summed, slices):
        key_part, value_part, pos_part = slices
        scores, allowed = masked_scores(queries, own_pos, key_part, pos_part)
        probs_low = jnp.where(allowed, jnp.exp(scores - log_total[..., None]), 0.0).astype(bf16)
        return (
            summed + jnp.einsum("hqk,khd->qhd", probs_low, value_part, preferred_element_type=f32),
            None,
        )

    attended, unused = lax.scan(
        output_step, jnp.zeros((own_rows, H, HD), f32), (key_blocks, value_blocks, pos_blocks)
    )
    mixed = attended.reshape(own_rows, model_width).astype(bf16)
    attn_out = jnp.dot(mixed, full_wdense, preferred_element_type=f32) + full_bdense.astype(f32)
    hidden = jnp.dot(normed2, full_win, preferred_element_type=f32) + full_bin.astype(f32)
    active = jax.nn.gelu(hidden, approximate=False).astype(bf16)
    mlp_out = jnp.dot(active, full_wout, preferred_element_type=f32) + full_bout.astype(f32)
    output = (inputs + attn_out + mlp_out).astype(bf16)
    grad_out32 = cotangent.astype(f32)
    grad_b_out = jnp.sum(grad_out32, axis=0)
    back_wdense, back_wqkv = (
        lax.all_gather(w_dense, "seq", axis=0, tiled=True),
        lax.all_gather(w_qkv, "seq", axis=0, tiled=True),
    )
    grad_w_dense = jnp.einsum("nd,ne->de", mixed, cotangent, preferred_element_type=f32)
    grad_mixed = (
        jnp.einsum("ne,de->nd", cotangent, back_wdense, preferred_element_type=f32)
        .astype(bf16)
        .reshape(own_rows, H, HD)
    )

    def shift_step(summed, slices):
        key_part, value_part, pos_part = slices
        scores, allowed = masked_scores(queries, own_pos, key_part, pos_part)
        probabilities = jnp.where(allowed, jnp.exp(scores - log_total[..., None]), 0.0)
        grad_probs = jnp.einsum("qhd,khd->hqk", grad_mixed, value_part, preferred_element_type=f32)
        return (summed + jnp.sum(probabilities * grad_probs, axis=-1), None)

    row_shift, unused = lax.scan(
        shift_step, jnp.zeros((H, own_rows), f32), (key_blocks, value_blocks, pos_blocks)
    )
    zero_rows = jnp.zeros((own_rows, H, HD), f32)

    def grad_step(grad_query, slices):
        key_part, value_part, pos_part = slices
        probabilities, grad_scores = softmax_grads(
            queries, grad_mixed, log_total, row_shift, own_pos, key_part, value_part, pos_part
        )
        grad_query = (
            grad_query
            + jnp.einsum("hqk,khd->qhd", grad_scores, key_part, preferred_element_type=f32)
            * scale_attn
        )
        grad_key = (
            jnp.einsum("hqk,qhd->khd", grad_scores, queries, preferred_element_type=f32)
            * scale_attn
        )
        grad_value = jnp.einsum(
            "hqk,qhd->khd", probabilities.astype(bf16), grad_mixed, preferred_element_type=f32
        )
        return (
            grad_query,
            (grad_key.reshape(key_block, model_width), grad_value.reshape(key_block, model_width)),
        )

    grad_queries, (key_terms, value_terms) = lax.scan(
        grad_step, zero_rows, (key_blocks, value_blocks, pos_blocks)
    )
    grad_keys, grad_values = (
        lax.psum_scatter(
            key_terms.reshape(key_rows, model_width), "ctx", scatter_dimension=0, tiled=True
        ),
        lax.psum_scatter(
            value_terms.reshape(key_rows, model_width), "ctx", scatter_dimension=0, tiled=True
        ),
    )
    unused, rotation_back = jax.vjp(rotation, query_pre)
    grad_query_pre = rotation_back(grad_queries)[0].reshape(own_rows, model_width)
    grad_key_pre = rotation_back(grad_keys.reshape(own_rows, H, HD))[0].reshape(
        own_rows, model_width
    )
    grad_project = jnp.concatenate([grad_query_pre, grad_key_pre, grad_values], axis=1).astype(bf16)
    grad_w_qkv = jnp.einsum("nd,ne->de", normed1, grad_project, preferred_element_type=f32)
    grad_b_qkv = jnp.sum(grad_project.astype(f32), axis=0)
    grad_normed1 = jnp.einsum("ne,de->nd", grad_project, back_wqkv, preferred_element_type=f32)
    unused, norm_back_one = jax.vjp(layer_norm, inputs, gain_one, bias_one)
    term_one, grad_gain_one, grad_bias_one = norm_back_one(grad_normed1)
    attn_part = (
        lax.psum_scatter(grad_gain_one, ("seq", "ctx"), scatter_dimension=0, tiled=True),
        lax.psum_scatter(grad_bias_one, ("seq", "ctx"), scatter_dimension=0, tiled=True),
        lax.psum_scatter(grad_w_qkv, ("seq", "ctx"), scatter_dimension=0, tiled=True),
        lax.psum_scatter(grad_b_qkv, ("seq", "ctx"), scatter_dimension=0, tiled=True),
        lax.psum_scatter(grad_w_dense, ("seq", "ctx"), scatter_dimension=0, tiled=True),
        lax.psum_scatter(grad_b_out, ("seq", "ctx"), scatter_dimension=0, tiled=True),
    )
    sum_gain_one, sum_bias_one, sum_wqkv, sum_bqkv, sum_wdense, sum_bdense = attn_part
    back_win, back_wout = (
        lax.all_gather(w_in, "seq", axis=0, tiled=True),
        lax.all_gather(w_out, "seq", axis=0, tiled=True),
    )
    grad_w_out = jnp.einsum("nf,nd->fd", active, cotangent, preferred_element_type=f32)
    grad_active = jnp.einsum("nd,fd->nf", cotangent, back_wout, preferred_element_type=f32)
    unused, gelu_back = jax.vjp(partial(jax.nn.gelu, approximate=False), hidden)
    grad_hidden = gelu_back(grad_active)[0].astype(bf16)
    grad_w_in = jnp.einsum("nd,nf->df", normed2, grad_hidden, preferred_element_type=f32)
    grad_b_in = jnp.sum(grad_hidden.astype(f32), axis=0)
    grad_normed2 = jnp.einsum("nf,df->nd", grad_hidden, back_win, preferred_element_type=f32)
    unused, norm_back_two = jax.vjp(layer_norm, inputs, gain_two, bias_two)
    term_two, grad_gain_two, grad_bias_two = norm_back_two(grad_normed2)
    grad_tokens = (grad_out32 + term_one + term_two).astype(bf16)
    mlp_part = (
        lax.psum_scatter(grad_gain_two, ("seq", "ctx"), scatter_dimension=0, tiled=True),
        lax.psum_scatter(grad_bias_two, ("seq", "ctx"), scatter_dimension=0, tiled=True),
        lax.psum_scatter(grad_w_in, ("seq", "ctx"), scatter_dimension=0, tiled=True),
        lax.psum_scatter(grad_b_in, ("seq", "ctx"), scatter_dimension=0, tiled=True),
        lax.psum_scatter(grad_w_out, ("seq", "ctx"), scatter_dimension=0, tiled=True),
        lax.psum_scatter(grad_b_out, ("seq", "ctx"), scatter_dimension=0, tiled=True),
    )
    sum_gain_two, sum_bias_two, sum_win, sum_bin, sum_wout, sum_bout = mlp_part
    owner_part = (
        lax.all_gather(sum_gain_one, "ctx", axis=0, tiled=True),
        lax.all_gather(sum_bias_one, "ctx", axis=0, tiled=True),
        lax.all_gather(sum_gain_two, "ctx", axis=0, tiled=True),
        lax.all_gather(sum_bias_two, "ctx", axis=0, tiled=True),
        lax.all_gather(sum_wqkv, "ctx", axis=0, tiled=True),
        lax.all_gather(sum_bqkv, "ctx", axis=0, tiled=True),
        lax.all_gather(sum_wdense, "ctx", axis=0, tiled=True),
        lax.all_gather(sum_bdense, "ctx", axis=0, tiled=True),
        lax.all_gather(sum_win, "ctx", axis=0, tiled=True),
        lax.all_gather(sum_bin, "ctx", axis=0, tiled=True),
        lax.all_gather(sum_wout, "ctx", axis=0, tiled=True),
        lax.all_gather(sum_bout, "ctx", axis=0, tiled=True),
    )
    (
        total_gain_one,
        total_bias_one,
        total_gain_two,
        total_bias_two,
        total_wqkv,
        total_bqkv,
        total_wdense,
        total_bdense,
        total_win,
        total_bin,
        total_wout,
        total_bout,
    ) = owner_part
    return (
        output,
        grad_tokens,
        total_gain_one,
        total_bias_one,
        total_gain_two,
        total_bias_two,
        total_wqkv,
        total_bqkv,
        total_wdense,
        total_bdense,
        total_win,
        total_bin,
        total_wout,
        total_bout,
    )


def solution(mesh):
    in_specs = (
        P(("seq", "ctx"), None),
        P("seq", None),
        P(("seq", "ctx"), None),
        P("seq"),
        P("seq"),
        P("seq"),
        P("seq"),
        P("seq", None),
        P("seq"),
        P("seq", None),
        P("seq"),
        P("seq", None),
        P("seq"),
        P("seq", None),
        P("seq"),
    )
    out_specs = (
        P(("seq", "ctx"), None),
        P(("seq", "ctx"), None),
        P("seq"),
        P("seq"),
        P("seq"),
        P("seq"),
        P("seq", None),
        P("seq"),
        P("seq", None),
        P("seq"),
        P("seq", None),
        P("seq"),
        P("seq", None),
        P("seq"),
    )
    return jax.shard_map(
        on_device, mesh=mesh, in_specs=in_specs, out_specs=out_specs, check_vma=False
    )
```

profile of v0, /device:TPU:0, one launch (start us, length us, event | category | flops | bytes accessed | tf_op | source)
XLA Modules:
  0.0 4656.5 jit_solution(13373068768158495820)
XLA Ops:
  8.8 13.5 all-gather.1
  22.4 12.0 all-gather
  34.4 33.2 all-gather.2
  68.8 369.1 %all-gather.19.cloned.1.call-done = bf16[2048,6144]{1,0:T(8,128)(2,1)} async-done(((bf16[512,6144]{1,0:T(8,128)(2,1)}), bf16[2048,6144]{1,0:T(8,128)(2,1)}) %all-gather.19.cloned.1.call-update) | async-done | bytes 25165840 | tf_op jit(solution)/shard_map/all_gather | solution.py:87
  437.9 11.8 convolution_add_fusion.1
  461.7 125.7 %all-gather.25.cloned.1.call-done = bf16[2048,2048]{1,0:T(8,128)(2,1)} async-done(((bf16[512,2048]{1,0:T(8,128)(2,1)}), bf16[2048,2048]{1,0:T(8,128)(2,1)}) %all-gather.25.cloned.1.call-update) | async-done | bytes 8388624 | tf_op jit(solution)/shard_map/all_gather | solution.py:89
  587.4 6.3 convolution_convert_fusion
  595.6 38.0 all-gather.21.cloned.1.call-done
  643.3 38.2 all-gather.23.cloned.1.call-done
  691.2 11.9 while.50
  703.1 16.9 while.52
  720.0 103.5 %while.53 = (s32[]{:T(128)}, f32[192,8,256]{2,0,1:T(8,128)}, f32[3,512,2048]{2,1,0:T(8,128)}, f32[3,512,2048]{2,1,0:T(8,128)}, bf16[3,512,8,256]{3,1,2,0:T(8,128...) while((s32[]{:T(128)}, f32[192,8,256]{2,0,1:T(8,128)}, ...), condition=%wide.region_12.13_spmd.clone, body=%wide.region_11.12_spmd.clone.sunk | while | flops 2025029632 | bytes 69002152 | solution.py:220
  746.3 8.0 constant_dynamic-update-slice_fusion.3
  780.9 8.0 constant_dynamic-update-slice_fusion.3
  815.6 8.0 constant_dynamic-update-slice_fusion.3
  825.7 19.3 while.51
  831.1 6.9 bitcast_add_fusion.4
  838.2 6.9 bitcast_add_fusion.4
  847.6 9.0 fusion.118
  859.4 56.8 %reduce-scatter.7.cloned.1.call-done = f32[192,2048]{1,0:T(8,128)} async-done(((f32[1536,2048]{1,0:T(8,128)}), f32[192,2048]{1,0:T(8,128)}) %reduce-scatter.7.cloned.1.call-update) | async-done | bytes 1572880 | tf_op jit(solution)/shard_map/reduce_scatter | solution.py:224
  921.8 90.7 %reduce-scatter.9.cloned.1.call-done = f32[192,2048]{1,0:T(8,128)} async-done(((f32[1536,2048]{1,0:T(8,128)}), f32[192,2048]{1,0:T(8,128)}) %reduce-scatter.9.cloned.1.call-update) | async-done | bytes 1572880 | tf_op jit(solution)/shard_map/reduce_scatter | solution.py:227
  1014.1 27.3 fusion.106
  1042.1 38.5 all-gather.5
  1080.6 45.1 all-gather.4
  1125.8 45.1 all_gather.91
  1170.9 405.1 %all-gather.27.cloned.1.call-done = bf16[2048,8192]{1,0:T(8,128)(2,1)} async-done(((bf16[512,8192]{1,0:T(8,128)(2,1)}), bf16[2048,8192]{1,0:T(8,128)(2,1)}) %all-gather.27.cloned.1.call-update) | async-done | bytes 33554448 | tf_op jit(solution)/shard_map/all_gather | solution.py:91
  1576.0 21.2 convolution_add_fusion
  1597.2 540.0 %all-gather.29.cloned.1.call-done = bf16[8192,2048]{1,0:T(8,128)(2,1)} async-done(((bf16[2048,2048]{1,0:T(8,128)(2,1)}), bf16[8192,2048]{1,0:T(8,128)(2,1)}) %all-gather.29.cloned.1.call-update) | async-done | bytes 33554448 | tf_op jit(solution)/shard_map/all_gather | solution.py:93
  2137.2 32.4 convert_reduce_fusion
  2169.6 26.1 fusion.103
  2203.0 23.9 fusion.119
  2227.1 18.2 fusion.117
  2246.3 15.5 fusion.113
  2268.6 52.5 %reduce-scatter.13.cloned.1.call-done = f32[64,2048]{1,0:T(8,128)} async-done(((f32[2048,2048]{1,0:T(8,128)}), f32[64,2048]{1,0:T(8,128)}) %reduce-scatter.13.cloned.1.call-update) | async-done | bytes 524304 | tf_op jit(solution)/shard_map/reduce_scatter | solution.py:247
  2321.2 439.5 %reduce-scatter.11.cloned.1.call-done = f32[64,6144]{1,0:T(8,128)} async-done(((f32[2048,6144]{1,0:T(8,128)}), f32[64,6144]{1,0:T(8,128)}) %reduce-scatter.11.cloned.1.call-update) | async-done | bytes 1572880 | tf_op jit(solution)/shard_map/reduce_scatter | solution.py:245
  2760.7 703.9 %reduce-scatter.15.cloned.1.call-done = f32[64,8192]{1,0:T(8,128)} async-done(((f32[2048,8192]{1,0:T(8,128)}), f32[64,8192]{1,0:T(8,128)}) %reduce-scatter.15.cloned.1.call-update) | async-done | bytes 2097168 | tf_op jit(solution)/shard_map/reduce_scatter | solution.py:268
  3464.7 712.4 %reduce-scatter.17.cloned.1.call-done = f32[256,2048]{1,0:T(8,128)} async-done(((f32[8192,2048]{1,0:T(8,128)}), f32[256,2048]{1,0:T(8,128)}) %reduce-scatter.17.cloned.1.call-update) | async-done | bytes 2097168 | tf_op jit(solution)/shard_map/reduce_scatter | solution.py:270
  4179.0 12.1 all-gather.6
  4191.2 11.9 all-gather.3
  4208.5 15.5 fusion.80
  4224.0 92.4 %all-reduce.23.cloned.1.call-done = (f32[2048]{0:T(1024)}, f32[2048]{0:T(1024)}, f32[2048]{0:T(1024)}, f32[2048]{0:T(1024)}, f32[6144]{0:T(1024)}, /*index=5*/f32[2048]{0:T(1024)}, f32[8192]{0:T(1024)}) async-done(((f32[2048]{0:T(1024)}, f32[2048]{0:T(1024)}, f32[2048]{0:T(1024)}, f32[2048]{0:T(1024)}, f32[6144]{0:T(1024)}, /*index=5*/f32[2048]{0:T(1024)}, f32[8192]{0:T(1024)}), (f32[2048]{0:T(1024)}, ...) | async-done | bytes 98320
  4321.4 23.7 all-reduce.20
  4345.9 8.8 all-gather.7
  4356.3 74.0 %all-gather.31.cloned.1.call-done = f32[512,6144]{1,0:T(8,128)} async-done(((f32[64,6144]{1,0:T(8,128)}), f32[512,6144]{1,0:T(8,128)}) %all-gather.31.cloned.1.call-update) | async-done | bytes 12582928 | tf_op jit(solution)/shard_map/all_gather | solution.py:279
  4430.3 91.8 %all-gather.35.cloned.1.call-done = f32[512,8192]{1,0:T(8,128)} async-done(((f32[64,8192]{1,0:T(8,128)}), f32[512,8192]{1,0:T(8,128)}) %all-gather.35.cloned.1.call-update) | async-done | bytes 16777232 | tf_op jit(solution)/shard_map/all_gather | solution.py:283
  4522.1 91.8 %all-gather.37.cloned.1.call-done = f32[2048,2048]{1,0:T(8,128)} async-done(((f32[256,2048]{1,0:T(8,128)}), f32[2048,2048]{1,0:T(8,128)}) %all-gather.37.cloned.1.call-update) | async-done | bytes 16777232 | tf_op jit(solution)/shard_map/all_gather | solution.py:285
  4614.4 11.0 copy.173
  4627.6 13.9 copy.175
  (302 shorter events, 203.7 us)
Async XLA Ops:
  7.2 27.2 copy-start.40
  7.2 60.4 %copy-start.1 = (bf16[192,2048]{1,0:T(8,128)(2,1)S(1)}, bf16[192,2048]{1,0:T(8,128)(2,1)}, u32[]{:S(2)}) copy-start(bf16[192,2048]{1,0:T(8,128)(2,1)} %param.23) | copy-start | bytes 2359300
  7.2 430.7 %all-gather.19.cloned.1.call-start = ((), (), s32[]{:S(2)}) async-start(), calls=%async_computation.6 | async-start | bytes 31457280 | tf_op jit(solution)/shard_map/all_gather | solution.py:87
  8.0 579.4 %all-gather.25.cloned.1.call-start = ((), (), s32[]{:S(2)}) async-start(), calls=%async_computation.9 | async-start | bytes 10485760 | tf_op jit(solution)/shard_map/all_gather | solution.py:89
  8.7 624.9 %all-gather.21.cloned.1.call-start = ((), (), s32[]{:S(2)}) async-start(), calls=%async_computation.7 | async-start | bytes 7077888 | tf_op jit(solution)/shard_map/all_gather | solution.py:134
  22.4 427.4 %copy-start.31 = (f32[4,1,512]{2,1,0:T(1,128)}, f32[4,1,512]{2,1,0:T(1,128)S(1)}, u32[]{:S(2)}) copy-start(f32[4,1,512]{2,1,0:T(1,128)S(1)} %convert_element_type.109) | copy-start | bytes 24580
  34.4 415.4 %copy-start.25 = (f32[4,1,512]{2,1,0:T(1,128)}, f32[4,1,512]{2,1,0:T(1,128)S(1)}, u32[]{:S(2)}) copy-start(f32[4,1,512]{2,1,0:T(1,128)S(1)} %convert_element_type.108) | copy-start | bytes 24580
  67.8 381.9 %copy-start.33 = (f32[192]{0:T(256)}, f32[192]{0:T(256)S(1)}, u32[]{:S(2)}) copy-start(f32[192]{0:T(256)S(1)} %broadcast_multiply_fusion) | copy-start | bytes 2308
  68.8 381.0 %copy-start.35 = (f32[192]{0:T(256)}, f32[192]{0:T(256)S(1)}, u32[]{:S(2)}) copy-start(f32[192]{0:T(256)S(1)} %fusion.102) | copy-start | bytes 2308
  437.9 15.1 copy-start.48
  453.0 228.5 %all-gather.23.cloned.1.call-start = ((), (), s32[]{:S(2)}) async-start(), calls=%async_computation.8 | async-start | bytes 7077888 | tf_op jit(solution)/shard_map/all_gather | solution.py:133
  458.9 128.5 %copy-start.5 = (bf16[192,2048]{1,0:T(8,128)(2,1)S(1)}, bf16[192,2048]{1,0:T(8,128)(2,1)}, u32[]{:S(2)}) copy-start(bf16[192,2048]{1,0:T(8,128)(2,1)} %param.25) | copy-start | bytes 2359300
  460.7 455.4 %reduce-scatter.7.cloned.1.call-start = ((), (), s32[]{:S(2)}) async-start(), calls=%async_computation.12 | async-start | bytes 14155776 | tf_op jit(solution)/shard_map/reduce_scatter | solution.py:224
  823.6 188.9 %reduce-scatter.9.cloned.1.call-start = ((), (), s32[]{:S(2)}) async-start(), calls=%async_computation.13 | async-start | bytes 14155776 | tf_op jit(solution)/shard_map/reduce_scatter | solution.py:227
  824.2 751.8 %all-gather.27.cloned.1.call-start = ((), (), s32[]{:S(2)}) async-start(), calls=%async_computation.10 | async-start | bytes 41943040 | tf_op jit(solution)/shard_map/all_gather | solution.py:91
  824.9 1312.3 %all-gather.29.cloned.1.call-start = ((), (), s32[]{:S(2)}) async-start(), calls=%async_computation.11 | async-start | bytes 41943040 | tf_op jit(solution)/shard_map/all_gather | solution.py:93
  825.7 1495.4 %reduce-scatter.13.cloned.1.call-start = ((), (), s32[]{:S(2)}) async-start(), calls=%async_computation.16 | async-start | bytes 17301504 | tf_op jit(solution)/shard_map/reduce_scatter | solution.py:247
  856.6 1904.1 %reduce-scatter.11.cloned.1.call-start = ((), (), s32[]{:S(2)}) async-start(), calls=%async_computation.14 | async-start | bytes 51904512 | tf_op jit(solution)/shard_map/reduce_scatter | solution.py:245
  921.3 92.7 %copy-start.2 = (bf16[192,2048]{1,0:T(8,128)(2,1)S(1)}, bf16[192,2048]{1,0:T(8,128)(2,1)}, u32[]{:S(2)}) copy-start(bf16[192,2048]{1,0:T(8,128)(2,1)} %param.23) | copy-start | bytes 2359300
  921.3 92.7 %copy-start.26 = (f32[4,1,512]{2,1,0:T(1,128)S(1)}, f32[4,1,512]{2,1,0:T(1,128)}, u32[]{:S(2)}) copy-start(f32[4,1,512]{2,1,0:T(1,128)} %copy-done.25) | copy-start | bytes 24580
  921.3 92.7 %copy-start.32 = (f32[4,1,512]{2,1,0:T(1,128)S(1)}, f32[4,1,512]{2,1,0:T(1,128)}, u32[]{:S(2)}) copy-start(f32[4,1,512]{2,1,0:T(1,128)} %copy-done.31) | copy-start | bytes 24580
  921.3 92.7 %copy-start.34 = (f32[192]{0:T(256)S(1)}, f32[192]{0:T(256)}, u32[]{:S(2)}) copy-start(f32[192]{0:T(256)} %copy-done.33) | copy-start | bytes 2308
  921.3 92.7 %copy-start.36 = (f32[192]{0:T(256)S(1)}, f32[192]{0:T(256)}, u32[]{:S(2)}) copy-start(f32[192]{0:T(256)} %copy-done.35) | copy-start | bytes 2308
  921.6 119.9 %copy-start.8 = (bf16[24,8,8,256]{3,1,2,0:T(8,128)(2,1)}, bf16[24,8,8,256]{3,1,2,0:T(8,128)(2,1)S(1)}, u32[]{:S(2)}) copy-start(bf16[24,8,8,256]{3,1,2,0:T(8,128)(2,1)S(1)} %copy.111) | copy-start | bytes 2359300
  921.8 119.7 %copy-start.10 = (bf16[24,8,8,256]{3,1,2,0:T(8,128)(2,1)}, bf16[24,8,8,256]{3,1,2,0:T(8,128)(2,1)S(1)}, u32[]{:S(2)}) copy-start(bf16[24,8,8,256]{3,1,2,0:T(8,128)(2,1)S(1)} %copy.109) | copy-start | bytes 2359300
  1014.0 27.4 copy-start.12
  1041.5 84.3 %copy-start.39 = (bf16[2048]{0:T(1024)(128)(2,1)S(1)}, bf16[2048]{0:T(1024)(128)(2,1)}, u32[]{:S(2)}) copy-start(bf16[2048]{0:T(1024)(128)(2,1)} %param.35) | copy-start | bytes 12292
  1041.5 2423.1 %reduce-scatter.15.cloned.1.call-start = ((), (), s32[]{:S(2)}) async-start(), calls=%async_computation.18 | async-start | bytes 69206016 | tf_op jit(solution)/shard_map/reduce_scatter | solution.py:268
  1576.0 561.2 %copy-start.7 = (bf16[192,2048]{1,0:T(8,128)(2,1)S(1)}, bf16[192,2048]{1,0:T(8,128)(2,1)}, u32[]{:S(2)}) copy-start(bf16[192,2048]{1,0:T(8,128)(2,1)} %param.25) | copy-start | bytes 2359300
  2195.7 1981.3 %reduce-scatter.17.cloned.1.call-start = ((), (), s32[]{:S(2)}) async-start(), calls=%async_computation.20 | async-start | bytes 69206016 | tf_op jit(solution)/shard_map/reduce_scatter | solution.py:270
  2227.0 18.3 copy-start.9
  2227.0 18.3 copy-start.11
  2227.0 19.3 copy-start.27
  2227.0 2089.4 %all-reduce.23.cloned.1.call-start = ((), (), s32[]{:S(2)}) async-start(), calls=%async_computation.22 | async-start | bytes 196608
  2227.1 18.3 copy-start.13
  2246.3 15.5 copy-start.38
  2268.6 2087.7 %all-gather.33.cloned.1.call-start = ((), (), s32[]{:S(2)}) async-start(), calls=%async_computation.17 | async-start | bytes 4718592 | tf_op jit(solution)/shard_map/all_gather | solution.py:281
  2321.1 1856.0 %copy-start.49 = (u32[32]{0:T(128)S(1)}, u32[32]{0:T(128)}, u32[]{:S(2)}) copy-start(u32[32]{0:T(128)} %constant.177) | copy-start | bytes 388
  2321.1 1857.9 %copy-start.46 = (bf16[512]{0:T(512)(128)(2,1)S(1)}, bf16[512]{0:T(512)(128)(2,1)}, u32[]{:S(2)}) copy-start(bf16[512]{0:T(512)(128)(2,1)} %param.33) | copy-start | bytes 3076
  2321.1 1857.9 %copy-start.47 = (bf16[512]{0:T(512)(128)(2,1)S(1)}, bf16[512]{0:T(512)(128)(2,1)}, u32[]{:S(2)}) copy-start(bf16[512]{0:T(512)(128)(2,1)} %param.37) | copy-start | bytes 3076
  2321.1 1882.0 %copy-start.19 = (bf16[8,24,8,256]{3,2,0,1:T(8,128)(2,1)S(1)}, bf16[8,24,8,256]{3,2,0,1:T(8,128)(2,1)}, u32[]{:S(2)}) copy-start(bf16[8,24,8,256]{3,2,0,1:T(8,128)(2,1)} %copy-done.18) | copy-start | bytes 2359300
  2321.1 2109.2 %all-gather.31.cloned.1.call-start = ((), (), s32[]{:S(2)}) async-start(), calls=%async_computation.15 | async-start | bytes 14155776 | tf_op jit(solution)/shard_map/all_gather | solution.py:279
  2760.7 1761.4 %all-gather.35.cloned.1.call-start = ((), (), s32[]{:S(2)}) async-start(), calls=%async_computation.19 | async-start | bytes 18874368 | tf_op jit(solution)/shard_map/all_gather | solution.py:283
  3464.6 1149.2 %all-gather.37.cloned.1.call-start = ((), (), s32[]{:S(2)}) async-start(), calls=%async_computation.21 | async-start | bytes 18874368 | tf_op jit(solution)/shard_map/all_gather | solution.py:285
  4345.1 280.3 %copy-start.41 = (f32[512]{0:T(512)}, f32[512]{0:T(512)S(1)}, u32[]{:S(2)}) copy-start(f32[512]{0:T(512)S(1)} %get-tuple-element.973) | copy-start | bytes 6148
  4625.4 16.6 slice-start
  4627.6 14.5 slice-start.2
  4627.6 16.0 slice-start.3
  (23 other events, 86.5 us)
Sparse Core Ops, SparseCore 0:
  9.6 428.2 all-gather.18
  439.5 147.8 all-gather.24
  589.8 43.7 all-gather.20
  635.9 45.5 all-gather.22
  823.7 92.3 reduce-scatter.6
  920.1 92.3 reduce-scatter.8
  1014.1 561.8 all-gather.26
  1577.6 559.5 all-gather.28
  2140.1 180.9 reduce-scatter.12
  2327.3 433.2 reduce-scatter.10
  2763.0 701.5 reduce-scatter.14
  3466.8 710.1 reduce-scatter.16
  4184.6 131.7 all-reduce.22
  4318.3 37.9 all-gather.32
  4358.2 72.0 all-gather.30
  4432.2 89.8 all-gather.34
  4524.0 89.8 all-gather.36
where the time goes:
time: 4660 us
  waiting for transfers between devices  3930 us (84%)
  matrix products  302 us (6%)
  blocking collectives  244 us (5%)
  local copies, waits for them, and re-layouts  138 us (3%)
    reduce_scatter x1, waiting for transfers between devices, on_device(): lax.psum_scatter(grad_w_out, ('seq', 'ctx'), scatter_dimension=0, tiled=T...  712 us
    reduce_scatter x1, waiting for transfers between devices, on_device(): lax.psum_scatter(grad_w_in, ('seq', 'ctx'), scatter_dimension=0, tiled=True)  704 us
    all_gather x1, waiting for transfers between devices, on_device(): lax.all_gather(w_out, 'seq', axis=0, tiled=True)  540 us
    reduce_scatter x1, waiting for transfers between devices, on_device(): lax.psum_scatter(grad_w_qkv, ('seq', 'ctx'), scatter_dimension=0, tiled=T...  440 us
    all_gather x1, waiting for transfers between devices, on_device(): lax.all_gather(w_in, 'seq', axis=0, tiled=True)  405 us
    all_gather x1, waiting for transfers between devices, on_device(): lax.all_gather(w_qkv, 'seq', axis=0, tiled=True)  369 us
    all_gather x1, waiting for transfers between devices, on_device(): lax.all_gather(w_dense, 'seq', axis=0, tiled=True)  126 us
    unnamed x18, waiting for transfers between devices  95.8 us
  transfers between devices with their start and end apart: 17, of which 17 were waited for; matrix products, arithmetic and copies ran while one was open for 6% of the time, Pallas kernels for 0%

commit v1 on v0

v1 whole, which is shorter than its diff:
```python
import functools

import jax
import jax.numpy as jnp
from jax import lax
from jax.experimental import pallas as pl
from jax.experimental.pallas import tpu as pltpu
from jax.sharding import Mesh, PartitionSpec as P

H = 8
HD = 256
ROT = 64
BLOCK = 96
EPSILON = 1e-05
ROT_BASE = 10000.0
SCALE = HD ** (-0.5)

f32 = jnp.float32
bf16 = jnp.bfloat16
TP = ("seq", "core")


def angles_of(positions):
    half = ROT // 2
    inverse_freq = jnp.power(ROT_BASE, -(jnp.arange(half, dtype=f32) * 2.0) / ROT)
    angles = positions.astype(f32)[:, None] * inverse_freq[None, :]
    return jnp.cos(angles), jnp.sin(angles)


def rotate(u, cosine, sine):
    half = ROT // 2
    a, b = u[..., :half], u[..., half:ROT]
    return jnp.concatenate([a * cosine - b * sine, b * cosine + a * sine, u[..., ROT:]], axis=-1)


def attention_forward(q, k, v, row_pos, col_pos, tile):
    rows = q.shape[0]

    def kernel(q_ref, k_ref, v_ref, rp_ref, cp_ref, o_ref, lse_ref):
        s = lax.dot_general(
            q_ref[...], k_ref[...], (((1,), (1,)), ((), ())), preferred_element_type=f32
        ) * SCALE
        allowed = rp_ref[...] >= cp_ref[...]
        s = jnp.where(allowed, s, -1e30)
        top = jnp.max(s, axis=-1, keepdims=True)
        e = jnp.exp(s - top)
        total = jnp.sum(e, axis=-1, keepdims=True)
        p = (e / total).astype(bf16)
        o_ref[...] = jnp.dot(p, v_ref[...], preferred_element_type=f32).astype(bf16)
        lse_ref[...] = top + jnp.log(total)

    whole = pl.BlockSpec((rows, HD), lambda i: (0, 0))
    part = pl.BlockSpec((tile, HD), lambda i: (i, 0))
    one = pl.BlockSpec((tile, 1), lambda i: (i, 0))
    return pl.pallas_call(
        kernel,
        grid=(rows // tile,),
        in_specs=[part, whole, whole, one, pl.BlockSpec((1, rows), lambda i: (0, 0))],
        out_specs=[part, one],
        out_shape=[
            jax.ShapeDtypeStruct((rows, HD), bf16),
            jax.ShapeDtypeStruct((rows, 1), f32),
        ],
        compiler_params=pltpu.CompilerParams(vmem_limit_bytes=56 * 2**20),
        cost_estimate=pl.CostEstimate(
            flops=4 * rows * rows * HD, bytes_accessed=8 * rows * HD, transcendentals=rows * rows
        ),
        name="attention_forward",
    )(q, k, v, row_pos, col_pos)


def attention_backward(q, k, v, g, lse, row_pos, col_pos, tile):
    rows = q.shape[0]

    def kernel(q_ref, k_ref, v_ref, g_ref, lse_ref, rp_ref, cp_ref, dq_ref, dk_ref, dv_ref):
        nt = (((1,), (1,)), ((), ()))
        tn = (((0,), (0,)), ((), ()))

        @pl.when(pl.program_id(0) == 0)
        def _():
            dk_ref[...] = jnp.zeros_like(dk_ref)
            dv_ref[...] = jnp.zeros_like(dv_ref)

        s = lax.dot_general(q_ref[...], k_ref[...], nt, preferred_element_type=f32) * SCALE
        allowed = rp_ref[...] >= cp_ref[...]
        p = jnp.where(allowed, jnp.exp(s - lse_ref[...]), 0.0)
        dp = lax.dot_general(g_ref[...], v_ref[...], nt, preferred_element_type=f32)
        shift = jnp.sum(p * dp, axis=-1, keepdims=True)
        ds = (p * (dp - shift)).astype(bf16)
        dq_ref[...] = jnp.dot(ds, k_ref[...], preferred_element_type=f32) * SCALE
        dk_ref[...] += lax.dot_general(ds, q_ref[...], tn, preferred_element_type=f32) * SCALE
        dv_ref[...] += lax.dot_general(p.astype(bf16), g_ref[...], tn, preferred_element_type=f32)

    whole = pl.BlockSpec((rows, HD), lambda i: (0, 0))
    part = pl.BlockSpec((tile, HD), lambda i: (i, 0))
    one = pl.BlockSpec((tile, 1), lambda i: (i, 0))
    return pl.pallas_call(
        kernel,
        grid=(rows // tile,),
        in_specs=[part, whole, whole, part, one, one, pl.BlockSpec((1, rows), lambda i: (0, 0))],
        out_specs=[part, whole, whole],
        out_shape=[jax.ShapeDtypeStruct((rows, HD), f32)] * 3,
        compiler_params=pltpu.CompilerParams(vmem_limit_bytes=56 * 2**20),
        cost_estimate=pl.CostEstimate(
            flops=10 * rows * rows * HD, bytes_accessed=20 * rows * HD, transcendentals=rows * rows
        ),
        name="attention_backward",
    )(q, k, v, g, lse, row_pos, col_pos)


def on_device(
    nz,
    nchip,
    ncore,
    tokens,
    block_ids,
    cotangent,
    norm1_gain,
    norm1_bias,
    norm2_gain,
    norm2_bias,
    w_qkv,
    b_qkv,
    w_dense,
    b_dense,
    w_in,
    b_in,
    w_out,
    b_out,
):
    own, width = tokens.shape
    z = lax.axis_index("seq")
    chip = lax.axis_index("chip")
    core = lax.axis_index("core")
    ranks = nz * ncore
    rank = z * ncore + core
    rows = ranks * own
    ff = w_out.shape[0] * nz
    ffr = ff // ranks
    hc = width // ranks
    split = max(1, HD // hc)
    wrows = width // nz
    piece = wrows // nchip // ncore

    small = jnp.concatenate(
        [norm1_gain, norm1_bias, norm2_gain, norm2_bias, b_qkv, b_dense, b_in, b_out,
         block_ids.reshape(-1).astype(bf16)]
    )
    small = lax.all_gather(small, "seq", axis=0, tiled=False)
    d4 = wrows
    f4 = b_in.shape[0]
    q4 = b_qkv.shape[0]
    cuts = [0, d4, 2 * d4, 3 * d4, 4 * d4, 4 * d4 + q4, 5 * d4 + q4, 5 * d4 + q4 + f4,
            6 * d4 + q4 + f4, small.shape[1]]
    gain1, bias1, gain2, bias2, full_bqkv, full_bdense, full_bin, full_bout, ids = [
        small[:, cuts[i] : cuts[i + 1]].reshape(-1) for i in range(9)
    ]
    gain1, bias1, gain2, bias2 = [v.astype(f32) for v in (gain1, bias1, gain2, bias2)]
    ids = ids.reshape(nz, -1).astype(jnp.int32)

    tok = lax.all_gather(tokens, TP, axis=0, tiled=True)
    cot = lax.all_gather(cotangent, TP, axis=0, tiled=True)

    def reshard(w, groups):
        c = w.shape[1] // groups // ranks
        mine = lax.dynamic_slice_in_dim(
            w.reshape(nchip * ncore, piece, groups, nz, ncore * c), chip * ncore + core, 1, 0
        )[0]
        mine = mine.transpose(2, 0, 1, 3)
        got = lax.all_to_all(mine, "seq", 0, 0, tiled=True)
        every = lax.all_gather(got, ("chip", "core"), axis=0, tiled=False)
        every = every.transpose(1, 0, 2, 3, 4).reshape(width, groups, ncore, c)
        return lax.dynamic_index_in_dim(every, core, 2, keepdims=False).reshape(width, groups * c)

    w_in_c = reshard(w_in, 1)
    w_qkv_c = reshard(w_qkv, 3)
    w_out_r = lax.dynamic_slice_in_dim(w_out, core * ffr, ffr, 0)
    w_dense_r = lax.dynamic_slice_in_dim(w_dense, core * hc, hc, 0)

    def layer_stats(x):
        mean = jnp.mean(x, axis=-1, keepdims=True)
        center = x - mean
        spread = jnp.mean(center * center, axis=-1, keepdims=True)
        inv = lax.rsqrt(spread + EPSILON)
        return center * inv, inv

    xhat, unused = layer_stats(tok.astype(f32))
    normed1 = (xhat * gain1 + bias1).astype(bf16)
    normed2 = (xhat * gain2 + bias2).astype(bf16)

    project = jnp.dot(normed1, w_qkv_c, preferred_element_type=f32)
    bias_c = lax.dynamic_slice_in_dim(full_bqkv.reshape(3, ranks, hc), rank, 1, 1)
    project = (project + bias_c.reshape(1, 3 * hc).astype(f32)).reshape(rows, 3, hc)
    blocks = ids.shape[1]
    pos_all = jnp.repeat(ids, BLOCK, axis=1) * BLOCK + jnp.tile(
        jnp.arange(BLOCK, dtype=jnp.int32), blocks
    )
    pos_seq = lax.dynamic_index_in_dim(pos_all, chip, 0, keepdims=False)
    length = pos_seq.shape[0]

    def heads_of(x):
        if split > 1:
            x = lax.all_gather(x, "core", axis=2, tiled=True)
        x = x.reshape(nz, rows // nz, x.shape[1], HD).transpose(0, 2, 1, 3)
        x = lax.all_to_all(x, "chip", 0, 0, tiled=True)
        return x.transpose(1, 0, 2, 3).reshape(x.shape[1], length, HD)

    def heads_back(x):
        g = x.shape[0]
        x = x.reshape(g, nchip, length // nchip, HD).transpose(1, 0, 2, 3)
        x = lax.all_to_all(x, "chip", 0, 0, tiled=True)
        x = x.transpose(0, 2, 1, 3).reshape(rows, g, HD)
        if split > 1:
            x = lax.dynamic_slice_in_dim(x, core * hc, hc, 2)
        return x

    cosine, sine = angles_of(pos_seq)
    if split == 1:
        pos_rows = lax.dynamic_slice_in_dim(pos_all, chip * (rows // nz), rows // nz, 1).reshape(-1)
        cos_r, sin_r = angles_of(pos_rows)
        q = rotate(project[:, 0], cos_r, sin_r).astype(bf16)
        k = rotate(project[:, 1], cos_r, sin_r).astype(bf16)
        v = project[:, 2].astype(bf16)
        q, k, v = heads_of(jnp.stack([q, k, v], axis=1))
    else:
        q, k, v = heads_of(project)
        q = rotate(q, cosine, sine).astype(bf16)
        k = rotate(k, cosine, sine).astype(bf16)
        v = v.astype(bf16)
    row_pos, col_pos = pos_seq[:, None], pos_seq[None, :]
    tile = 256
    attended, lse = attention_forward(q, k, v, row_pos, col_pos, tile)
    mixed = heads_back(attended[None]).reshape(rows, hc)

    hidden = jnp.dot(normed2, w_in_c, preferred_element_type=f32)
    hidden = hidden + lax.dynamic_slice_in_dim(full_bin, rank * ffr, ffr).astype(f32)
    active, gelu_back = jax.vjp(functools.partial(jax.nn.gelu, approximate=False), hidden)
    active = active.astype(bf16)
    part_out = jnp.dot(mixed, w_dense_r, preferred_element_type=f32) + jnp.dot(
        active, w_out_r, preferred_element_type=f32
    )
    summed_out = lax.psum_scatter(part_out.astype(bf16), TP, scatter_dimension=0, tiled=True)
    output = (
        tokens.astype(f32)
        + summed_out.astype(f32)
        + full_bdense.astype(f32)
        + full_bout.astype(f32)
    ).astype(bf16)

    tn = (((0,), (0,)), ((), ()))
    nt = (((1,), (1,)), ((), ()))
    grad_active = lax.dot_general(cot, w_out_r, nt, preferred_element_type=f32)
    grad_hidden32 = gelu_back(grad_active)[0]
    grad_hidden = grad_hidden32.astype(bf16)
    dw_out = lax.dot_general(active, cot, tn, preferred_element_type=f32).astype(bf16)
    dw_in = lax.dot_general(normed2, grad_hidden, tn, preferred_element_type=f32).astype(bf16)
    gn2 = lax.dot_general(grad_hidden, w_in_c, nt, preferred_element_type=f32)

    dw_dense = lax.dot_general(mixed, cot, tn, preferred_element_type=f32).astype(bf16)
    grad_mixed = lax.dot_general(cot, w_dense_r, nt, preferred_element_type=f32).astype(bf16)
    g = heads_of(grad_mixed[:, None])[0]
    dq, dk, dv = attention_backward(q, k, v, g, lse, row_pos, col_pos, tile)
    dq = rotate(dq, cosine, -sine).astype(bf16)
    dk = rotate(dk, cosine, -sine).astype(bf16)
    grad_project = heads_back(jnp.stack([dq, dk, dv.astype(bf16)])).reshape(rows, 3 * hc)
    dw_qkv = lax.dot_general(normed1, grad_project, tn, preferred_element_type=f32).astype(bf16)
    gn1 = lax.dot_general(grad_project, w_qkv_c, nt, preferred_element_type=f32)

    e_part = (gn1 * gain1 + gn2 * gain2).astype(bf16)
    e = lax.psum_scatter(e_part, TP, scatter_dimension=0, tiled=True).astype(f32)
    xhat_own, inv_own = layer_stats(tokens.astype(f32))
    terms = (
        e
        - jnp.mean(e, axis=-1, keepdims=True)
        - xhat_own * jnp.mean(e * xhat_own, axis=-1, keepdims=True)
    ) * inv_own
    grad_tokens = (cotangent.astype(f32) + terms).astype(bf16)

    sum_cot = jnp.sum(cotangent.astype(f32), axis=0)
    mine_bin = jnp.zeros((ranks, ffr), f32)
    mine_bin = lax.dynamic_update_slice_in_dim(
        mine_bin, jnp.sum(grad_hidden.astype(f32), axis=0)[None], rank, 0
    ).reshape(-1)
    mine_bqkv = jnp.zeros((3, ranks, hc), f32)
    mine_bqkv = lax.dynamic_update_slice_in_dim(
        mine_bqkv, jnp.sum(grad_project.astype(f32), axis=0).reshape(3, 1, hc), rank, 1
    ).reshape(-1)
    vectors = [
        jnp.sum(gn1 * xhat, axis=0),
        jnp.sum(gn1, axis=0),
        jnp.sum(gn2 * xhat, axis=0),
        jnp.sum(gn2, axis=0),
        mine_bqkv,
        sum_cot,
        mine_bin,
    ]
    sizes = [v.shape[0] for v in vectors]
    sums = lax.psum(jnp.concatenate(vectors), ("seq", "chip", "core"))
    at = 0
    small_out = []
    for size in sizes:
        small_out.append(lax.dynamic_slice_in_dim(sums, at + z * (size // nz), size // nz))
        at += size
    g_gain1, g_bias1, g_gain2, g_bias2, g_bqkv, g_bdense, g_bin = small_out

    def rows_back(dw):
        part = lax.psum_scatter(dw, "chip", scatter_dimension=0, tiled=True)
        every = lax.all_gather(part, ("core", "chip"), axis=0, tiled=True)
        return every.astype(f32)

    def columns_back(dw, groups):
        c = dw.shape[1] // groups
        part = dw.reshape(nz, nchip, wrows // nchip, groups * c).transpose(1, 0, 2, 3)
        part = lax.psum_scatter(part, "chip", scatter_dimension=0, tiled=True)[0]
        part = lax.all_to_all(part, "seq", 0, 0, tiled=True)
        every = lax.all_gather(part, ("chip", "core"), axis=0, tiled=False)
        every = every.reshape(nchip, ncore, nz, wrows // nchip, groups, c)
        every = every.transpose(0, 3, 4, 2, 1, 5)
        return every.reshape(wrows, groups * ranks * c).astype(f32)

    g_wout = rows_back(dw_out)
    g_wdense = rows_back(dw_dense)
    g_win = columns_back(dw_in, 1)
    g_wqkv = columns_back(dw_qkv, 3)
    return (
        output,
        grad_tokens,
        g_gain1,
        g_bias1,
        g_gain2,
        g_bias2,
        g_wqkv,
        g_bqkv,
        g_wdense,
        g_bdense,
        g_win,
        g_bin,
        g_wout,
        g_bdense,
    )


def solution(mesh):
    nz, nctx = mesh.shape["seq"], mesh.shape["ctx"]
    ncore = 2
    nchip = nctx // ncore
    fine = Mesh(mesh.devices.reshape(nz, nchip, ncore), ("seq", "chip", "core"))
    own = P(("seq", "chip", "core"), None)
    vec = P("seq")
    mat = P("seq", None)
    return jax.shard_map(
        functools.partial(on_device, nz, nchip, ncore),
        mesh=fine,
        in_specs=(own, mat, own, vec, vec, vec, vec, mat, vec, mat, vec, mat, vec, mat, vec),
        out_specs=(own, own, vec, vec, vec, vec, mat, vec, mat, vec, mat, vec, mat, vec),
        check_vma=False,
    )
```

time: 4660 us -> 1160 us (0.25)
  waiting for transfers between devices: 3930 us -> 484 us
  matrix products: 302 us -> 138 us
  local copies, waits for them, and re-layouts: 138 us -> 263 us
  blocking collectives: 244 us -> 125 us
  other arithmetic: 27.9 us -> 78.6 us
    reduce_scatter x6 -> x4, waiting for transfers between devices: 2060 us -> 131 us  [the longest x1 72.8 us: on_device(): lax.psum_scatter(part_out.astype(bf16), TP, scatter_dimension=0, tiled=True)]
    all_gather x10 -> x8, waiting for transfers between devices: 1780 us -> 76.8 us  [the longest x2 46.8 us: columns_back(): every = lax.all_gather(part, ('chip', 'core'), axis=0, tiled=False)]
    all_gather x9 -> x0, blocking collectives: 220 us -> none  [the longest x1 45.1 us: on_device(): lax.all_gather(norm2_gain, 'seq', axis=0, tiled=True)]
    dot_general x39 -> x12, matrix products: 302 us -> 138 us  [the longest x1 26.9 us: on_device(): hidden = jnp.dot(normed2, w_in_c, preferred_element_type=f32)]
    psum x0 -> x1, waiting for transfers between devices: none -> 123 us  [on_device(): sums = lax.psum(jnp.concatenate(vectors), ('seq', 'chip', 'core'))]
    all_to_all x0 -> x3, blocking collectives: none -> 107 us  [the longest x2 76.4 us: reshard(): got = lax.all_to_all(mine, 'seq', 0, 0, tiled=True)]
    convert_element_type x1 -> x6, local copies, waits for them, and re-layouts: 0.08 us -> 86.7 us  [the longest x4 86.7 us: columns_back(): return every.reshape(wrows, groups * ranks * c).astype(f32)]
    unnamed x146 -> x87, local copies, waits for them, and re-layouts: 74.6 us -> 14.2 us
  transfers between devices with their start and end apart: 17 -> 20, of which waited for: 17 -> 11; matrix products, arithmetic and copies ran while one was open for 6% -> 40% of each run, Pallas kernels for 0% -> 2%
where the time goes in v1:
time: 1160 us; the launch traced here: 1150 us
  waiting for transfers between devices  484 us (42%)
  local copies, waits for them, and re-layouts  263 us (23%)
  matrix products  138 us (12%)
  blocking collectives  125 us (11%)
  other arithmetic  78.6 us (7%)
  Pallas kernels  24.1 us (2%)
  starting transfers between devices  21.3 us (2%)
  between operations  15.8 us (1%)
    psum x1, waiting for transfers between devices, on_device(): sums = lax.psum(jnp.concatenate(vectors), ('seq', 'chip', 'core'))  123 us
    unnamed x17, waiting for transfers between devices  101 us
    convert_element_type x4, local copies, waits for them, and re-layouts, columns_back(): return every.reshape(wrows, groups * ranks * c).astype(f32)  86.7 us
    all_to_all x2, blocking collectives, reshard(): got = lax.all_to_all(mine, 'seq', 0, 0, tiled=True)  76.4 us
    reduce_scatter x1, waiting for transfers between devices, on_device(): lax.psum_scatter(part_out.astype(bf16), TP, scatter_dimension=0, tiled=True)  72.8 us
    all_gather x2, waiting for transfers between devices, columns_back(): every = lax.all_gather(part, ('chip', 'core'), axis=0, tiled=False)  46.8 us
    dynamic_slice x3, local copies, waits for them, and re-layouts, reshard(): lax.dynamic_index_in_dim(every, core, 2, keepdims=False)  34 us
    reduce_scatter x1, waiting for transfers between devices, on_device(): lax.psum_scatter(e_part, TP, scatter_dimension=0, tiled=True).astype(f32)  34 us
  transfers between devices with their start and end apart: 20, of which 11 were waited for; matrix products, arithmetic and copies ran while one was open for 40% of the time, Pallas kernels for 2%

profile of v1, /device:TPU:0, one launch (start us, length us, event | category | flops | bytes accessed | tf_op | source)
XLA Modules:
  0.0 1149.3 jit_solution(8306152056986123135)
XLA Ops:
  8.0 13.4 %reshape.421 = bf16[8,64,3,4,512]{4,3,2,1,0:T(4,128)(2,1)} reshape(bf16[512,6144]{1,0:T(8,128)(2,1)} %param.22) | data formatting | bytes 12582912 | tf_op jit(solution)/shard_map/reshape | solution.py:167
  23.1 48.1 %all_to_all.40 = bf16[4,64,3,512]{3,1,2,0:T(8,128)(2,1)} all-to-all(bf16[4,64,3,512]{3,1,2,0:T(8,128)(2,1)S(1)} %bitcast.199), channel_id=1, replica_groups=mesh['seq'=4,'chip'=4,'core'=2] {'seq'}, dimensions={0} | all-to-all | bytes 1572864 | tf_op jit(solution)/shard_map/all_to_all | solution.py:170
  71.9 14.6 %reshape.425 = bf16[8,64,1,4,2048]{4,3,1,0,2:T(4,128)(2,1)} reshape(bf16[512,8192]{1,0:T(8,128)(2,1)} %param.26) | data formatting | bytes 16777216 | tf_op jit(solution)/shard_map/reshape | solution.py:167
  89.0 28.3 %all_to_all.41 = bf16[4,64,1,2048]{3,1,2,0:T(8,128)(2,1)} all-to-all(bf16[4,64,1,2048]{3,1,2,0:T(8,128)(2,1)S(1)} %bitcast.192), channel_id=1, replica_groups=mesh['seq'=4,'chip'=4,'core'=2] {'seq'}, dimensions={0} | all-to-all | bytes 2097152 | tf_op jit(solution)/shard_map/all_to_all | solution.py:170
  120.9 18.2 %all-reduce = bf16[26688]{0:T(1024)(128)(2,1)S(1)} all-reduce(bf16[26688]{0:T(1024)(128)(2,1)S(1)} %dynamic-update-slice), channel_id=2, replica_groups=mesh['seq'=4,'chip'=4,'core'=2] {'seq'}, use_global_device_ids=true, to_apply=%add | all-reduce | flops 26688 | bytes 106752
  151.2 6.3 copy.73
  157.5 9.8 reshape.422
  167.2 8.6 constant_dynamic-slice_fusion.3
  175.8 15.2 %copy.74 = bf16[2048,3,1,256]{0,3,1,2:T(8,128)(2,1)} copy(bf16[2048,3,1,256]{3,2,0,1:T(2,128)(2,1)} %constant_dynamic-slice_fusion.3) | data formatting | bytes 6291456 | tf_op jit(solution)/shard_map/jit(dynamic_index_in_dim)/dynamic_slice | solution.py:173
  191.0 8.2 convolution_add_fusion
  214.8 5.8 fusion.62
  224.7 4.7 all-to-all-start.1
  229.4 4.6 fusion.33
  235.2 24.8 %all-to-all-done.1 = bf16[4,3,384,256]{3,2,1,0:T(8,128)(2,1)} async-done(((bf16[4,3,384,256]{3,2,1,0:T(8,128)(2,1)}), bf16[4,3,384,256]{3,2,1,0:T(8,128)(2,1)}, u32[]{:S(2)}, u32[]{:S(2)}) %all-to-all-start.1) | async-done | bytes 2359328 | tf_op jit(solution)/shard_map/all_to_all | solution.py:205
  267.8 11.1 attention_forward.1
  287.1 13.0 %attention_backward.1 = (f32[1536,256]{1,0:T(8,128)}, f32[1536,256]{1,0:T(8,128)}, f32[1536,256]{1,0:T(8,128)}) custom-call(bf16[1536,256]{1,0:T(8,128)(2,1)} %bitcast.220, bf16[1536,256]{1,0:T(8,128)(2,1)} %bitcast.218, bf16[1536,256]{1,0:T(8,128)(2,1)} %bitcast.216, bf16[1536,256]{1,0:T(8,128)(2,1)} %bitcast.223, f32[1536,1]{1,0:T(8,128)} %get-tuple-element.20.lse_ref, ...), custom_call_target="tpu_custom_call" | custom-call | flops 6039797760 | bytes 7864320 | tf_op jit(solution)/shard_map/attention_backward/pallas_call | solution.py:97
  300.1 6.7 fusion.70
  333.1 5.6 convolution_convert_fusion.3
  339.0 23.5 %all-to-all-done.5 = bf16[4,3,384,256]{2,3,1,0:T(8,128)(2,1)} async-done(((bf16[4,3,384,256]{2,3,1,0:T(8,128)(2,1)}), bf16[4,3,384,256]{2,3,1,0:T(8,128)(2,1)}, u32[]{:S(2)}, u32[]{:S(2)}) %all-to-all-start.5) | async-done | bytes 2359328 | tf_op jit(solution)/shard_map/all_to_all | solution.py:211
  366.4 10.4 convolution_convert_fusion.2
  376.8 4.6 copy.99
  381.4 10.2 fusion.94
  391.7 8.4 copy.87
  400.2 15.0 %reshape.426 = bf16[2048,1,2,1024]{3,2,0,1:T(2,128)(2,1)} reshape(bf16[4,8,64,1,2048]{4,2,1,0,3:T(8,128)(2,1)} %copy.87) | data formatting | bytes 16777216 | tf_op jit(solution)/shard_map/reshape | solution.py:172
  415.1 10.2 constant_dynamic-slice_fusion
  425.4 26.9 %multiply_convert_fusion = (bf16[1536,1024]{1,0:T(8,128)(2,1)}, f32[1536,1024]{1,0:T(8,128)}, f32[1536,1024]{1,0:T(8,128)}) fusion(f32[1024]{0:T(1024)S(1)} %dynamic-slice_convert_fusion.1, bf16[2048,1,1,1024]{3,2,0,1:T(2,128)(2,1)S(1)} %constant_dynamic-slice_fusion, bf16[1536,2048]{1,0:T(8,128)(2,1)} %all-gather.14.cloned.1.call-done, ...), kind=kOutput, calls=%fused_computation.31 | convolution fusion | flops 6565134336 | bytes 26247168 | tf_op jit(solution)/shard_map/dot_general | solution.py:235
  452.3 14.2 %convert_reduce_fusion.1 = (f32[1024]{0:T(1024)S(1)}, bf16[1536,1024]{1,0:T(8,128)(2,1)}) fusion(f32[1536,1024]{1,0:T(8,128)} %get-tuple-element.33, bf16[1536,2048]{1,0:T(8,128)(2,1)S(1)} %bitcast.179, bf16[2048,2048]{1,0:T(8,128)(2,1)} %param.28, s32[]{:T(128)S(6)} %select_n.59, f32[1536,1024]{1,0:T(8,128)} %get-tuple-element.68, ...), kind=kOutput, calls=%fused_computation.30 | convolution fusion | flops 6469188608 | bytes 26222596 | tf_op jit(solution)/shard_map/dot_general | solution.py:252
  466.5 20.1 %fusion.88 = (f32[2048]{0:T(1024)S(1)}, f32[2048]{0:T(1024)S(1)}, bf16[1536,2048]{1,0:T(8,128)(2,1)}, f32[2048]{0:T(1024)S(1)}, f32[2048]{0:T(1024)S(1)}) fusion(f32[1536]{0:T(1024)S(1)} %add_rsqrt_fusion, f32[1536]{0:T(1024)S(1)} %broadcast_multiply_fusion, bf16[1536,2048]{1,0:T(8,128)(2,1)} %all-gather.14.cloned.1.call-done, f32[2048]{0:T(1024)S(1)} %bitcast.235, ...), kind=kOutput, calls=%fused_computation.168 | convolution fusion | flops 6483337216 | bytes 32567296 | tf_op jit(solution)/shard_map/dot_general | solution.py:257
  486.7 9.6 fusion.31
  496.3 4.7 add_convert_fusion.1
  501.1 12.5 %convolution_convert_fusion.1 = bf16[2048,1024]{1,0:T(8,128)(2,1)} fusion(bf16[1536,1024]{1,0:T(8,128)(2,1)} %get-tuple-element.70, bf16[1536,2048]{1,0:T(8,128)(2,1)} %all-gather.14.cloned.1.call-done, f32[2048]{0:T(1024)S(1)} %bitcast.238, f32[2048]{0:T(1024)S(1)} %bitcast.236, f32[1536]{0:T(1024)S(1)} %add_rsqrt_fusion, f32[1536]{0:T(1024)S(1)} %broadcast_multiply_fusion), kind=kOutput, calls=%fused_computation.51 | convolution fusion | flops 6463422464 | bytes 13660160 | tf_op jit(solution)/shard_map/dot_general | solution.py:256
  513.7 11.3 convolution_convert_fusion
  533.1 34.0 %reduce-scatter.13.cloned.1.call-done = bf16[192,2048]{1,0:T(8,128)(2,1)} async-done(((bf16[1536,2048]{1,0:T(8,128)(2,1)}), bf16[192,2048]{1,0:T(8,128)(2,1)}) %reduce-scatter.13.cloned.1.call-update) | async-done | bytes 786448 | tf_op jit(solution)/shard_map/reduce_scatter | solution.py:270
  568.7 72.8 %reduce-scatter.11.cloned.1.call-done = bf16[192,2048]{1,0:T(8,128)(2,1)} async-done(((bf16[1536,2048]{1,0:T(8,128)(2,1)}), bf16[192,2048]{1,0:T(8,128)(2,1)}) %reduce-scatter.11.cloned.1.call-update) | async-done | bytes 786448 | tf_op jit(solution)/shard_map/reduce_scatter | solution.py:242
  649.1 98.9 %all-reduce.8.cloned.1.call-done = bf16[4,4,128,1024]{3,2,0,1:T(8,128)(2,1)} async-done(((bf16[4,4,128,1024]{3,2,0,1:T(8,128)(2,1)}), bf16[4,4,128,1024]{3,2,0,1:T(8,128)(2,1)}) %all-reduce.8.cloned.1.call-update) | async-done | bytes 4194320
  749.9 30.2 %all_to_all.42 = bf16[4,128,1024]{2,1,0:T(8,128)(2,1)} all-to-all(bf16[4,128,1024]{2,1,0:T(8,128)(2,1)S(1)} %dynamic-slice_bitcast_fusion), channel_id=1, replica_groups=mesh['seq'=4,'chip'=4,'core'=2] {'seq'}, dimensions={0} | all-to-all | bytes 2097152 | tf_op jit(solution)/shard_map/all_to_all | solution.py:315
  780.2 23.9 %reduce-scatter.17.cloned.1.call-done = bf16[256,2048]{1,0:T(8,128)(2,1)} async-done(((bf16[1024,2048]{1,0:T(8,128)(2,1)}), bf16[256,2048]{1,0:T(8,128)(2,1)}) %reduce-scatter.17.cloned.1.call-update) | async-done | bytes 1048592 | tf_op jit(solution)/shard_map/reduce_scatter | solution.py:307
  804.1 29.9 %all-gather.18.cloned.1.call-done = bf16[512,2048]{1,0:T(8,128)(2,1)} async-done(((bf16[64,2048]{1,0:T(8,128)(2,1)}), bf16[512,2048]{1,0:T(8,128)(2,1)}) %all-gather.18.cloned.1.call-update) | async-done | bytes 2097168 | tf_op jit(solution)/shard_map/all_gather | solution.py:308
  838.2 123.4 %all-reduce.6.cloned.1.call-done = f32[24576]{0:T(1024)} async-done(((f32[24576]{0:T(1024)}), f32[24576]{0:T(1024)}) %all-reduce.6.cloned.1.call-update) | async-done | bytes 98320 | tf_op jit(solution)/shard_map/psum | solution.py:298
  965.6 45.0 %all-gather.26.cloned.1.call-done = bf16[32,128,768]{2,1,0:T(8,128)(2,1)} async-done(((bf16[4,128,768]{2,1,0:T(8,128)(2,1)}), bf16[32,128,768]{2,1,0:T(8,128)(2,1)}) %all-gather.26.cloned.1.call-update) | async-done | bytes 6291472 | tf_op jit(solution)/shard_map/all_gather | solution.py:316
  1010.6 8.8 copy.101
  1019.5 10.0 convert_bitcast_fusion.1
  1029.4 19.3 %copy.102 = f32[4,128,3,4,2,256]{5,4,3,2,1,0:T(2,128)} copy(f32[4,128,3,4,2,256]{1,5,2,3,4,0:T(8,128)} %convert_bitcast_fusion.1) | data formatting | bytes 25165824 | tf_op jit(solution)/shard_map/convert_element_type | solution.py:319
  1048.8 16.4 %reshape.441 = f32[512,6144]{1,0:T(8,128)} reshape(f32[4,128,3,4,2,256]{5,4,3,2,1,0:T(2,128)} %copy.102) | data formatting | bytes 25165824 | tf_op jit(solution)/shard_map/convert_element_type | solution.py:319
  1066.9 12.2 %convert_bitcast_fusion = f32[4,128,1,4,2,1024]{5,1,3,4,0,2:T(8,128)} fusion(bf16[4,2,4,128,1,1024]{5,3,2,1,0,4:T(8,128)(2,1)} %bitcast.188), kind=kLoop, calls=%fused_computation | loop fusion | flops 4194304 | bytes 25165824 | tf_op jit(solution)/shard_map/convert_element_type | solution.py:319
  1079.1 28.7 %copy.103 = f32[4,128,1,4,2,1024]{5,4,3,1,0,2:T(2,128)} copy(f32[4,128,1,4,2,1024]{5,1,3,4,0,2:T(8,128)} %convert_bitcast_fusion) | data formatting | bytes 33554432 | tf_op jit(solution)/shard_map/convert_element_type | solution.py:319
  1107.8 22.3 %reshape.442 = f32[512,8192]{1,0:T(8,128)} reshape(f32[4,128,1,4,2,1024]{5,4,3,1,0,2:T(2,128)} %copy.103) | data formatting | bytes 33554432 | tf_op jit(solution)/shard_map/convert_element_type | solution.py:319
  1130.1 11.7 %convert_element_type.293 = f32[2048,2048]{1,0:T(8,128)} convert(bf16[2048,2048]{1,0:T(8,128)(2,1)} %all-gather.20.cloned.1.call-done) | non-fusion elementwise | flops 4194304 | bytes 25165824 | tf_op jit(solution)/shard_map/convert_element_type | solution.py:309
  (201 shorter events, 117.6 us)
Async XLA Ops:
  7.2 222.2 %copy-start = (bf16[512,2048]{1,0:T(8,128)(2,1)S(1)}, bf16[512,2048]{1,0:T(8,128)(2,1)}, u32[]{:S(2)}) copy-start(bf16[512,2048]{1,0:T(8,128)(2,1)} %param.24) | copy-start | bytes 6291460
  7.2 133.1 %all-gather.14.cloned.1.call-start = ((), (), s32[]{:S(2)}) async-start(), calls=%async_computation.13 | async-start | bytes 7077888 | tf_op jit(solution)/shard_map/all_gather | solution.py:161
  7.9 143.2 %all-gather.22.cloned.1.call-start = ((), (), s32[]{:S(2)}) async-start(), calls=%async_computation.22 | async-start | bytes 7077888 | tf_op jit(solution)/shard_map/all_gather | solution.py:171
  71.1 158.2 %all-gather.16.cloned.1.call-start = ((), (), s32[]{:S(2)}) async-start(), calls=%async_computation.15 | async-start | bytes 7077888 | tf_op jit(solution)/shard_map/all_gather | solution.py:162
  71.9 319.8 %all-gather.24.cloned.1.call-start = ((), (), s32[]{:S(2)}) async-start(), calls=%async_computation.23 | async-start | bytes 9437184 | tf_op jit(solution)/shard_map/all_gather | solution.py:171
  86.5 30.8 %copy-start.24 = (u32[32]{0:T(128)S(1)}, u32[32]{0:T(128)}, u32[]{:S(2)}) copy-start(u32[32]{0:T(128)} %constant.154) | copy-start | bytes 388
  86.6 32.0 %copy-start.16 = (bf16[512]{0:T(512)(128)(2,1)S(1)}, bf16[512]{0:T(512)(128)(2,1)}, u32[]{:S(2)}) copy-start(bf16[512]{0:T(512)(128)(2,1)} %param.18) | copy-start | bytes 3076
  86.6 32.3 %copy-start.17 = (bf16[512]{0:T(512)(128)(2,1)S(1)}, bf16[512]{0:T(512)(128)(2,1)}, u32[]{:S(2)}) copy-start(bf16[512]{0:T(512)(128)(2,1)} %param.19) | copy-start | bytes 3076
  86.6 32.5 %copy-start.18 = (bf16[512]{0:T(512)(128)(2,1)S(1)}, bf16[512]{0:T(512)(128)(2,1)}, u32[]{:S(2)}) copy-start(bf16[512]{0:T(512)(128)(2,1)} %param.20) | copy-start | bytes 3076
  86.6 32.7 %copy-start.19 = (bf16[512]{0:T(512)(128)(2,1)S(1)}, bf16[512]{0:T(512)(128)(2,1)}, u32[]{:S(2)}) copy-start(bf16[512]{0:T(512)(128)(2,1)} %param.21) | copy-start | bytes 3076
  86.6 32.9 %copy-start.14 = (bf16[1536]{0:T(1024)(128)(2,1)S(1)}, bf16[1536]{0:T(1024)(128)(2,1)}, u32[]{:S(2)}) copy-start(bf16[1536]{0:T(1024)(128)(2,1)} %param.23) | copy-start | bytes 9220
  86.6 33.2 %copy-start.20 = (bf16[512]{0:T(512)(128)(2,1)S(1)}, bf16[512]{0:T(512)(128)(2,1)}, u32[]{:S(2)}) copy-start(bf16[512]{0:T(512)(128)(2,1)} %param.25) | copy-start | bytes 3076
  86.6 33.4 %copy-start.15 = (bf16[2048]{0:T(1024)(128)(2,1)S(1)}, bf16[2048]{0:T(1024)(128)(2,1)}, u32[]{:S(2)}) copy-start(bf16[2048]{0:T(1024)(128)(2,1)} %param.27) | copy-start | bytes 12292
  86.6 33.4 %copy-start.21 = (bf16[512]{0:T(512)(128)(2,1)S(1)}, bf16[512]{0:T(512)(128)(2,1)}, u32[]{:S(2)}) copy-start(bf16[512]{0:T(512)(128)(2,1)} %param.29) | copy-start | bytes 3076
  86.6 33.6 %copy-start.22 = (s32[1,16]{1,0:T(1,128)S(1)}, s32[1,16]{1,0:T(1,128)}, u32[]{:S(2)}) copy-start(s32[1,16]{1,0:T(1,128)} %param.16) | copy-start | bytes 196
  139.9 6.8 copy-start.8
  140.3 4.6 copy-start.1
  224.7 35.3 %all-to-all-start.1 = ((bf16[4,3,384,256]{3,2,1,0:T(8,128)(2,1)}), bf16[4,3,384,256]{3,2,1,0:T(8,128)(2,1)}, u32[]{:S(2)}, u32[]{:S(2)}) async-start(bf16[4,3,384,256]{3,2,1,0:T(8,128)(2,1)} %maximum_bitcast_fusion), calls=%async_computation.1 | async-start | bytes 4718592 | tf_op jit(solution)/shard_map/all_to_all | solution.py:205
  260.0 22.8 %all-to-all-start.4 = ((bf16[4,1,384,256]{3,2,1,0:T(8,128)(2,1)}), bf16[4,1,384,256]{3,2,1,0:T(8,128)(2,1)S(1)}, u32[]{:S(2)}, u32[]{:S(2)}) async-start(bf16[4,1,384,256]{3,2,1,0:T(8,128)(2,1)} %bitcast.37), calls=%async_computation.5 | async-start | bytes 1572864 | tf_op jit(solution)/shard_map/all_to_all | solution.py:205
  263.5 4.3 copy-start.12
  282.7 0.9 copy-start.6
  283.6 44.2 %all-to-all-start.2 = ((bf16[4,1,384,256]{3,2,1,0:T(8,128)(2,1)}), bf16[4,1,384,256]{3,2,1,0:T(8,128)(2,1)S(1)}, u32[]{:S(2)}, u32[]{:S(2)}) async-start(bf16[4,1,384,256]{3,2,1,0:T(8,128)(2,1)} %bitcast.222), calls=%async_computation.2 | async-start | bytes 1572864 | tf_op jit(solution)/shard_map/all_to_all | solution.py:211
  300.1 9.3 copy-start.4
  327.8 34.7 %all-to-all-start.5 = ((bf16[4,3,384,256]{2,3,1,0:T(8,128)(2,1)}), bf16[4,3,384,256]{2,3,1,0:T(8,128)(2,1)}, u32[]{:S(2)}, u32[]{:S(2)}) async-start(bf16[4,3,384,256]{2,3,1,0:T(8,128)(2,1)} %maximum_bitcast_fusion.1), calls=%async_computation.6 | async-start | bytes 4718592 | tf_op jit(solution)/shard_map/all_to_all | solution.py:211
  332.3 192.7 %reduce-scatter.15.cloned.1.call-start = ((), (), s32[]{:S(2)}) async-start(), calls=%async_computation.18 | async-start | bytes 1310720 | tf_op jit(solution)/shard_map/reduce_scatter | solution.py:307
  338.7 189.9 %reduce-scatter.19.cloned.1.call-start = ((), (), s32[]{:S(2)}) async-start(), calls=%async_computation.27 | async-start | bytes 3932160
  366.4 10.4 copy-start.5
  391.6 175.4 %reduce-scatter.13.cloned.1.call-start = ((), (), s32[]{:S(2)}) async-start(), calls=%async_computation.16 | async-start | bytes 7077888 | tf_op jit(solution)/shard_map/reduce_scatter | solution.py:270
  415.1 37.2 %slice-start = ((s8[6291456]{0:T(1024)(128)(4,1)}), s8[4194304]{0:T(1024)(128)(4,1)S(1)}, s32[]{:S(2)}) async-start(s8[6291456]{0:T(1024)(128)(4,1)} %bitcast.178), calls=%async_computation.28 | async-start | bytes 8388608
  425.3 26.9 %copy-start.3 = (bf16[2048,1,1,1024]{3,2,0,1:T(2,128)(2,1)}, bf16[2048,1,1,1024]{3,2,0,1:T(2,128)(2,1)S(1)}, u32[]{:S(2)}) copy-start(bf16[2048,1,1,1024]{3,2,0,1:T(2,128)(2,1)S(1)} %constant_dynamic-slice_fusion) | copy-start | bytes 12582916
  425.3 26.9 %slice-start.1 = ((s8[6291456]{0:T(1024)(128)(4,1)}), s8[2097152]{0:T(1024)(128)(4,1)S(1)}, s32[]{:S(2)}) async-start(s8[6291456]{0:T(1024)(128)(4,1)} %bitcast.178), calls=%async_computation.29 | async-start | bytes 4194304
  452.3 14.3 %copy-start.9 = (f32[1,4,4,128]{3,1,2,0:T(4,128)S(1)}, f32[1,4,4,128]{3,1,2,0:T(4,128)}, u32[]{:S(2)}) copy-start(f32[1,4,4,128]{3,1,2,0:T(4,128)} %copy-done.8) | copy-start | bytes 24580
  486.7 154.8 %reduce-scatter.11.cloned.1.call-start = ((), (), s32[]{:S(2)}) async-start(), calls=%async_computation.14 | async-start | bytes 7077888 | tf_op jit(solution)/shard_map/reduce_scatter | solution.py:242
  501.1 246.9 %all-reduce.8.cloned.1.call-start = ((), (), s32[]{:S(2)}) async-start(), calls=%async_computation.26 | async-start | bytes 8388608
  513.6 12.1 %copy-start.11 = (f32[1,4,4,128]{3,2,1,0:T(4,128)S(1)}, f32[1,4,4,128]{3,2,1,0:T(4,128)}, u32[]{:S(2)}) copy-start(f32[1,4,4,128]{3,2,1,0:T(4,128)} %get-tuple-element.58) | copy-start | bytes 24580
  513.6 12.2 %copy-start.10 = (f32[1,4,4,128]{3,2,1,0:T(4,128)S(1)}, f32[1,4,4,128]{3,2,1,0:T(4,128)}, u32[]{:S(2)}) copy-start(f32[1,4,4,128]{3,2,1,0:T(4,128)} %get-tuple-element.59) | copy-start | bytes 24580
  513.6 12.2 %copy-start.2 = (bf16[192,2048]{1,0:T(8,128)(2,1)S(1)}, bf16[192,2048]{1,0:T(8,128)(2,1)}, u32[]{:S(2)}) copy-start(bf16[192,2048]{1,0:T(8,128)(2,1)} %param.15) | copy-start | bytes 2359300
  513.6 290.5 %reduce-scatter.17.cloned.1.call-start = ((), (), s32[]{:S(2)}) async-start(), calls=%async_computation.20 | async-start | bytes 5242880 | tf_op jit(solution)/shard_map/reduce_scatter | solution.py:307
  525.0 309.1 %all-gather.18.cloned.1.call-start = ((), (), s32[]{:S(2)}) async-start(), calls=%async_computation.19 | async-start | bytes 2359296 | tf_op jit(solution)/shard_map/all_gather | solution.py:308
  526.3 122.2 %copy-start.23 = (u32[32]{0:T(128)S(1)}, u32[32]{0:T(128)}, u32[]{:S(2)}) copy-start(u32[32]{0:T(128)} %constant.160) | copy-start | bytes 388
  528.7 117.5 %all-to-all-start.6 = ((bf16[4,128,768]{1,2,0:T(8,128)(2,1)}), bf16[4,128,768]{1,2,0:T(8,128)(2,1)}, u32[]{:S(2)}, u32[]{:S(2)}) async-start(bf16[4,128,768]{1,2,0:T(8,128)(2,1)} %bitcast.221), calls=%async_computation.8 | async-start | bytes 1572864 | tf_op jit(solution)/shard_map/all_to_all | solution.py:315
  532.9 428.7 %all-reduce.6.cloned.1.call-start = ((), (), s32[]{:S(2)}) async-start(), calls=%async_computation.17 | async-start | bytes 196608 | tf_op jit(solution)/shard_map/psum | solution.py:298
  645.4 0.6 copy-start.7
  646.1 364.5 %all-gather.26.cloned.1.call-start = ((), (), s32[]{:S(2)}) async-start(), calls=%async_computation.24 | async-start | bytes 7077888 | tf_op jit(solution)/shard_map/all_gather | solution.py:316
  648.5 418.5 %all-gather.28.cloned.1.call-start = ((), (), s32[]{:S(2)}) async-start(), calls=%async_computation.25 | async-start | bytes 9437184 | tf_op jit(solution)/shard_map/all_gather | solution.py:316
  780.2 349.9 %all-gather.20.cloned.1.call-start = ((), (), s32[]{:S(2)}) async-start(), calls=%async_computation.21 | async-start | bytes 9437184 | tf_op jit(solution)/shard_map/all_gather | solution.py:308
  963.0 178.8 %copy-start.13 = (f32[512]{0:T(512)}, f32[512]{0:T(512)S(1)}, u32[]{:S(2)}) copy-start(f32[512]{0:T(512)S(1)} %get-tuple-element.100) | copy-start | bytes 6148
Sparse Core Ops, SparseCore 0:
  9.7 83.9 all-gather.13
  95.5 44.1 all-gather.21
  141.4 64.6 all-gather.15
  207.8 79.0 all-gather.23
  338.9 33.3 reduce-scatter.14
  391.8 41.6 reduce-scatter.18
  486.8 80.1 reduce-scatter.12
  570.0 71.4 reduce-scatter.10
  645.7 102.2 all-reduce.7
  751.4 52.6 reduce-scatter.16
  806.2 27.8 all-gather.17
  841.0 120.5 all-reduce.5
  964.2 46.3 all-gather.25
  1012.5 54.3 all-gather.27
  1068.8 54.3 all-gather.19

commit v2 on v1

--- a/solution.py
+++ b/solution.py
@@ -18,6 +18,561 @@
 f32 = jnp.float32
 bf16 = jnp.bfloat16
 TP = ("seq", "core")
+MESH = pl.DeviceIdType.MESH
+
+
+def remote(src, dst, send, recv, target):
+    return pltpu.make_async_remote_copy(
+        src_ref=src, dst_ref=dst, send_sem=send, recv_sem=recv, device_id=target,
+        device_id_type=MESH,
+    )
+
+
+def greet(targets):
+    barrier = pltpu.get_barrier_semaphore()
+    for target in targets:
+        pl.semaphore_signal(barrier, inc=1, device_id=target, device_id_type=MESH)
+    pl.semaphore_wait(barrier, len(targets))
+
+
+def front(nz, nchip, ncore, tokens, w_in, w_qkv):
+    own, width = tokens.shape
+    wrows, ff = w_in.shape
+    heads3 = w_qkv.shape[1]
+    nctx = nchip * ncore
+    piece = wrows // nctx
+    zi, zq = ff // nz, heads3 // 3 // nz
+    ci, cq = zi // ncore, zq // ncore
+
+    def kernel(
+        tok_ref, wi_ref, wq_ref, tok_out, wi_out, wq_out, buf_i, buf_q,
+        up_s, up_r, dn_s, dn_r, sib_s, sib_r, zi_s, zi_r, zq_s, zq_r, pi_s, pi_r, pq_s, pq_r, loc,
+    ):
+        z = lax.axis_index("seq")
+        chip = lax.axis_index("chip")
+        core = lax.axis_index("core")
+        share = chip * ncore + core
+        sibling = {"core": 1 - core}
+
+        def z_at(d):
+            return lax.rem(z + d, nz)
+
+        def plane_at(d):
+            other = lax.rem(share + d, nctx)
+            return other // ncore, lax.rem(other, ncore)
+
+        greet(
+            [{"seq": z_at(d)} for d in range(1, nz)]
+            + [{"chip": plane_at(d)[0], "core": plane_at(d)[1]} for d in range(1, nctx)]
+        )
+
+        rows = pl.ds(share * piece, piece)
+        hop = []
+        for d in range(1, nz):
+            to = z_at(d)
+            hop.append(
+                remote(
+                    wi_ref.at[rows, pl.ds(to * zi, zi)], buf_i.at[z], zi_s.at[d], zi_r.at[z],
+                    {"seq": to},
+                )
+            )
+            for g in range(3):
+                hop.append(
+                    remote(
+                        wq_ref.at[rows, pl.ds(g * zq * nz + to * zq, zq)], buf_q.at[z, g],
+                        zq_s.at[d, g], zq_r.at[z, g], {"seq": to},
+                    )
+                )
+        def up(s):
+            shard = z - s
+            src = tok_ref if s == 0 else tok_out.at[jnp.maximum(shard, 0), core]
+            return remote(
+                src, tok_out.at[jnp.maximum(shard, 0), core], up_s.at[s], up_r.at[s],
+                {"seq": jnp.minimum(z + 1, nz - 1)},
+            )
+
+        def down(s):
+            shard = z + s
+            src = tok_ref if s == 0 else tok_out.at[jnp.minimum(shard, nz - 1), core]
+            return remote(
+                src, tok_out.at[jnp.minimum(shard, nz - 1), core], dn_s.at[s], dn_r.at[s],
+                {"seq": jnp.maximum(z - 1, 0)},
+            )
+
+        def side(shard, own_rows=False):
+            src = tok_ref if own_rows else tok_out.at[shard, core]
+            return remote(src, tok_out.at[shard, core], sib_s.at[shard], sib_r.at[shard], sibling)
+
+        for copy in hop:
+            copy.start()
+
+        @pl.when(z + 1 < nz)
+        def _():
+            up(0).start()
+
+        @pl.when(z > 0)
+        def _():
+            down(0).start()
+
+        side(z, True).start()
+        locals_ = [
+            pltpu.make_async_copy(tok_ref, tok_out.at[z, core], loc.at[0]),
+            pltpu.make_async_copy(wi_ref.at[rows, pl.ds(z * zi, zi)], buf_i.at[z], loc.at[1]),
+        ] + [
+            pltpu.make_async_copy(
+                wq_ref.at[rows, pl.ds(g * zq * nz + z * zq, zq)], buf_q.at[z, g], loc.at[2 + g]
+            )
+            for g in range(3)
+        ]
+        for copy in locals_:
+            copy.start()
+
+        def spread_i(source, d):
+            to_chip, to_core = plane_at(d)
+            dst = wi_out.at[pl.ds(source * wrows + share * piece, piece), :]
+            src = buf_i.at[source, :, pl.ds(to_core * ci, ci)]
+            return src, dst, to_chip, to_core
+
+        def spread(source, d):
+            to_chip, to_core = plane_at(d)
+            target_rows = pl.ds(source * wrows + share * piece, piece)
+            pairs = [
+                (
+                    buf_i.at[source, :, pl.ds(to_core * ci, ci)], wi_out.at[target_rows, :],
+                    pi_s.at[source, d], pi_r.at[source, share],
+                )
+            ] + [
+                (
+                    buf_q.at[source, g, :, pl.ds(to_core * cq, cq)],
+                    wq_out.at[target_rows, pl.ds(g * cq, cq)],
+                    pq_s.at[source, d, g], pq_r.at[source, share, g],
+                )
+                for g in range(3)
+            ]
+            if d == 0:
+                return [pltpu.make_async_copy(a, b, c) for a, b, c, r in pairs]
+            return [remote(a, b, c, r, {"chip": to_chip, "core": to_core}) for a, b, c, r in pairs]
+
+        def hop_arrival(source):
+            remote(buf_i.at[source], buf_i.at[source], zi_s.at[0], zi_r.at[source], sibling).wait_recv()
+            for g in range(3):
+                remote(
+                    buf_q.at[source, g], buf_q.at[source, g], zq_s.at[0, 0], zq_r.at[source, g],
+                    sibling,
+                ).wait_recv()
+
+        for copy in locals_[1:]:
+            copy.wait()
+        for d in range(nctx):
+            for copy in spread(z, d):
+                copy.start()
+        for dz in range(1, nz):
+            source = z_at(dz if dz % 2 else nz - dz // 2) if False else z_at(dz)
+            hop_arrival(source)
+            for d in range(nctx):
+                for copy in spread(source, d):
+                    copy.start()
+
+        for s in range(nz - 1):
+            from_below = z - 1 - s
+            from_above = z + 1 + s
+
+            @pl.when(from_below >= 0)
+            def _():
+                shard = jnp.maximum(from_below, 0)
+                remote(tok_ref, tok_out.at[shard, core], up_s.at[s], up_r.at[s], sibling).wait_recv()
+                if s + 1 < nz - 1:
+                    @pl.when(z + 1 < nz)
+                    def _():
+                        up(s + 1).start()
+                side(shard).start()
+
+            @pl.when(from_above < nz)
+            def _():
+                shard = jnp.minimum(from_above, nz - 1)
+                remote(tok_ref, tok_out.at[shard, core], dn_s.at[s], dn_r.at[s], sibling).wait_recv()
+                if s + 1 < nz - 1:
+                    @pl.when(z > 0)
+                    def _():
+                        down(s + 1).start()
+                side(shard).start()
+
+        locals_[0].wait()
+        for shard in range(nz):
+            remote(tok_ref, tok_out.at[shard, 1 - core], sib_s.at[shard], sib_r.at[shard], sibling).wait()
+        for s in range(nz - 1):
+            @pl.when(jnp.logical_and(z + 1 < nz, z - s >= 0))
+            def _():
+                up(s).wait_send()
+
+            @pl.when(jnp.logical_and(z > 0, z + s < nz))
+            def _():
+                down(s).wait_send()
+        for copy in hop:
+            copy.wait_send()
+        for source in range(nz):
+            for d in range(nctx):
+                if d == 0:
+                    for copy in spread(source, d):
+                        copy.wait()
+                    continue
+                for copy in spread(source, d):
+                    copy.wait_send()
+                other = lax.rem(share + d, nctx)
+                rows_there = pl.ds(source * wrows + other * piece, piece)
+                remote(
+                    wi_out.at[rows_there, :], wi_out.at[rows_there, :], pi_s.at[source, d],
+                    pi_r.at[source, other], sibling,
+                ).wait_recv()
+                for g in range(3):
+                    cols = pl.ds(g * cq, cq)
+                    remote(
+                        wq_out.at[rows_there, cols], wq_out.at[rows_there, cols],
+                        pq_s.at[source, d, g], pq_r.at[source, other, g], sibling,
+                    ).wait_recv()
+
+    dma = pltpu.SemaphoreType.DMA
+    anywhere = pl.BlockSpec(memory_space=pl.ANY)
+    return pl.pallas_call(
+        kernel,
+        in_specs=[anywhere] * 3,
+        out_specs=[anywhere] * 3,
+        out_shape=[
+            jax.ShapeDtypeStruct((nz, ncore, own, width), bf16),
+            jax.ShapeDtypeStruct((nz * wrows, ci), bf16),
+            jax.ShapeDtypeStruct((nz * wrows, 3 * cq), bf16),
+        ],
+        scratch_shapes=[
+            pltpu.VMEM((nz, piece, zi), bf16),
+            pltpu.VMEM((nz, 3, piece, zq), bf16),
+            dma((nz,)), dma((nz,)), dma((nz,)), dma((nz,)),
+            dma((nz,)), dma((nz,)),
+            dma((nz,)), dma((nz,)), dma((nz, 3)), dma((nz, 3)),
+            dma((nz, nctx)), dma((nz, nctx)), dma((nz, nctx, 3)), dma((nz, nctx, 3)),
+            dma((5,)),
+        ],
+        compiler_params=pltpu.CompilerParams(collective_id=1, has_side_effects=True),
+        name="front",
+    )(tokens, w_in, w_qkv)
+
+
+def tail(nz, nchip, ncore, dwo, dwd, dwi, dwq, part_e, part_o, vectors):
+    width = dwo.shape[1]
+    ro, rd = dwo.shape[0] // nchip, dwd.shape[0] // nchip
+    ci, cq = dwi.shape[1], dwq.shape[1] // 3
+    wrows = width // nz
+    ri = wrows // nchip
+    own = part_e.shape[0] // nz // ncore
+    vr = vectors.shape[0]
+    dwi = dwi.reshape(nz, nchip, ri, ci)
+    dwq = dwq.reshape(nz, nchip, ri, 3 * cq)
+    part_e = part_e.reshape(nz, ncore, own, width)
+    part_o = part_o.reshape(nz, ncore, own, width)
+
+    def kernel(
+        dwo_ref, dwd_ref, dwi_ref, dwq_ref, pe_ref, po_ref, vec_ref,
+        go_ref, gd_ref, gi_ref, gq_ref, e_ref, o_ref, vsum_ref,
+        bo, bd, bi, bq, ti, tq, se, so, me, mo, ze, zo, v1, v2, v3,
+        rs_s, rs_r, rs_l, x_s, x_r, x_l, ez_s, ez_r, t_s, t_r, t_l,
+        go_s, go_r, gd_s, gd_r, gi_s, gi_r, gq_s, gq_r, own_l, fin_l,
+        v_s, v_r, v_l,
+    ):
+        z = lax.axis_index("seq")
+        chip = lax.axis_index("chip")
+        core = lax.axis_index("core")
+        sibling = {"core": 1 - core}
+
+        def z_at(d):
+            return lax.rem(z + d, nz)
+
+        def chip_at(d):
+            return lax.rem(chip + d, nchip)
+
+        greet(
+            [{"seq": z_at(d)} for d in range(1, nz)]
+            + [{"chip": chip_at(d)} for d in range(1, nchip)]
+            + [sibling]
+        )
+
+        halves = [
+            remote(pe_ref.at[:, 1 - core], se, x_s.at[0], x_r.at[0], sibling),
+            remote(po_ref.at[:, 1 - core], so, x_s.at[1], x_r.at[1], sibling),
+        ]
+        keep = [
+            pltpu.make_async_copy(pe_ref.at[:, core], me, x_l.at[0]),
+            pltpu.make_async_copy(po_ref.at[:, core], mo, x_l.at[1]),
+        ]
+        for copy in halves + keep:
+            copy.start()
+
+        def rs(d):
+            to = chip_at(d)
+            pairs = [
+                (dwi_ref.at[:, to], bi.at[d]),
+                (dwq_ref.at[:, to], bq.at[d]),
+                (dwo_ref.at[pl.ds(to * ro, ro), :], bo.at[d]),
+                (dwd_ref.at[pl.ds(to * rd, rd), :], bd.at[d]),
+            ]
+            if d == 0:
+                return [pltpu.make_async_copy(a, b, rs_l.at[i]) for i, (a, b) in enumerate(pairs)]
+            return [
+                remote(a, b, rs_s.at[d, i], rs_r.at[d, i], {"chip": to})
+                for i, (a, b) in enumerate(pairs)
+            ]
+
+        scattered = [rs(d) for d in range(nchip)]
+        for kind in range(4):
+            for d in range(1, nchip):
+                scattered[d][kind].start()
+            scattered[0][kind].start()
+
+        v_own = pltpu.make_async_copy(vec_ref, v1.at[chip], v_l.at[0])
+        v_own.start()
+        v_chips = [
+            remote(vec_ref, v1.at[chip], v_s.at[d], v_r.at[chip], {"chip": chip_at(d)})
+            for d in range(1, nchip)
+        ]
+        for copy in v_chips:
+            copy.start()
+
+        def add_rows(total, count, step, body):
+            @pl.loop(0, count // step)
+            def _(i):
+                body(pl.ds(pl.multiple_of(i * step, step), step))
+
+        z_copies = []
+        for which, (mine, theirs, landing) in enumerate(((me, se, ze), (mo, so, zo))):
+            halves[which].wait_recv()
+            keep[which].wait()
+
+            @pl.loop(0, nz)
+            def _(b):
+                @pl.loop(0, own // 16)
+                def _(i):
+                    at = pl.ds(pl.multiple_of(i * 16, 16), 16)
+                    mine[b, at, :] = (
+                        mine[b, at, :].astype(f32) + theirs[b, at, :].astype(f32)
+                    ).astype(bf16)
+
+            for d in range(1, nz):
+                copy = remote(
+                    mine.at[z_at(d)], landing.at[d], ez_s.at[which, d], ez_r.at[which, d],
+                    {"seq": z_at(d)},
+                )
+                copy.start()
+                z_copies.append(copy)
+
+        v_own.wait()
+        for d in range(1, nchip):
+            other = chip_at(d)
+            remote(vec_ref, v1.at[other], v_s.at[d], v_r.at[other], sibling).wait_recv()
+        total = v1[0]
+        for d in range(1, nchip):
+            total = total + v1[d]
+        v2[core] = total
+        v_side = remote(v2.at[core], v2.at[core], v_s.at[nchip], v_r.at[nchip], sibling)
+        v_side.start()
+
+        def add_four(buf, count, pieces):
+            @pl.loop(0, count // 16)
+            def _(i):
+                at = pl.ds(pl.multiple_of(i * 16, 16), 16)
+                acc = buf[(0,) + pieces + (at,)].astype(f32)
+                for d in range(1, nchip):
+                    acc = acc + buf[(d,) + pieces + (at,)].astype(f32)
+                buf[(0,) + pieces + (at,)] = acc.astype(bf16)
+
+        turns = []
+        for kind, (buf, turned) in enumerate(((bi, ti), (bq, tq))):
+            scattered[0][kind].wait()
+            for d in range(1, nchip):
+                scattered[d][kind].wait_recv()
+
+            @pl.loop(0, nz)
+            def _(b):
+                add_four(buf, ri, (b,))
+
+            for d in range(1, nz):
+                to = z_at(d)
+                copy = remote(
+                    buf.at[0, to], turned.at[z], t_s.at[kind, d], t_r.at[kind, z], {"seq": to}
+                )
+                copy.start()
+                turns.append(copy)
+            local = pltpu.make_async_copy(buf.at[0, z], turned.at[z], t_l.at[kind])
+            local.start()
+            turns.append(local)
+
+        v_side.wait_recv()
+        vz = v2[0]
+        for c in range(1, ncore):
+            vz = vz + v2[c]
+        v3[z] = vz
+        v_zs = [
+            remote(v3.at[z], v3.at[z], v_s.at[nchip + d], v_r.at[nchip + 1 + z], {"seq": z_at(d)})
+            for d in range(1, nz)
+        ]
+        for copy in v_zs:
+            copy.start()
+
+        def spread(src, dst_of, send, recv, local):
+            copies = [pltpu.make_async_copy(src, dst_of(chip, core), local)]
+            copies += [
+                remote(src, dst_of(chip, core), send.at[d], recv.at[chip], {"chip": chip_at(d)})
+                for d in range(1, nchip)
+            ]
+            copies.append(
+                remote(
+                    src, dst_of(chip, core), send.at[nchip + chip], recv.at[nchip + chip], sibling
+                )
+            )
+            for copy in copies:
+                copy.start()
+            return copies
+
+        go_at = lambda c, k: go_ref.at[pl.ds(k * (ro * nchip) + c * ro, ro), :]
+        gd_at = lambda c, k: gd_ref.at[pl.ds(k * (rd * nchip) + c * rd, rd), :]
+        gi_at = lambda c, k, s: gi_ref.at[
+            pl.ds(c * ri, ri), pl.ds((s * ncore + k) * ci, ci)
+        ]
+        gq_at = lambda c, k, s, g: gq_ref.at[
+            pl.ds(c * ri, ri), pl.ds(g * nz * ncore * cq + (s * ncore + k) * cq, cq)
+        ]
+        groups = []
+        for kind, (buf, count) in enumerate(((bo, ro), (bd, rd))):
+            scattered[0][2 + kind].wait()
+            for d in range(1, nchip):
+                scattered[d][2 + kind].wait_recv()
+            add_four(buf, count, ())
+            group = (
+                (bo.at[0], go_at, go_s, go_r, own_l.at[0])
+                if kind == 0
+                else (bd.at[0], gd_at, gd_s, gd_r, own_l.at[1])
+            )
+            groups.append(group + (spread(*group),))
+        for dz in range(nz):
+            source = z_at(dz)
+            if dz > 0:
+                remote(bi.at[0, 0], ti.at[source], t_s.at[0, dz], t_r.at[0, source], sibling).wait_recv()
+            else:
+                turns[nz - 1].wait()
+            group = (
+                ti.at[source], functools.partial(gi_at, s=source), gi_s.at[source], gi_r.at[source],
+                own_l.at[2 + source],
+            )
+            groups.append(group + (spread(*group),))
+        for dz in range(nz):
+            source = z_at(dz)
+            if dz > 0:
+                remote(bq.at[0, 0], tq.at[source], t_s.at[1, dz], t_r.at[1, source], sibling).wait_recv()
+            else:
+                turns[2 * nz - 1].wait()
+            for g in range(3):
+                group = (
+                    tq.at[source, :, pl.ds(g * cq, cq)],
+                    functools.partial(gq_at, s=source, g=g),
+                    gq_s.at[source, g], gq_r.at[source, g], own_l.at[2 + nz + 3 * source + g],
+                )
+                groups.append(group + (spread(*group),))
+
+        for which, (mine, landing, out) in enumerate(((me, ze, e_ref), (mo, zo, o_ref))):
+            for d in range(1, nz):
+                z_copies[which * (nz - 1) + d - 1].wait_recv()
+
+            @pl.loop(0, own // 16)
+            def _(i):
+                at = pl.ds(pl.multiple_of(i * 16, 16), 16)
+                acc = mine[z, at, :].astype(f32)
+                for d in range(1, nz):
+                    acc = acc + landing[d, at, :].astype(f32)
+                out[at, :] = acc
+
+        for d in range(1, nz):
+            other = z_at(d)
+            remote(v3.at[0], v3.at[other], v_s.at[0], v_r.at[nchip + 1 + other], sibling).wait_recv()
+        total = v3[0]
+        for d in range(1, nz):
+            total = total + v3[d]
+        vsum_ref[...] = total
+
+        passed = []
+        for src, dst_of, send, recv, local, copies in groups:
+            for d in range(1, nchip):
+                other = chip_at(d)
+                here = dst_of(other, core)
+                remote(here, here, send.at[0], recv.at[other], sibling).wait_recv()
+                copy = remote(here, here, send.at[nchip + other], recv.at[nchip + other], sibling)
+                copy.start()
+                passed.append(copy)
+        for src, dst_of, send, recv, local, copies in groups:
+            copies[0].wait()
+            for copy in copies[1:]:
+                copy.wait_send()
+            for d in range(nchip):
+                other = chip_at(d)
+                there = dst_of(other, 1 - core)
+                remote(there, there, send.at[0], recv.at[nchip + other], sibling).wait_recv()
+        for copy in passed:
+            copy.wait_send()
+        for d in range(1, nchip):
+            for copy in scattered[d]:
+                copy.wait_send()
+        for copy in halves + z_copies + v_chips + v_zs + [v_side]:
+            copy.wait_send()
+        for kind in range(2):
+            for d in range(1, nz):
+                turns[kind * nz + d - 1].wait_send()
+
+    dma = pltpu.SemaphoreType.DMA
+    anywhere = pl.BlockSpec(memory_space=pl.ANY)
+    vmem = pl.BlockSpec(memory_space=pltpu.VMEM)
+    out_shape = [
+        jax.ShapeDtypeStruct((ncore * nchip * ro, width), bf16),
+        jax.ShapeDtypeStruct((ncore * nchip * rd, width), bf16),
+        jax.ShapeDtypeStruct((wrows, nz * ncore * ci), bf16),
+        jax.ShapeDtypeStruct((wrows, 3 * nz * ncore * cq), bf16),
+        jax.ShapeDtypeStruct((own, width), f32),
+        jax.ShapeDtypeStruct((own, width), f32),
+        jax.ShapeDtypeStruct((vr, 128), f32),
+    ]
+    ranked = (nz, own, width)
+    return pl.pallas_call(
+        kernel,
+        in_specs=[anywhere] * 6 + [vmem],
+        out_specs=[anywhere] * 4 + [vmem] * 3,
+        out_shape=out_shape,
+        scratch_shapes=[
+            pltpu.VMEM((nchip, ro, width), bf16),
+            pltpu.VMEM((nchip, rd, width), bf16),
+            pltpu.VMEM((nchip, nz, ri, ci), bf16),
+            pltpu.VMEM((nchip, nz, ri, 3 * cq), bf16),
+            pltpu.VMEM((nz, ri, ci), bf16),
+            pltpu.VMEM((nz, ri, 3 * cq), bf16),
+            pltpu.VMEM(ranked, bf16),
+            pltpu.VMEM(ranked, bf16),
+            pltpu.VMEM(ranked, bf16),
+            pltpu.VMEM(ranked, bf16),
+            pltpu.VMEM(ranked, bf16),
+            pltpu.VMEM(ranked, bf16),
+            pltpu.VMEM((nchip, vr, 128), f32),
+            pltpu.VMEM((ncore, vr, 128), f32),
+            pltpu.VMEM((nz, vr, 128), f32),
+            dma((nchip, 4)), dma((nchip, 4)), dma((4,)),
+            dma((2,)), dma((2,)), dma((2,)),
+            dma((2, nz)), dma((2, nz)),
+            dma((2, nz)), dma((2, nz)), dma((2,)),
+            dma((2 * nchip,)), dma((2 * nchip,)),
+            dma((2 * nchip,)), dma((2 * nchip,)),
+            dma((nz, 2 * nchip)), dma((nz, 2 * nchip)),
+            dma((nz, 3, 2 * nchip)), dma((nz, 3, 2 * nchip)),
+            dma((2 + 4 * nz,)), dma((2,)),
+            dma((nchip + nz,)), dma((nchip + nz + 1,)), dma((1,)),
+        ],
+        compiler_params=pltpu.CompilerParams(
+            collective_id=2, has_side_effects=True, vmem_limit_bytes=60 * 2**20
+        ),
+        name="tail",
+    )(dwo, dwd, dwi, dwq, part_e, part_o, vectors)
 
 
 def angles_of(positions):
@@ -158,22 +713,10 @@
     gain1, bias1, gain2, bias2 = [v.astype(f32) for v in (gain1, bias1, gain2, bias2)]
     ids = ids.reshape(nz, -1).astype(jnp.int32)
 
-    tok = lax.all_gather(tokens, TP, axis=0, tiled=True)
-    cot = lax.all_gather(cotangent, TP, axis=0, tiled=True)
-
-    def reshard(w, groups):
-        c = w.shape[1] // groups // ranks
-        mine = lax.dynamic_slice_in_dim(
-            w.reshape(nchip * ncore, piece, groups, nz, ncore * c), chip * ncore + core, 1, 0
-        )[0]
-        mine = mine.transpose(2, 0, 1, 3)
-        got = lax.all_to_all(mine, "seq", 0, 0, tiled=True)
-        every = lax.all_gather(got, ("chip", "core"), axis=0, tiled=False)
-        every = every.transpose(1, 0, 2, 3, 4).reshape(width, groups, ncore, c)
-        return lax.dynamic_index_in_dim(every, core, 2, keepdims=False).reshape(width, groups * c)
-
-    w_in_c = reshard(w_in, 1)
-    w_qkv_c = reshard(w_qkv, 3)
+    tok, w_in_c, w_qkv_c = front(nz, nchip, ncore, tokens, w_in, w_qkv)
+    tok = tok.reshape(rows, width)
+    tok, cot_own = lax.optimization_barrier((tok, cotangent))
+    cot = lax.all_gather(cot_own, TP, axis=0, tiled=True)
     w_out_r = lax.dynamic_slice_in_dim(w_out, core * ffr, ffr, 0)
     w_dense_r = lax.dynamic_slice_in_dim(w_dense, core * hc, hc, 0)
 
@@ -239,14 +782,6 @@
     part_out = jnp.dot(mixed, w_dense_r, preferred_element_type=f32) + jnp.dot(
         active, w_out_r, preferred_element_type=f32
     )
-    summed_out = lax.psum_scatter(part_out.astype(bf16), TP, scatter_dimension=0, tiled=True)
-    output = (
-        tokens.astype(f32)
-        + summed_out.astype(f32)
-        + full_bdense.astype(f32)
-        + full_bout.astype(f32)
-    ).astype(bf16)
-
     tn = (((0,), (0,)), ((), ()))
     nt = (((1,), (1,)), ((), ()))
     grad_active = lax.dot_general(cot, w_out_r, nt, preferred_element_type=f32)
@@ -267,15 +802,6 @@
     gn1 = lax.dot_general(grad_project, w_qkv_c, nt, preferred_element_type=f32)
 
     e_part = (gn1 * gain1 + gn2 * gain2).astype(bf16)
-    e = lax.psum_scatter(e_part, TP, scatter_dimension=0, tiled=True).astype(f32)
-    xhat_own, inv_own = layer_stats(tokens.astype(f32))
-    terms = (
-        e
-        - jnp.mean(e, axis=-1, keepdims=True)
-        - xhat_own * jnp.mean(e * xhat_own, axis=-1, keepdims=True)
-    ) * inv_own
-    grad_tokens = (cotangent.astype(f32) + terms).astype(bf16)
-
     sum_cot = jnp.sum(cotangent.astype(f32), axis=0)
     mine_bin = jnp.zeros((ranks, ffr), f32)
     mine_bin = lax.dynamic_update_slice_in_dim(
@@ -295,7 +821,11 @@
         mine_bin,
     ]
     sizes = [v.shape[0] for v in vectors]
-    sums = lax.psum(jnp.concatenate(vectors), ("seq", "chip", "core"))
+    vectors = jnp.concatenate(vectors).reshape(-1, 128)
+    g_wout, g_wdense, g_win, g_wqkv, e, summed_out, sums = tail(
+        nz, nchip, ncore, dw_out, dw_dense, dw_in, dw_qkv, e_part, part_out.astype(bf16), vectors
+    )
+    sums = sums.reshape(-1)
     at = 0
     small_out = []
     for size in sizes:
@@ -303,25 +833,18 @@
         at += size
     g_gain1, g_bias1, g_gain2, g_bias2, g_bqkv, g_bdense, g_bin = small_out
 
-    def rows_back(dw):
-        part = lax.psum_scatter(dw, "chip", scatter_dimension=0, tiled=True)
-        every = lax.all_gather(part, ("core", "chip"), axis=0, tiled=True)
-        return every.astype(f32)
-
-    def columns_back(dw, groups):
-        c = dw.shape[1] // groups
-        part = dw.reshape(nz, nchip, wrows // nchip, groups * c).transpose(1, 0, 2, 3)
-        part = lax.psum_scatter(part, "chip", scatter_dimension=0, tiled=True)[0]
-        part = lax.all_to_all(part, "seq", 0, 0, tiled=True)
-        every = lax.all_gather(part, ("chip", "core"), axis=0, tiled=False)
-        every = every.reshape(nchip, ncore, nz, wrows // nchip, groups, c)
-        every = every.transpose(0, 3, 4, 2, 1, 5)
-        return every.reshape(wrows, groups * ranks * c).astype(f32)
-
-    g_wout = rows_back(dw_out)
-    g_wdense = rows_back(dw_dense)
-    g_win = columns_back(dw_in, 1)
-    g_wqkv = columns_back(dw_qkv, 3)
+    output = (
+        tokens.astype(f32) + summed_out + full_bdense.astype(f32) + full_bout.astype(f32)
+    ).astype(bf16)
+    xhat_own, inv_own = layer_stats(tokens.astype(f32))
+    terms = (
+        e
+        - jnp.mean(e, axis=-1, keepdims=True)
+        - xhat_own * jnp.mean(e * xhat_own, axis=-1, keepdims=True)
+    ) * inv_own
+    grad_tokens = (cotangent.astype(f32) + terms).astype(bf16)
+
+    g_wout, g_wdense, g_win, g_wqkv = [g.astype(f32) for g in (g_wout, g_wdense, g_win, g_wqkv)]
     return (
         output,
         grad_tokens,

time: 1160 us -> 770 us (0.66)
  waiting for transfers between devices: 484 us -> 28.6 us
  Pallas kernels: 24.1 us -> 419 us
  local copies, waits for them, and re-layouts: 263 us -> 52 us
  blocking collectives: 125 us -> 21.4 us
    pallas_call x0 -> x2, Pallas kernels: none -> 395 us  [the longest x1 294 us: tail(): pl.pallas_call(kernel, in_specs=[anywhere] * 6 + [vmem], out_specs=[anywh...]
    reduce_scatter x4 -> x0, waiting for transfers between devices: 131 us -> none  [the longest x1 72.8 us: on_device(): lax.psum_scatter(part_out.astype(bf16), TP, scatter_dimension=0, tiled=True)]
    psum x1 -> x0, waiting for transfers between devices: 123 us -> none  [on_device(): sums = lax.psum(jnp.concatenate(vectors), ('seq', 'chip', 'core'))]
    all_to_all x3 -> x0, blocking collectives: 107 us -> none  [the longest x2 76.4 us: reshard(): got = lax.all_to_all(mine, 'seq', 0, 0, tiled=True)]
    unnamed x17 -> x1, waiting for transfers between devices: 101 us -> 0.68 us
    convert_element_type x4 -> x0, local copies, waits for them, and re-layouts: 86.7 us -> none  [columns_back(): return every.reshape(wrows, groups * ranks * c).astype(f32)]
    all_gather x8 -> x1, waiting for transfers between devices: 76.8 us -> 0.01 us  [on_device(): cot = lax.all_gather(cot_own, TP, axis=0, tiled=True)]
    reshape x5 -> x0, local copies, waits for them, and re-layouts: 57.4 us -> none  [the longest x2 28.1 us: reshard(): w.reshape(nchip * ncore, piece, groups, nz, ncore * c)]
  transfers between devices with their start and end apart: 20 -> 5, of which waited for: 11 -> 2; matrix products, arithmetic and copies ran while one was open for 40% -> 13% of each run, Pallas kernels for 2% -> 1%
where the time goes in v2:
time: 770 us; the launch traced here: 763 us
  Pallas kernels  419 us (54%)
  matrix products  135 us (18%)
  other arithmetic  73.9 us (10%)
  local copies, waits for them, and re-layouts  52 us (7%)
  waiting for transfers between devices  28.6 us (4%)
  blocking collectives  21.4 us (3%)
  starting transfers between devices  16.9 us (2%)
  between operations  15.6 us (2%)
    pallas_call x1, Pallas kernels, tail(): pl.pallas_call(kernel, in_specs=[anywhere] * 6 + [vmem], out_specs=[anywh...  294 us
    pallas_call x1, Pallas kernels, front(): pl.pallas_call(kernel, in_specs=[anywhere] * 3, out_specs=[anywhere] * 3,...  101 us
    convert_element_type x4, other arithmetic, on_device(): g.astype(f32)  35.4 us
    all_to_all x2, waiting for transfers between devices, heads_back(): x = lax.all_to_all(x, 'chip', 0, 0, tiled=True)  27.9 us
    dot_general x1, matrix products, on_device(): hidden = jnp.dot(normed2, w_in_c, preferred_element_type=f32)  25.4 us
    unnamed x1, blocking collectives  21.4 us
    unnamed x90, local copies, waits for them, and re-layouts  19 us
    dot_general x1, matrix products, on_device(): gn2 = lax.dot_general(grad_hidden, w_in_c, nt, preferred_element_type=f32)  17 us
  transfers between devices with their start and end apart: 5, of which 2 were waited for; matrix products, arithmetic and copies ran while one was open for 13% of the time, Pallas kernels for 1%

profile of v2, /device:TPU:0, one launch (start us, length us, event | category | flops | bytes accessed | tf_op | source)
XLA Modules:
  0.0 762.7 jit_solution(7765757084417975390)
XLA Ops:
  17.2 21.4 %all-reduce = bf16[26688]{0:T(1024)(128)(2,1)S(1)} all-reduce(bf16[26688]{0:T(1024)(128)(2,1)S(1)} %dynamic-update-slice), channel_id=2, replica_groups=mesh['seq'=4,'chip'=4,'core'=2] {'seq'}, use_global_device_ids=true, to_apply=%add | all-reduce | flops 26688 | bytes 106752
  38.8 100.9 %front.1 = (bf16[4,2,192,2048]{3,2,1,0:T(8,128)(2,1)}, bf16[2048,1024]{1,0:T(8,128)(2,1)}, bf16[2048,768]{1,0:T(8,128)(2,1)}) custom-call(bf16[192,2048]{1,0:T(8,128)(2,1)} %tok_ref.1, bf16[512,8192]{1,0:T(8,128)(2,1)} %wi_ref.1, bf16[512,6144]{1,0:T(8,128)(2,1)} %wq_ref.1), custom_call_target="tpu_custom_call" | custom-call | tf_op jit(solution)/shard_map/front/pallas_call | solution.py:236
  139.8 3.8 convert_reduce_fusion
  144.4 1.8 fusion.12
  146.3 5.3 fusion.9
  151.6 5.4 convolution_add_fusion
  157.0 1.9 fusion.83
  159.0 3.0 copy.64
  162.0 3.0 copy.63
  165.3 2.6 slice.157
  167.9 2.6 slice.156
  171.7 5.8 fusion.52
  177.5 4.2 maximum_bitcast_fusion
  181.7 4.5 all-to-all-start
  187.7 25.4 %multiply_convert_fusion = (bf16[1536,1024]{1,0:T(8,128)(2,1)}, f32[1536,1024]{1,0:T(8,128)}, f32[1536,1024]{1,0:T(8,128)}) fusion(f32[1024]{0:T(1024)S(1)} %dynamic-slice_convert_fusion.1, bf16[2048,1024]{1,0:T(8,128)(2,1)} %get-tuple-element.33, bf16[1536,2048]{1,0:T(8,128)(2,1)} %bitcast.110, f32[2048]{0:T(1024)S(1)} %bitcast.166, ...), kind=kOutput, calls=%fused_computation.21 | convolution fusion | flops 6565134336 | bytes 26247168 | tf_op jit(solution)/shard_map/dot_general | solution.py:778
  215.7 12.2 %fusion.19 = f32[1536,2048]{1,0:T(8,128)} fusion(bf16[1536,1024]{1,0:T(8,128)(2,1)} %get-tuple-element.56, bf16[2048,2048]{1,0:T(8,128)(2,1)} %param.28, s32[]{:T(128)S(6)} %select_n.46), kind=kOutput, calls=%fused_computation.39 | convolution fusion | flops 6442450944 | bytes 19922948 | tf_op jit(solution)/shard_map/dot_general | solution.py:782
  228.0 3.1 fusion.84
  231.1 11.0 %attention_forward.1 = (bf16[1536,256]{1,0:T(8,128)(2,1)}, f32[1536,1]{1,0:T(8,128)}) custom-call(bf16[1536,256]{1,0:T(8,128)(2,1)} %bitcast.147, bf16[1536,256]{1,0:T(8,128)(2,1)} %bitcast.145, bf16[1536,256]{1,0:T(8,128)(2,1)} %bitcast.143, s32[1536,1]{1,0:T(8,128)} %copy.50.rp_ref, s32[1,1536]{1,0:T(1,128)} %copy-done.22), custom_call_target="tpu_custom_call" | custom-call | flops 2415919104 | bytes 3145728 | tf_op jit(solution)/shard_map/attention_forward/pallas_call | solution.py:610
  242.1 4.4 all-to-all-start.1
  246.9 11.3 %all-to-all-done.1 = bf16[4,1,384,256]{3,2,1,0:T(8,128)(2,1)} async-done(((bf16[4,1,384,256]{3,2,1,0:T(8,128)(2,1)}), bf16[4,1,384,256]{3,2,1,0:T(8,128)(2,1)}, u32[]{:S(2)}, u32[]{:S(2)}) %all-to-all-start.1) | async-done | bytes 786464 | tf_op jit(solution)/shard_map/all_to_all | solution.py:754
  258.2 9.3 %add_convert_fusion = bf16[1536,2048]{1,0:T(8,128)(2,1)} fusion(f32[1536,2048]{1,0:T(8,128)} %fusion.19, bf16[1536,256]{1,0:T(8,128)(2,1)} %bitcast.27, bf16[512,2048]{1,0:T(8,128)(2,1)S(1)} %copy-done, s32[]{:T(128)S(6)} %select_n.47), kind=kOutput, calls=%fused_computation.15 | convolution fusion | flops 1616904192 | bytes 20709380 | tf_op jit(solution)/shard_map/dot_general | solution.py:782
  267.5 5.5 convolution_convert_fusion.3
  273.0 3.5 all-to-all-start.2
  276.5 15.7 %convert_reduce_fusion.1 = (f32[1024]{0:T(1024)S(1)}, bf16[1536,1024]{1,0:T(8,128)(2,1)S(1)}) fusion(f32[1536,1024]{1,0:T(8,128)} %get-tuple-element.57, bf16[1536,2048]{1,0:T(8,128)(2,1)} %all-gather.3.cloned.1.call-done, bf16[2048,2048]{1,0:T(8,128)(2,1)} %param.28, s32[]{:T(128)S(6)} %select_n.46, f32[1536,1024]{1,0:T(8,128)} %get-tuple-element.91, ...), kind=kOutput, calls=%fused_computation.19 | convolution fusion | flops 6469188608 | bytes 26222596 | tf_op jit(solution)/shard_map/dot_general | solution.py:787
  292.3 12.6 %convolution_convert_fusion = bf16[2048,1024]{1,0:T(8,128)(2,1)} fusion(bf16[1536,1024]{1,0:T(8,128)(2,1)S(1)} %get-tuple-element.93, bf16[1536,2048]{1,0:T(8,128)(2,1)} %bitcast.111, f32[2048]{0:T(1024)S(1)} %bitcast.167, f32[2048]{0:T(1024)S(1)} %bitcast.164, f32[1536]{0:T(1024)S(1)} %add_rsqrt_fusion, f32[1536]{0:T(1024)S(1)} %broadcast_multiply_fusion), kind=kOutput, calls=%fused_computation.36 | convolution fusion | flops 6463422464 | bytes 13660160 | tf_op jit(solution)/shard_map/dot_general | solution.py:791
  305.4 5.9 convolution_convert_fusion.4.dwd_ref
  312.3 12.9 %attention_backward.1 = (f32[1536,256]{1,0:T(8,128)}, f32[1536,256]{1,0:T(8,128)}, f32[1536,256]{1,0:T(8,128)}) custom-call(bf16[1536,256]{1,0:T(8,128)(2,1)} %bitcast.148, bf16[1536,256]{1,0:T(8,128)(2,1)} %bitcast.146, bf16[1536,256]{1,0:T(8,128)(2,1)} %bitcast.144, bf16[1536,256]{1,0:T(8,128)(2,1)} %bitcast.149, f32[1536,1]{1,0:T(8,128)} %get-tuple-element.37.lse_ref, ...), custom_call_target="tpu_custom_call" | custom-call | flops 6039797760 | bytes 7864320 | tf_op jit(solution)/shard_map/attention_backward/pallas_call | solution.py:652
  325.2 2.6 slice.154
  327.8 1.7 slice.153
  329.5 5.8 fusion.60
  337.9 2.4 convert_element_type.241
  340.3 1.5 copy.60
  344.4 2.5 maximum_bitcast_fusion.1
  346.9 4.5 all-to-all-start.3
  351.4 11.2 %convolution_convert_fusion.1.dwo_ref = bf16[1024,2048]{1,0:T(8,128)(2,1)} fusion(bf16[1536,1024]{1,0:T(8,128)(2,1)} %get-tuple-element.56, bf16[1536,2048]{1,0:T(8,128)(2,1)} %all-gather.3.cloned.1.call-done), kind=kOutput, calls=%fused_computation.37 | convolution fusion | flops 6444548096 | bytes 13631488 | tf_op jit(solution)/shard_map/dot_general | solution.py:790
  362.6 16.6 %all-to-all-done.3 = bf16[4,3,384,256]{2,3,1,0:T(8,128)(2,1)} async-done(((bf16[4,3,384,256]{2,3,1,0:T(8,128)(2,1)}), bf16[4,3,384,256]{2,3,1,0:T(8,128)(2,1)}, u32[]{:S(2)}, u32[]{:S(2)}) %all-to-all-start.3) | async-done | bytes 2359328 | tf_op jit(solution)/shard_map/all_to_all | solution.py:754
  379.1 3.6 copy.61
  383.2 8.2 %fusion.86 = f32[1536,2048]{1,0:T(8,128)} fusion(bf16[1536,768]{0,1:T(8,128)(2,1)S(1)} %bitcast.133, bf16[2048,768]{1,0:T(8,128)(2,1)S(1)} %copy-done.26), kind=kOutput, calls=%fused_computation.150 | convolution fusion | flops 4831838208 | bytes 18087936 | tf_op jit(solution)/shard_map/dot_general | solution.py:802
  391.4 6.5 convolution_convert_fusion.2
  397.9 17.0 %fusion.79 = (f32[2048]{0:T(1024)S(1)}, f32[2048]{0:T(1024)S(1)}, bf16[1536,2048]{1,0:T(8,128)(2,1)}, f32[2048]{0:T(1024)S(1)}, f32[2048]{0:T(1024)S(1)}) fusion(f32[1536]{0:T(1024)S(1)} %add_rsqrt_fusion, f32[1536]{0:T(1024)S(1)} %broadcast_multiply_fusion, bf16[1536,2048]{1,0:T(8,128)(2,1)} %bitcast.112, f32[2048]{0:T(1024)S(1)} %bitcast.165, ...), kind=kOutput, calls=%fused_computation.144 | convolution fusion | flops 6483337216 | bytes 32567296 | tf_op jit(solution)/shard_map/dot_general | solution.py:792
  414.9 2.0 convert_reduce_fusion.2
  417.8 294.5 %tail.1 = (bf16[2048,2048]{1,0:T(8,128)(2,1)}, bf16[512,2048]{1,0:T(8,128)(2,1)}, bf16[512,8192]{1,0:T(8,128)(2,1)}, bf16[512,6144]{1,0:T(8,128)(2,1)}, f32[192,...) custom-call(bf16[1024,2048]{1,0:T(8,128)(2,1)} %convolution_convert_fusion.1.dwo_ref, ...), custom_call_target="tpu_custom_call" | custom-call | tf_op jit(solution)/shard_map/tail/pallas_call | solution.py:539
  712.3 11.7 %convert_element_type.256 = f32[512,8192]{1,0:T(8,128)} convert(bf16[512,8192]{1,0:T(8,128)(2,1)} %get-tuple-element.46) | non-fusion elementwise | flops 4194304 | bytes 25165824 | tf_op jit(solution)/shard_map/convert_element_type | solution.py:847
  724.0 11.7 %convert_element_type.257 = f32[2048,2048]{1,0:T(8,128)} convert(bf16[2048,2048]{1,0:T(8,128)(2,1)} %get-tuple-element.47) | non-fusion elementwise | flops 4194304 | bytes 25165824 | tf_op jit(solution)/shard_map/convert_element_type | solution.py:847
  735.7 9.4 %convert_element_type.254 = f32[512,6144]{1,0:T(8,128)} convert(bf16[512,6144]{1,0:T(8,128)(2,1)} %get-tuple-element.44) | non-fusion elementwise | flops 3145728 | bytes 18874368 | tf_op jit(solution)/shard_map/convert_element_type | solution.py:847
  745.1 2.7 convert_element_type.255
  747.7 2.0 fusion.85
  752.9 2.2 fusion.33
  (141 shorter events, 27.7 us)
Async XLA Ops:
  7.2 251.0 %copy-start = (bf16[512,2048]{1,0:T(8,128)(2,1)S(1)}, bf16[512,2048]{1,0:T(8,128)(2,1)}, u32[]{:S(2)}) copy-start(bf16[512,2048]{1,0:T(8,128)(2,1)} %param.24) | copy-start | bytes 6291460
  38.8 101.0 %copy-start.14 = (bf16[4,6672]{1,0:T(4,128)(2,1)}, bf16[4,6672]{1,0:T(4,128)(2,1)S(1)}, u32[]{:S(2)}) copy-start(bf16[4,6672]{1,0:T(4,128)(2,1)S(1)} %reshape.423) | copy-start | bytes 160132
  139.8 4.6 copy-start.2
  139.8 6.4 slice-start.2
  146.2 5.4 copy-start.17
  146.3 5.3 copy-start.25
  151.6 5.4 copy-start.6
  177.5 9.4 %copy-start.15 = (bf16[4,6672]{1,0:T(4,128)(2,1)S(1)}, bf16[4,6672]{1,0:T(4,128)(2,1)}, u32[]{:S(2)}) copy-start(bf16[4,6672]{1,0:T(4,128)(2,1)} %copy-done.14) | copy-start | bytes 160132
  177.5 9.5 %copy-start.4 = (bf16[192,2048]{1,0:T(8,128)(2,1)S(1)}, bf16[192,2048]{1,0:T(8,128)(2,1)}, u32[]{:S(2)}) copy-start(bf16[192,2048]{1,0:T(8,128)(2,1)} %param.17) | copy-start | bytes 2359300
  181.7 46.3 %all-to-all-start = ((bf16[4,3,384,256]{3,2,1,0:T(8,128)(2,1)}), bf16[4,3,384,256]{3,2,1,0:T(8,128)(2,1)}, u32[]{:S(2)}, u32[]{:S(2)}) async-start(bf16[4,3,384,256]{3,2,1,0:T(8,128)(2,1)} %maximum_bitcast_fusion), calls=%async_computation | async-start | bytes 4718592 | tf_op jit(solution)/shard_map/all_to_all | solution.py:748
  186.2 81.3 %all-gather.3.cloned.1.call-start = ((), (), s32[]{:S(2)}) async-start(), calls=%async_computation.4 | async-start | bytes 7077888 | tf_op jit(solution)/shard_map/all_gather | solution.py:719
  187.7 27.8 %copy-start.3 = (bf16[192,2048]{1,0:T(8,128)(2,1)S(1)}, bf16[192,2048]{1,0:T(8,128)(2,1)}, u32[]{:S(2)}) copy-start(bf16[192,2048]{1,0:T(8,128)(2,1)} %tok_ref.1) | copy-start | bytes 2359300
  213.2 14.8 %copy-start.22 = (s32[1,1536]{1,0:T(1,128)}, s32[1,1536]{1,0:T(1,128)S(1)}, u32[]{:S(2)}) copy-start(s32[1,1536]{1,0:T(1,128)S(1)} %get-tuple-element.55.cp_ref) | copy-start | bytes 18436
  242.1 16.1 %all-to-all-start.1 = ((bf16[4,1,384,256]{3,2,1,0:T(8,128)(2,1)}), bf16[4,1,384,256]{3,2,1,0:T(8,128)(2,1)}, u32[]{:S(2)}, u32[]{:S(2)}) async-start(bf16[4,1,384,256]{3,2,1,0:T(8,128)(2,1)} %bitcast.151), calls=%async_computation.1 | async-start | bytes 1572864 | tf_op jit(solution)/shard_map/all_to_all | solution.py:754
  273.0 38.3 %all-to-all-start.2 = ((bf16[4,1,384,256]{3,2,1,0:T(8,128)(2,1)}), bf16[4,1,384,256]{3,2,1,0:T(8,128)(2,1)S(1)}, u32[]{:S(2)}, u32[]{:S(2)}) async-start(bf16[4,1,384,256]{3,2,1,0:T(8,128)(2,1)} %bitcast.150), calls=%async_computation.2 | async-start | bytes 1572864 | tf_op jit(solution)/shard_map/all_to_all | solution.py:748
  292.3 12.6 %copy-start.27 = (bf16[1536,1024]{1,0:T(8,128)(2,1)}, bf16[1536,1024]{1,0:T(8,128)(2,1)S(1)}, u32[]{:S(2)}) copy-start(bf16[1536,1024]{1,0:T(8,128)(2,1)S(1)} %get-tuple-element.93) | copy-start | bytes 9437188
  311.4 0.9 copy-start.10
  337.9 6.5 copy-start.11
  337.9 6.5 copy-start.12
  337.9 6.5 copy-start.13
  346.9 32.2 %all-to-all-start.3 = ((bf16[4,3,384,256]{2,3,1,0:T(8,128)(2,1)}), bf16[4,3,384,256]{2,3,1,0:T(8,128)(2,1)}, u32[]{:S(2)}, u32[]{:S(2)}) async-start(bf16[4,3,384,256]{2,3,1,0:T(8,128)(2,1)} %maximum_bitcast_fusion.1), calls=%async_computation.3 | async-start | bytes 4718592 | tf_op jit(solution)/shard_map/all_to_all | solution.py:754
  379.1 4.0 copy-start.26
  379.1 12.2 %slice-start = ((s8[6291456]{0:T(1024)(128)(4,1)}), s8[4194304]{0:T(1024)(128)(4,1)S(1)}, s32[]{:S(2)}) async-start(s8[6291456]{0:T(1024)(128)(4,1)} %bitcast.120), calls=%async_computation.5 | async-start | bytes 8388608
  383.2 8.2 %slice-start.1 = ((s8[6291456]{0:T(1024)(128)(4,1)}), s8[2097152]{0:T(1024)(128)(4,1)S(1)}, s32[]{:S(2)}) async-start(s8[6291456]{0:T(1024)(128)(4,1)} %bitcast.120), calls=%async_computation.6 | async-start | bytes 4194304
  391.4 6.5 copy-start.18
  391.4 6.5 copy-start.24
  397.9 19.2 %copy-start.21 = (f32[2048]{0:T(1024)S(1)}, f32[2048]{0:T(1024)}, u32[]{:S(2)}) copy-start(f32[2048]{0:T(1024)} %convert_reduce_fusion.4) | copy-start | bytes 24580
  417.1 0.6 copy-start.16
  735.7 9.4 %copy-start.8 = (bf16[512,2048]{1,0:T(8,128)(2,1)S(1)}, bf16[512,2048]{1,0:T(8,128)(2,1)}, u32[]{:S(2)}) copy-start(bf16[512,2048]{1,0:T(8,128)(2,1)} %get-tuple-element.45) | copy-start | bytes 6291460
  745.0 7.4 copy-start.7
  745.0 7.8 %copy-start.5 = (bf16[192,2048]{1,0:T(8,128)(2,1)S(1)}, bf16[192,2048]{1,0:T(8,128)(2,1)}, u32[]{:S(2)}) copy-start(bf16[192,2048]{1,0:T(8,128)(2,1)} %param.17) | copy-start | bytes 2359300
  745.0 7.8 %copy-start.9 = (f32[192,2048]{1,0:T(8,128)S(1)}, f32[192,2048]{1,0:T(8,128)}, u32[]{:S(2)}) copy-start(f32[192,2048]{1,0:T(8,128)} %get-tuple-element.41) | copy-start | bytes 4718596
  745.0 7.8 %copy-start.19 = (f32[1,4,4,128]{3,1,2,0:T(4,128)S(1)}, f32[1,4,4,128]{3,1,2,0:T(4,128)}, u32[]{:S(2)}) copy-start(f32[1,4,4,128]{3,1,2,0:T(4,128)} %copy.73) | copy-start | bytes 24580
  745.0 7.8 %copy-start.20 = (f32[1,4,4,128]{3,1,2,0:T(4,128)S(1)}, f32[1,4,4,128]{3,1,2,0:T(4,128)}, u32[]{:S(2)}) copy-start(f32[1,4,4,128]{3,1,2,0:T(4,128)} %copy.74) | copy-start | bytes 24580
  745.1 10.6 %copy-start.1 = (bf16[512,2048]{1,0:T(8,128)(2,1)S(1)}, bf16[512,2048]{1,0:T(8,128)(2,1)}, u32[]{:S(2)}) copy-start(bf16[512,2048]{1,0:T(8,128)(2,1)} %param.24) | copy-start | bytes 6291460
  749.7 5.9 copy-start.23
Sparse Core Ops, SparseCore 0:
  188.7 68.5 all-gather.2

commit v3 on v2

v3 whole, which is shorter than its diff:
```python
import functools
import math

import jax
import jax.numpy as jnp
import numpy as np
from jax import lax
from jax.experimental import pallas as pl
from jax.experimental.pallas import tpu as pltpu
from jax.sharding import Mesh, PartitionSpec as P

HD = 256
ROT = 64
BLOCK = 96
EPSILON = 1e-05
ROT_BASE = 10000.0
SCALE = HD ** (-0.5)
f32 = jnp.float32
bf16 = jnp.bfloat16
TP = ("seq", "core")
MESH = pl.DeviceIdType.MESH
NT = (((1,), (1,)), ((), ()))
TN = (((0,), (0,)), ((), ()))
BIG = pltpu.CompilerParams(vmem_limit_bytes=56 * 2**20)


def remote(src, dst, send, recv, target):
    return pltpu.make_async_remote_copy(
        src_ref=src, dst_ref=dst, send_sem=send, recv_sem=recv, device_id=target,
        device_id_type=MESH,
    )


def greet(targets):
    barrier = pltpu.get_barrier_semaphore()
    for target in targets:
        pl.semaphore_signal(barrier, inc=1, device_id=target, device_id_type=MESH)
    pl.semaphore_wait(barrier, len(targets))


def front(nz, nchip, ncore, tokens, w_in, w_qkv, small):
    own, width = tokens.shape
    wrows, ff = w_in.shape
    heads3 = w_qkv.shape[1]
    nctx = nchip * ncore
    piece = wrows // nctx
    zi, zq = ff // nz, heads3 // 3 // nz
    ci, cq = zi // ncore, zq // ncore

    def kernel(
        tok_ref, wi_ref, wq_ref, sm_ref, tok_out, wi_out, wq_out, sm_out, buf_i, buf_q,
        up_s, up_r, dn_s, dn_r, sib_s, sib_r, zi_s, zi_r, zq_s, zq_r, pi_s, pi_r, pq_s, pq_r, loc, sm_s, sm_r,
    ):
        z = lax.axis_index("seq")
        chip = lax.axis_index("chip")
        core = lax.axis_index("core")
        share = chip * ncore + core
        sibling = {"core": 1 - core}

        def z_at(d):
            return lax.rem(z + d, nz)

        def plane_at(d):
            other = lax.rem(share + d, nctx)
            return other // ncore, lax.rem(other, ncore)

        greet(
            [{"seq": z_at(d)} for d in range(1, nz)]
            + [{"chip": plane_at(d)[0], "core": plane_at(d)[1]} for d in range(1, nctx)]
        )

        rows = pl.ds(share * piece, piece)
        def hop(to):
            to = jnp.clip(to, 0, nz - 1)
            copies = [
                remote(
                    wi_ref.at[rows, pl.ds(to * zi, zi)], buf_i.at[z], zi_s.at[to], zi_r.at[z],
                    {"seq": to},
                )
            ]
            for g in range(3):
                copies.append(
                    remote(
                        wq_ref.at[rows, pl.ds(g * zq * nz + to * zq, zq)], buf_q.at[z, g],
                        zq_s.at[to, g], zq_r.at[z, g], {"seq": to},
                    )
                )
            return copies

        def around(body):
            for distance in range(1, nz):
                for other in (z + distance, z - distance):
                    @pl.when(jnp.logical_and(other >= 0, other < nz))
                    def _():
                        body(jnp.clip(other, 0, nz - 1))

        def up(s):
            shard = z - s
            src = tok_ref if s == 0 else tok_out.at[jnp.maximum(shard, 0), core]
            return remote(
                src, tok_out.at[jnp.maximum(shard, 0), core], up_s.at[s], up_r.at[s],
                {"seq": jnp.minimum(z + 1, nz - 1)},
            )

        def down(s):
            shard = z + s
            src = tok_ref if s == 0 else tok_out.at[jnp.minimum(shard, nz - 1), core]
            return remote(
                src, tok_out.at[jnp.minimum(shard, nz - 1), core], dn_s.at[s], dn_r.at[s],
                {"seq": jnp.maximum(z - 1, 0)},
            )

        def side(shard, own_rows=False):
            src = tok_ref if own_rows else tok_out.at[shard, core]
            return remote(src, tok_out.at[shard, core], sib_s.at[shard], sib_r.at[shard], sibling)

        smalls = [
            remote(sm_ref, sm_out.at[z], sm_s.at[d], sm_r.at[z], {"seq": z_at(d)})
            for d in range(1, nz)
        ]
        for copy in smalls:
            copy.start()

        def send_hop(to):
            for copy in hop(to):
                copy.start()

        around(send_hop)

        @pl.when(z + 1 < nz)
        def _():
            up(0).start()

        @pl.when(z > 0)
        def _():
            down(0).start()

        side(z, True).start()
        locals_ = [
            pltpu.make_async_copy(tok_ref, tok_out.at[z, core], loc.at[0]),
            pltpu.make_async_copy(wi_ref.at[rows, pl.ds(z * zi, zi)], buf_i.at[z], loc.at[1]),
            pltpu.make_async_copy(sm_ref, sm_out.at[z], sm_s.at[0]),
        ] + [
            pltpu.make_async_copy(
                wq_ref.at[rows, pl.ds(g * zq * nz + z * zq, zq)], buf_q.at[z, g], loc.at[2 + g]
            )
            for g in range(3)
        ]
        for copy in locals_:
            copy.start()

        def spread(source, d):
            to_chip, to_core = plane_at(d)
            target_rows = pl.ds(source * wrows + share * piece, piece)
            pairs = [
                (
                    buf_i.at[source, :, pl.ds(to_core * ci, ci)], wi_out.at[target_rows, :],
                    pi_s.at[source, d], pi_r.at[source, share],
                )
            ] + [
                (
                    buf_q.at[source, g, :, pl.ds(to_core * cq, cq)],
                    wq_out.at[target_rows, pl.ds(g * cq, cq)],
                    pq_s.at[source, d, g], pq_r.at[source, share, g],
                )
                for g in range(3)
            ]
            if d == 0:
                return [pltpu.make_async_copy(a, b, c) for a, b, c, r in pairs]
            return [remote(a, b, c, r, {"chip": to_chip, "core": to_core}) for a, b, c, r in pairs]

        def hop_arrival(source):
            remote(buf_i.at[source], buf_i.at[source], zi_s.at[0], zi_r.at[source], sibling).wait_recv()
            for g in range(3):
                remote(
                    buf_q.at[source, g], buf_q.at[source, g], zq_s.at[0, 0], zq_r.at[source, g],
                    sibling,
                ).wait_recv()

        for copy in locals_[1:]:
            copy.wait()
        for d in range(nctx):
            for copy in spread(z, d):
                copy.start()
        def hand_on(source):
            hop_arrival(source)
            for d in range(nctx):
                for copy in spread(source, d):
                    copy.start()

        around(hand_on)

        for s in range(nz - 1):
            from_below = z - 1 - s
            from_above = z + 1 + s

            @pl.when(from_below >= 0)
            def _():
                shard = jnp.maximum(from_below, 0)
                remote(tok_ref, tok_out.at[shard, core], up_s.at[s], up_r.at[s], sibling).wait_recv()
                if s + 1 < nz - 1:
                    @pl.when(z + 1 < nz)
                    def _():
                        up(s + 1).start()
                side(shard).start()

            @pl.when(from_above < nz)
            def _():
                shard = jnp.minimum(from_above, nz - 1)
                remote(tok_ref, tok_out.at[shard, core], dn_s.at[s], dn_r.at[s], sibling).wait_recv()
                if s + 1 < nz - 1:
                    @pl.when(z > 0)
                    def _():
                        down(s + 1).start()
                side(shard).start()

        locals_[0].wait()
        for shard in range(nz):
            remote(tok_ref, tok_out.at[shard, 1 - core], sib_s.at[shard], sib_r.at[shard], sibling).wait()
        for s in range(nz - 1):
            @pl.when(jnp.logical_and(z + 1 < nz, z - s >= 0))
            def _():
                up(s).wait_send()

            @pl.when(jnp.logical_and(z > 0, z + s < nz))
            def _():
                down(s).wait_send()
        for copy in smalls:
            copy.wait_send()

        def hop_left(to):
            for copy in hop(to):
                copy.wait_send()

        around(hop_left)
        for d in range(1, nz):
            other = z_at(d)
            remote(sm_ref, sm_out.at[other], sm_s.at[d], sm_r.at[other], sibling).wait_recv()
        for source in range(nz):
            for d in range(nctx):
                if d == 0:
                    for copy in spread(source, d):
                        copy.wait()
                    continue
                for copy in spread(source, d):
                    copy.wait_send()
                other = lax.rem(share + d, nctx)
                rows_there = pl.ds(source * wrows + other * piece, piece)
                remote(
                    wi_out.at[rows_there, :], wi_out.at[rows_there, :], pi_s.at[source, d],
                    pi_r.at[source, other], sibling,
                ).wait_recv()
                for g in range(3):
                    cols = pl.ds(g * cq, cq)
                    remote(
                        wq_out.at[rows_there, cols], wq_out.at[rows_there, cols],
                        pq_s.at[source, d, g], pq_r.at[source, other, g], sibling,
                    ).wait_recv()

    dma = pltpu.SemaphoreType.DMA
    anywhere = pl.BlockSpec(memory_space=pl.ANY)
    return pl.pallas_call(
        kernel,
        in_specs=[anywhere] * 4,
        out_specs=[anywhere] * 4,
        out_shape=[
            jax.ShapeDtypeStruct((nz, ncore, own, width), bf16),
            jax.ShapeDtypeStruct((nz * wrows, ci), bf16),
            jax.ShapeDtypeStruct((nz * wrows, 3 * cq), bf16),
            jax.ShapeDtypeStruct((nz,) + small.shape, bf16),
        ],
        scratch_shapes=[
            pltpu.VMEM((nz, piece, zi), bf16),
            pltpu.VMEM((nz, 3, piece, zq), bf16),
            dma((nz,)), dma((nz,)), dma((nz,)), dma((nz,)),
            dma((nz,)), dma((nz,)),
            dma((nz,)), dma((nz,)), dma((nz, 3)), dma((nz, 3)),
            dma((nz, nctx)), dma((nz, nctx)), dma((nz, nctx, 3)), dma((nz, nctx, 3)),
            dma((5,)), dma((nz,)), dma((nz,)),
        ],
        compiler_params=pltpu.CompilerParams(collective_id=1, has_side_effects=True),
        name="front",
    )(tokens, w_in, w_qkv, small)


def turn_table(length):
    half = ROT // 2
    power = -(np.arange(half, dtype=np.float32) * np.float32(2.0)) / np.float32(ROT)
    angles = np.arange(length, dtype=np.float32)[:, None] * np.power(np.float32(ROT_BASE), power)
    table = np.zeros((3, length, 128), np.float32)
    table[0] = 1.0
    table[0, :, :half] = table[0, :, half:ROT] = np.cos(angles)
    table[1, :, :half] = -np.sin(angles)
    table[2, :, half:ROT] = np.sin(angles)
    return table


def turned(u, cosine, minus, plus):
    half = ROT // 2
    return u * cosine + pltpu.roll(u, 128 - half, 1) * minus + pltpu.roll(u, half, 1) * plus


def stats(x):
    center = x - jnp.mean(x, axis=-1, keepdims=True)
    inv = lax.rsqrt(jnp.mean(center * center, axis=-1, keepdims=True) + EPSILON)
    return center * inv, inv


def cost(flops, nbytes, trans=0):
    return pl.CostEstimate(flops=int(flops), bytes_accessed=int(nbytes), transcendentals=int(trans))


def projections(nz, ids, place, tok, w, bias, gain, offset, table):
    rows, width = tok.shape
    step = rows // nz
    blocks = step // BLOCK
    cols = w.shape[1]
    hc = cols // 3

    def kernel(ids_ref, place_ref, tok_ref, w_ref, b_ref, g_ref, o_ref, t_ref, n_ref, out_ref):
        xhat, inv = stats(tok_ref[...].astype(f32))
        normed = (xhat * g_ref[...] + o_ref[...]).astype(bf16)
        n_ref[...] = normed
        project = jnp.dot(normed, w_ref[...], preferred_element_type=f32) + b_ref[...]
        out_ref[...] = project.astype(bf16)
        first = place_ref[0] == 1

        @pl.when(first)
        def _():
            for b in range(blocks):
                at = pl.ds(pl.multiple_of(ids_ref[pl.program_id(0) * blocks + b] * BLOCK, BLOCK), BLOCK)
                c, m, p = t_ref[0, at, :], t_ref[1, at, :], t_ref[2, at, :]
                for g in range(2):
                    u = project[b * BLOCK : (b + 1) * BLOCK, g * hc : g * hc + 128]
                    out_ref[b * BLOCK : (b + 1) * BLOCK, g * hc : g * hc + 128] = turned(
                        u, c, m, p
                    ).astype(bf16)

    whole = lambda shape: pl.BlockSpec(shape, lambda i, *_: (0,) * len(shape))
    return pl.pallas_call(
        kernel,
        grid_spec=pltpu.PrefetchScalarGridSpec(
            num_scalar_prefetch=2,
            grid=(nz,),
            in_specs=[
                pl.BlockSpec((step, width), lambda i, *_: (i, 0)),
                whole((width, cols)),
                whole((1, cols)),
                whole((1, width)),
                whole((1, width)),
                whole(table.shape),
            ],
            out_specs=[
                pl.BlockSpec((step, width), lambda i, *_: (i, 0)),
                pl.BlockSpec((step, cols), lambda i, *_: (i, 0)),
            ],
        ),
        out_shape=[
            jax.ShapeDtypeStruct((rows, width), bf16),
            jax.ShapeDtypeStruct((rows, cols), bf16),
        ],
        compiler_params=BIG,
        cost_estimate=cost(2 * rows * width * cols, 4 * rows * width + 2 * width * cols),
        name="projections",
    )(ids, place, tok, w, bias, gain, offset, table)


def feed_forward(nz, tok, w, bias, gain, offset):
    rows, width = tok.shape
    step = rows // nz
    cols = w.shape[1]

    def kernel(tok_ref, w_ref, b_ref, g_ref, o_ref, n_ref, a_ref, d_ref):
        xhat, inv = stats(tok_ref[...].astype(f32))
        normed = (xhat * g_ref[...] + o_ref[...]).astype(bf16)
        n_ref[...] = normed
        v = jnp.dot(normed, w_ref[...], preferred_element_type=f32) + b_ref[...]
        gate = 0.5 * (1.0 + lax.erf(v * (0.5**0.5)))
        a_ref[...] = (v * gate).astype(bf16)
        bell = jnp.exp(v * v * -0.5) * ((2.0 * math.pi) ** -0.5)
        d_ref[...] = (gate + v * bell).astype(bf16)

    whole = lambda shape: pl.BlockSpec(shape, lambda i: (0, 0))
    part = lambda n: pl.BlockSpec((step, n), lambda i: (i, 0))
    return pl.pallas_call(
        kernel,
        grid=(nz,),
        in_specs=[part(width), whole((width, cols)), whole((1, cols)), whole((1, width)), whole((1, width))],
        out_specs=[part(width), part(cols), part(cols)],
        out_shape=[
            jax.ShapeDtypeStruct((rows, width), bf16),
            jax.ShapeDtypeStruct((rows, cols), bf16),
            jax.ShapeDtypeStruct((rows, cols), bf16),
        ],
        compiler_params=BIG,
        cost_estimate=cost(2 * rows * width * cols, 4 * rows * width + 2 * width * cols, 2 * rows * cols),
        name="feed_forward",
    )(tok, w, bias, gain, offset)


def layer_out(nz, core, mixed, w_dense, active, w_out):
    rows, hc = mixed.shape
    width = w_out.shape[1]
    step = rows // nz
    units = active.shape[1]

    def kernel(core_ref, m_ref, wd_ref, a_ref, wo_ref, out_ref):
        out_ref[...] = (
            jnp.dot(m_ref[...], wd_ref[...], preferred_element_type=f32)
            + jnp.dot(a_ref[...], wo_ref[...], preferred_element_type=f32)
        ).astype(bf16)

    part = lambda n: pl.BlockSpec((step, n), lambda i, c: (i, 0))
    held = lambda n: pl.BlockSpec((n, width), lambda i, c: (c[0], 0))
    return pl.pallas_call(
        kernel,
        grid_spec=pltpu.PrefetchScalarGridSpec(
            num_scalar_prefetch=1,
            grid=(nz,),
            in_specs=[part(hc), held(hc), part(units), held(units)],
            out_specs=part(width),
        ),
        out_shape=jax.ShapeDtypeStruct((rows, width), bf16),
        compiler_params=BIG,
        cost_estimate=cost(2 * rows * width * (hc + units), 4 * rows * width + 2 * width * units),
        name="layer_out",
    )(core, mixed, w_dense, active, w_out)


def grad_of_mixed(nz, core, cot, w_dense, hc):
    rows, width = cot.shape
    step = rows // nz

    def kernel(core_ref, c_ref, w_ref, out_ref):
        out_ref[...] = lax.dot_general(
            c_ref[...], w_ref[...], NT, preferred_element_type=f32
        ).astype(bf16)

    return pl.pallas_call(
        kernel,
        grid_spec=pltpu.PrefetchScalarGridSpec(
            num_scalar_prefetch=1,
            grid=(nz,),
            in_specs=[
                pl.BlockSpec((step, width), lambda i, c: (i, 0)),
                pl.BlockSpec((hc, width), lambda i, c: (c[0], 0)),
            ],
            out_specs=pl.BlockSpec((step, hc), lambda i, c: (i, 0)),
        ),
        out_shape=jax.ShapeDtypeStruct((rows, hc), bf16),
        compiler_params=BIG,
        cost_estimate=cost(2 * rows * width * hc, 2 * rows * width),
        name="grad_of_mixed",
    )(core, cot, w_dense)


def grad_of_hidden(nz, core, cot, w_out, slope):
    rows, width = cot.shape
    step = rows // nz
    units = slope.shape[1]

    def kernel(core_ref, c_ref, w_ref, d_ref, out_ref, sum_ref):
        g = lax.dot_general(c_ref[...], w_ref[...], NT, preferred_element_type=f32)
        g = (g * d_ref[...].astype(f32)).astype(bf16)
        out_ref[...] = g

        @pl.when(pl.program_id(0) == 0)
        def _():
            sum_ref[...] = jnp.zeros_like(sum_ref)

        sum_ref[...] += jnp.sum(g.astype(f32), axis=0, keepdims=True)

    return pl.pallas_call(
        kernel,
        grid_spec=pltpu.PrefetchScalarGridSpec(
            num_scalar_prefetch=1,
            grid=(nz,),
            in_specs=[
                pl.BlockSpec((step, width), lambda i, c: (i, 0)),
                pl.BlockSpec((units, width), lambda i, c: (c[0], 0)),
                pl.BlockSpec((step, units), lambda i, c: (i, 0)),
            ],
            out_specs=[
                pl.BlockSpec((step, units), lambda i, c: (i, 0)),
                pl.BlockSpec((1, units), lambda i, c: (0, 0)),
            ],
        ),
        out_shape=[
            jax.ShapeDtypeStruct((rows, units), bf16),
            jax.ShapeDtypeStruct((1, units), f32),
        ],
        compiler_params=BIG,
        cost_estimate=cost(2 * rows * width * units, 2 * rows * width + 2 * width * units),
        name="grad_of_hidden",
    )(core, cot, w_out, slope)


def norm_back(nz, grad, w, tok, gain, other, sums):
    rows, width = tok.shape
    step = rows // nz
    cols = grad.shape[1]

    def kernel(*refs):
        g_ref, w_ref, t_ref, gain_ref = refs[:4]
        at = 4
        if other is not None:
            other_ref = refs[at]
            at += 1
        e_ref, s_ref = refs[at : at + 2]
        gn = lax.dot_general(g_ref[...], w_ref[...], NT, preferred_element_type=f32)
        xhat, inv = stats(t_ref[...].astype(f32))
        e = gn * gain_ref[...]
        if other is not None:
            e = e + other_ref[...].astype(f32)
        e_ref[...] = e.astype(bf16)

        @pl.when(pl.program_id(0) == 0)
        def _():
            s_ref[...] = jnp.zeros_like(s_ref)
            if sums:
                refs[at + 2][...] = jnp.zeros_like(refs[at + 2])

        s_ref[0:1, :] += jnp.sum(gn * xhat, axis=0, keepdims=True)
        s_ref[1:2, :] += jnp.sum(gn, axis=0, keepdims=True)
        if sums:
            refs[at + 2][...] += jnp.sum(g_ref[...].astype(f32), axis=0, keepdims=True)

    part = lambda n: pl.BlockSpec((step, n), lambda i: (i, 0))
    whole = lambda shape: pl.BlockSpec(shape, lambda i: (0, 0))
    ins = [grad, w, tok, gain] + ([] if other is None else [other])
    return pl.pallas_call(
        kernel,
        grid=(nz,),
        in_specs=[part(cols), whole((width, cols)), part(width), whole((1, width))]
        + ([] if other is None else [part(width)]),
        out_specs=[part(width), whole((2, width))] + ([whole((1, cols))] if sums else []),
        out_shape=[
            jax.ShapeDtypeStruct((rows, width), bf16),
            jax.ShapeDtypeStruct((2, width), f32),
        ]
        + ([jax.ShapeDtypeStruct((1, cols), f32)] if sums else []),
        compiler_params=BIG,
        cost_estimate=cost(2 * rows * width * cols, 6 * rows * width + 2 * width * cols),
        name="norm_back",
    )(*ins)


def attention_forward(ids, order, qkv, tile):
    rows = qkv.shape[0]
    blocks = rows // BLOCK

    def kernel(ids_ref, order_ref, x_ref, o_ref, lse_ref, q_ref, k_ref, v_ref, s_ref):
        for b in range(blocks):
            at = pl.ds(pl.multiple_of(order_ref[b] * BLOCK, BLOCK), BLOCK)
            here = slice(b * BLOCK, (b + 1) * BLOCK)
            for i, ref in enumerate((q_ref, k_ref, v_ref)):
                ref[here, :] = x_ref[at, i * HD : (i + 1) * HD]
        for t in range(rows // tile):
            mine = slice(t * tile, (t + 1) * tile)
            n = (t + 1) * tile
            s = lax.dot_general(q_ref[mine, :], k_ref[:n, :], NT, preferred_element_type=f32)
            s = s * SCALE
            seen = t * tile + lax.broadcasted_iota(jnp.int32, (tile, n), 0) >= (
                lax.broadcasted_iota(jnp.int32, (tile, n), 1)
            )
            s = jnp.where(seen, s, -1e30)
            top = jnp.max(s, axis=-1, keepdims=True)
            e = jnp.exp(s - top)
            total = jnp.sum(e, axis=-1, keepdims=True)
            p = (e * (1.0 / total)).astype(bf16)
            s_ref[mine, :] = jnp.dot(p, v_ref[:n, :], preferred_element_type=f32).astype(bf16)
            lse_ref[mine, :] = top + jnp.log(total)
        for b in range(blocks):
            at = pl.ds(pl.multiple_of(ids_ref[b] * BLOCK, BLOCK), BLOCK)
            o_ref[b * BLOCK : (b + 1) * BLOCK, :] = s_ref[at, :]

    smem = pl.BlockSpec(memory_space=pltpu.SMEM)
    vmem = pl.BlockSpec(memory_space=pltpu.VMEM)
    return pl.pallas_call(
        kernel,
        in_specs=[smem, smem, vmem],
        out_specs=[vmem, vmem],
        out_shape=[
            jax.ShapeDtypeStruct((rows, HD), bf16),
            jax.ShapeDtypeStruct((rows, 1), f32),
        ],
        scratch_shapes=[pltpu.VMEM((rows, HD), bf16)] * 4,
        compiler_params=BIG,
        cost_estimate=cost(2.3 * rows * rows * HD, 8 * rows * HD, rows * rows / 2),
        name="attention_forward",
    )(ids, order, qkv)


def attention_backward(ids, order, qkv, grad, lse, table, tile):
    rows = qkv.shape[0]
    blocks = rows // BLOCK

    def kernel(ids_ref, order_ref, x_ref, g_ref, lse_ref, t_ref, out_ref, q_ref, k_ref, v_ref, m_ref,
               r_ref, dk_ref, dv_ref):
        for b in range(blocks):
            at = pl.ds(pl.multiple_of(order_ref[b] * BLOCK, BLOCK), BLOCK)
            here = slice(b * BLOCK, (b + 1) * BLOCK)
            for i, ref in enumerate((q_ref, k_ref, v_ref)):
                ref[here, :] = x_ref[at, i * HD : (i + 1) * HD]
            m_ref[here, :] = g_ref[at, :]
        for t in reversed(range(rows // tile)):
            mine = slice(t * tile, (t + 1) * tile)
            n = (t + 1) * tile
            q, g = q_ref[mine, :], m_ref[mine, :]
            s = lax.dot_general(q, k_ref[:n, :], NT, preferred_element_type=f32) * SCALE
            seen = t * tile + lax.broadcasted_iota(jnp.int32, (tile, n), 0) >= (
                lax.broadcasted_iota(jnp.int32, (tile, n), 1)
            )
            p = jnp.where(seen, jnp.exp(s - lse_ref[mine, :]), 0.0)
            dp = lax.dot_general(g, v_ref[:n, :], NT, preferred_element_type=f32)
            shift = jnp.sum(p * dp, axis=-1, keepdims=True)
            ds = (p * (dp - shift)).astype(bf16)
            low = p.astype(bf16)
            dq = jnp.dot(ds, k_ref[:n, :], preferred_element_type=f32) * SCALE
            r_ref[mine, :128] = turned(
                dq[:, :128], t_ref[0, mine, :], -t_ref[1, mine, :], -t_ref[2, mine, :]
            ).astype(bf16)
            r_ref[mine, 128:HD] = dq[:, 128:].astype(bf16)
            dk = lax.dot_general(ds, q, TN, preferred_element_type=f32) * SCALE
            dv = lax.dot_general(low, g, TN, preferred_element_type=f32)
            if n == rows:
                dk_ref[...] = dk
                dv_ref[...] = dv
            else:
                dk_ref[:n, :] += dk
                dv_ref[:n, :] += dv
        r_ref[:, HD : HD + 128] = turned(
            dk_ref[:, :128], t_ref[0], -t_ref[1], -t_ref[2]
        ).astype(bf16)
        r_ref[:, HD + 128 : 2 * HD] = dk_ref[:, 128:].astype(bf16)
        r_ref[:, 2 * HD :] = dv_ref[...].astype(bf16)
        for b in range(blocks):
            at = pl.ds(pl.multiple_of(ids_ref[b] * BLOCK, BLOCK), BLOCK)
            out_ref[b * BLOCK : (b + 1) * BLOCK, :] = r_ref[at, :]

    smem = pl.BlockSpec(memory_space=pltpu.SMEM)
    vmem = pl.BlockSpec(memory_space=pltpu.VMEM)
    return pl.pallas_call(
        kernel,
        in_specs=[smem, smem, vmem, vmem, vmem, vmem],
        out_specs=vmem,
        out_shape=jax.ShapeDtypeStruct((rows, 3 * HD), bf16),
        scratch_shapes=[pltpu.VMEM((rows, HD), bf16)] * 4
        + [pltpu.VMEM((rows, 3 * HD), bf16)]
        + [pltpu.VMEM((rows, HD), f32)] * 2,
        compiler_params=BIG,
        cost_estimate=cost(6 * rows * rows * HD, 20 * rows * HD, rows * rows / 2),
        name="attention_backward",
    )(ids, order, qkv, grad, lse, table)


def gather_plane(nchip, chip, core, src, dst_of, send, recv, local):
    sibling = {"core": 1 - core}
    rows = src.shape[0]
    half = rows // 2
    here = dst_of(chip, core)
    begun = [pltpu.make_async_copy(src, here, local)]
    begun.append(remote(src, here, send.at[0], recv.at[0], sibling))
    relays = []
    arrivals = []

    def cut(ref, h):
        return ref.at[pl.ds(h * half, half), :]

    if nchip == 4:
        beside = chip + 1 - 2 * lax.rem(chip, 2)
        below = lax.rem(chip + 2, 4)
        across = 3 - chip
        order = ((beside, 0, 1), (below, 1, 2), (beside, 1, 1), (below, 0, 2))
        for i, (to, h, d) in enumerate(order):
            slot = 4 + 2 * d + h
            begun.append(
                remote(cut(src, h), cut(here, h), send.at[slot], recv.at[slot], {"chip": to})
            )

        def passing(owner, h, to):
            part = cut(dst_of(owner, core), h)
            return remote(part, part, send.at[10 + h], recv.at[10 + h], {"chip": to})

        relays = [(passing(beside, 0, below), beside, 0, 6), (passing(below, 1, beside), below, 1, 9)]
        arrivals = [(beside, 1, 7, 1), (below, 0, 8, 2), (across, 0, 10, 3), (across, 1, 11, 3)]
        others = [(beside, 1), (below, 2), (across, 3)]
    else:
        others = [(lax.rem(chip + d, nchip), d) for d in range(1, nchip)]
        for to, d in others:
            begun.append(
                remote(src, here, send.at[nchip + d], recv.at[nchip + chip], {"chip": to})
            )

    def side(owner, slot):
        part = dst_of(owner, core)
        return remote(part, part, send.at[slot], recv.at[slot], sibling)

    def slot_of(owner, d):
        return d if nchip == 4 else 2 * nchip + owner

    def first():
        for copy in begun:
            copy.start()

    def onward():
        if nchip == 4:
            for copy, owner, h, slot in relays:
                part = cut(dst_of(owner, core), h)
                remote(part, part, send.at[0], recv.at[slot], sibling).wait_recv()
                copy.start()

    def pass_on():
        if nchip == 4:
            for owner, h, slot, d in arrivals:
                part = cut(dst_of(owner, core), h)
                remote(part, part, send.at[0], recv.at[slot], sibling).wait_recv()
                if slot != 10:
                    side(owner, d).start()
        else:
            for owner, d in others:
                part = dst_of(owner, core)
                remote(part, part, send.at[0], recv.at[nchip + owner], sibling).wait_recv()
                side(owner, slot_of(owner, d)).start()

    def last():
        begun[0].wait()
        for copy in begun[1:]:
            copy.wait_send()
        for copy, owner, h, slot in relays:
            copy.wait_send()
        there = dst_of(chip, 1 - core)
        remote(there, there, send.at[0], recv.at[0], sibling).wait_recv()
        for owner, d in others:
            side(owner, slot_of(owner, d)).wait_send()
            there = dst_of(owner, 1 - core)
            remote(there, there, send.at[0], recv.at[slot_of(owner, d)], sibling).wait_recv()

    return first, onward, pass_on, last


def scatter_plane(nchip, chip, part, own, first, second, send, recv, local):
    halves = own.shape[0]
    copies = []
    shape = own.shape[2:]

    def add(dst, terms):
        def rows(lead):
            @pl.loop(0, shape[-2] // 16)
            def _(i):
                at = lead + (pl.ds(pl.multiple_of(i * 16, 16), 16), slice(None))
                acc = dst[at].astype(f32)
                for term in terms:
                    acc = acc + term[at].astype(f32)
                dst[at] = acc.astype(bf16)

        if len(shape) == 2:
            rows(())
        else:

            @pl.loop(0, shape[0])
            def _(b):
                rows((b,))

    if nchip == 4:
        beside = chip + 1 - 2 * lax.rem(chip, 2)
        below = lax.rem(chip + 2, 4)
        across = 3 - chip
        ways = [(beside, below), (below, beside)]
        kept = [
            [
                pltpu.make_async_copy(part(chip, h), own.at[h, 0], local.at[h, 0]),
                pltpu.make_async_copy(part(ways[h][1], h), own.at[h, 1], local.at[h, 1]),
            ]
            for h in range(2)
        ]
        leave = [
            [
                remote(
                    part(across, h), first.at[h, 1], send.at[h, 1], recv.at[h, 1],
                    {"chip": ways[h][0]},
                ),
                remote(
                    part(ways[h][0], h), first.at[h, 0], send.at[h, 0], recv.at[h, 0],
                    {"chip": ways[h][0]},
                ),
            ]
            for h in range(2)
        ]
        follow = [
            remote(
                own.at[h, 1], second.at[h], send.at[h, 2], recv.at[h, 2], {"chip": ways[h][1]}
            )
            for h in range(2)
        ]

        def begin():
            for i in range(2):
                for h in range(2):
                    leave[h][i].start()
            for h in range(2):
                kept[h][1].start()
                kept[h][0].start()

        def middle():
            for h in range(2):
                kept[h][1].wait()
                leave[h][0].wait_recv()
                add(own.at[h, 1], [first.at[h, 1]])
                follow[h].start()

        def finish():
            for h in range(2):
                kept[h][0].wait()
                leave[h][1].wait_recv()
                follow[h].wait_recv()
                add(own.at[h, 0], [first.at[h, 0], second.at[h]])

        def last():
            for h in range(2):
                for copy in leave[h] + [follow[h]]:
                    copy.wait_send()
    else:
        to = [lax.rem(chip + d, nchip) for d in range(nchip)]
        kept = pltpu.make_async_copy(part(chip, 0), own.at[0, 0], local.at[0, 0])
        leave = [
            remote(part(to[d], 0), first.at[0, d], send.at[0, d], recv.at[0, d], {"chip": to[d]})
            for d in range(1, nchip)
        ]

        def begin():
            for copy in leave:
                copy.start()
            kept.start()

        def middle():
            pass

        def finish():
            kept.wait()
            for copy in leave:
                copy.wait_recv()
            add(own.at[0, 0], [first.at[0, d] for d in range(1, nchip)])

        def last():
            for copy in leave:
                copy.wait_send()

    return begin, middle, finish, last


def tail(nz, nchip, ncore, dwo, dwd, dwi, dwq, part_e, vectors):
    width = dwo.shape[1]
    ro, rd = dwo.shape[0] // nchip, dwd.shape[0] // nchip
    halves = 2 if nchip == 4 else 1
    hz = nz // halves
    ho, hd = ro // halves, rd // halves
    ci, cq = dwi.shape[2], dwq.shape[1] // 3
    wrows = width // nz
    ri = wrows // nchip
    own = part_e.shape[0] // nz // ncore
    vr = vectors.shape[0]
    dwo = dwo.reshape(nchip, ro, width)
    dwq = dwq.reshape(nz, nchip, ri, 3 * cq)
    dwd = dwd.reshape(nchip, rd, width)
    part_e = part_e.reshape(nz, ncore, own, width)

    def kernel(
        dwo_ref, dwd_ref, dwi_ref, dwq_ref, pe_ref, vec_ref,
        go_ref, gd_ref, gi_ref, gq_ref, e_ref, vsum_ref,
        oo, fo, so, oq, fq, sq, od, fd, sd, ti, tq, se, me, ze, v1, v2, v3,
        ro_s, ro_r, ro_l, rq_s, rq_r, rq_l, rd_s, rd_r, rd_l, x_s, x_r, x_l, ez_s, ez_r, t_s, t_r, t_l,
        go_s, go_r, gd_s, gd_r, gi_s, gi_r, gq_s, gq_r, own_l,
        v_s, v_r, v_l,
    ):
        z = lax.axis_index("seq")
        chip = lax.axis_index("chip")
        core = lax.axis_index("core")
        sibling = {"core": 1 - core}

        def z_at(d):
            return lax.rem(z + d, nz)

        def chip_at(d):
            return lax.rem(chip + d, nchip)

        greet(
            [{"seq": z_at(d)} for d in range(1, nz)]
            + [{"chip": chip_at(d)} for d in range(1, nchip)]
            + [sibling]
        )

        def turn(kind, part, turned):
            copies = [
                remote(
                    part(z_at(d)), turned.at[z], t_s.at[kind, d], t_r.at[kind, z],
                    {"seq": z_at(d)},
                )
                for d in range(1, nz)
            ]
            copies.append(pltpu.make_async_copy(part(z), turned.at[z], t_l.at[kind]))
            for copy in copies:
                copy.start()
            return copies

        def turned_at(kind, part, turned, source):
            return remote(part, turned.at[source], t_s.at[kind, 0], t_r.at[kind, source], sibling)

        sum_q = scatter_plane(
            nchip, chip, lambda c, h: dwq_ref.at[pl.ds(h * hz, hz), c], oq, fq, sq, rq_s, rq_r, rq_l
        )
        sum_o = scatter_plane(
            nchip, chip, lambda c, h: dwo_ref.at[c, pl.ds(h * ho, ho)], oo, fo, so, ro_s, ro_r, ro_l
        )
        sum_d = scatter_plane(
            nchip, chip, lambda c, h: dwd_ref.at[c, pl.ds(h * hd, hd)], od, fd, sd, rd_s, rd_r, rd_l
        )
        turn_i = turn(0, lambda to: dwi_ref.at[to], ti)
        sum_q[0]()

        exchanged = [
            remote(pe_ref.at[:, 1 - core], se, x_s.at[0], x_r.at[0], sibling),
        ]
        keep = [
            pltpu.make_async_copy(pe_ref.at[:, core], me, x_l.at[0]),
        ]
        for copy in exchanged + keep:
            copy.start()

        v_own = pltpu.make_async_copy(vec_ref, v1.at[chip], v_l.at[0])
        v_own.start()
        v_chips = [
            remote(vec_ref, v1.at[chip], v_s.at[d], v_r.at[chip], {"chip": chip_at(d)})
            for d in range(1, nchip)
        ]
        for copy in v_chips:
            copy.start()

        def pair_sum(which, mine, theirs):
            exchanged[which].wait_recv()
            keep[which].wait()

            @pl.loop(0, nz)
            def _(b):
                @pl.loop(0, own // 16)
                def _(i):
                    at = pl.ds(pl.multiple_of(i * 16, 16), 16)
                    mine[b, at, :] = (
                        mine[b, at, :].astype(f32) + theirs[b, at, :].astype(f32)
                    ).astype(bf16)

        def z_sends(which, mine, landing):
            return [
                remote(
                    mine.at[z_at(d)], landing.at[d], ez_s.at[which, d], ez_r.at[which, d],
                    {"seq": z_at(d)},
                )
                for d in range(1, nz)
            ]

        def z_sum(copies, mine, landing, out):
            for copy in copies:
                copy.wait_recv()

            @pl.loop(0, own // 16)
            def _(i):
                at = pl.ds(pl.multiple_of(i * 16, 16), 16)
                acc = mine[z, at, :].astype(f32)
                for d in range(1, nz):
                    acc = acc + landing[d, at, :].astype(f32)
                out[at, :] = acc

        pair_sum(0, me, se)
        sum_q[1]()
        sum_o[0]()
        sum_d[0]()

        go_at = lambda c, k, h: go_ref.at[pl.ds(k * (ro * nchip) + c * ro + h * ho, ho), :]
        gd_at = lambda c, k, h: gd_ref.at[pl.ds(k * (rd * nchip) + c * rd + h * hd, hd), :]
        gi_at = lambda c, k, s: gi_ref.at[
            pl.ds(c * ri, ri), pl.ds((s * ncore + k) * ci, ci)
        ]
        gq_at = lambda c, k, s, g: gq_ref.at[
            pl.ds(c * ri, ri), pl.ds(g * nz * ncore * cq + (s * ncore + k) * cq, cq)
        ]
        group = functools.partial(gather_plane, nchip, chip, core)
        groups = []
        for dz in range(1, nz):
            turned_at(0, dwi_ref.at[0], ti, z_at(dz)).wait_recv()
        turn_i[-1].wait()
        for source in range(nz):
            groups.append(
                group(
                    ti.at[source], functools.partial(gi_at, s=source), gi_s.at[source],
                    gi_r.at[source], own_l.at[source],
                )
            )
            groups[-1][0]()
        sent_e = z_sends(0, me, ze)
        for copy in sent_e:
            copy.start()
        sum_q[2]()
        turn_q = turn(1, lambda to: oq.at[to // hz, 0, lax.rem(to, hz)], tq)

        v_own.wait()
        for d in range(1, nchip):
            other = chip_at(d)
            remote(vec_ref, v1.at[other], v_s.at[d], v_r.at[other], sibling).wait_recv()
        total = v1[0]
        for d in range(1, nchip):
            total = total + v1[d]
        v2[core] = total
        v_side = remote(v2.at[core], v2.at[core], v_s.at[nchip], v_r.at[nchip], sibling)
        v_side.start()

        v_side.wait_recv()
        vz = v2[0]
        for c in range(1, ncore):
            vz = vz + v2[c]
        v3[z] = vz
        v_zs = [
            remote(v3.at[z], v3.at[z], v_s.at[nchip + d], v_r.at[nchip + 1 + z], {"seq": z_at(d)})
            for d in range(1, nz)
        ]
        for copy in v_zs:
            copy.start()

        sum_o[1]()
        sum_d[1]()
        for first, onward, pass_on, last in groups:
            onward()
        sum_o[2]()
        sum_d[2]()
        for h in range(halves):
            for at, (buf, place, sends, recvs) in enumerate(
                ((oo, go_at, go_s, go_r), (od, gd_at, gd_s, gd_r))
            ):
                groups.append(
                    group(
                        buf.at[h, 0], functools.partial(place, h=h), sends.at[h], recvs.at[h],
                        own_l.at[nz + 2 * at + h],
                    )
                )
                groups[-1][0]()

        for dz in range(1, nz):
            turned_at(1, oq.at[0, 0, 0], tq, z_at(dz)).wait_recv()
        turn_q[-1].wait()
        later = []
        for source in range(nz):
            for g in range(3):
                later.append(
                    group(
                        tq.at[source, :, pl.ds(g * cq, cq)],
                        functools.partial(gq_at, s=source, g=g),
                        gq_s.at[source, g], gq_r.at[source, g], own_l.at[4 + nz + 3 * source + g],
                    )
                )
        for first, onward, pass_on, last in later:
            first()
        for first, onward, pass_on, last in groups[nz:]:
            onward()
        for first, onward, pass_on, last in groups[:nz]:
            pass_on()
        for first, onward, pass_on, last in later:
            onward()
        for first, onward, pass_on, last in groups[nz:]:
            pass_on()

        for d in range(1, nz):
            other = z_at(d)
            remote(v3.at[0], v3.at[other], v_s.at[0], v_r.at[nchip + 1 + other], sibling).wait_recv()
        total = v3[0]
        for d in range(1, nz):
            total = total + v3[d]
        vsum_ref[...] = total

        z_sum(sent_e, me, ze, e_ref)
        for first, onward, pass_on, last in later:
            pass_on()

        for first, onward, pass_on, last in groups + later:
            last()
        for begin, middle, finish, last in (sum_o, sum_q, sum_d):
            last()
        for copy in exchanged + sent_e + v_chips + v_zs + [v_side]:
            copy.wait_send()
        for copy in turn_i[:-1] + turn_q[:-1]:
            copy.wait_send()

    dma = pltpu.SemaphoreType.DMA
    anywhere = pl.BlockSpec(memory_space=pl.ANY)
    vmem = pl.BlockSpec(memory_space=pltpu.VMEM)
    out_shape = [
        jax.ShapeDtypeStruct((ncore * nchip * ro, width), bf16),
        jax.ShapeDtypeStruct((ncore * nchip * rd, width), bf16),
        jax.ShapeDtypeStruct((wrows, nz * ncore * ci), bf16),
        jax.ShapeDtypeStruct((wrows, 3 * nz * ncore * cq), bf16),
        jax.ShapeDtypeStruct((own, width), f32),
        jax.ShapeDtypeStruct((vr, 128), f32),
    ]
    ranked = (nz, own, width)
    slots = max(3 * nchip, 12)
    pair = 2 if nchip == 4 else 1
    nfirst = 2 if nchip == 4 else nchip
    return pl.pallas_call(
        kernel,
        in_specs=[anywhere] * 5 + [vmem],
        out_specs=[anywhere] * 4 + [vmem] * 2,
        out_shape=out_shape,
        scratch_shapes=[
            pltpu.VMEM((halves, pair, ho, width), bf16),
            pltpu.VMEM((halves, nfirst, ho, width), bf16),
            pltpu.VMEM((halves, ho, width), bf16),
            pltpu.VMEM((halves, pair, hz, ri, 3 * cq), bf16),
            pltpu.VMEM((halves, nfirst, hz, ri, 3 * cq), bf16),
            pltpu.VMEM((halves, hz, ri, 3 * cq), bf16),
            pltpu.VMEM((halves, pair, hd, width), bf16),
            pltpu.VMEM((halves, nfirst, hd, width), bf16),
            pltpu.VMEM((halves, hd, width), bf16),
            pltpu.VMEM((nz, ri, ci), bf16),
            pltpu.VMEM((nz, ri, 3 * cq), bf16),
            pltpu.VMEM(ranked, bf16),
            pltpu.VMEM(ranked, bf16),
            pltpu.VMEM(ranked, bf16),
            pltpu.VMEM((nchip, vr, 128), f32),
            pltpu.VMEM((ncore, vr, 128), f32),
            pltpu.VMEM((nz, vr, 128), f32),
            dma((halves, nchip)), dma((halves, nchip)), dma((halves, 2)),
            dma((halves, nchip)), dma((halves, nchip)), dma((halves, 2)),
            dma((halves, nchip)), dma((halves, nchip)), dma((halves, 2)),
            dma((2,)), dma((2,)), dma((2,)),
            dma((2, nz)), dma((2, nz)),
            dma((2, nz)), dma((2, nz)), dma((2,)),
            dma((halves, slots)), dma((halves, slots)),
            dma((halves, slots)), dma((halves, slots)),
            dma((nz, slots)), dma((nz, slots)),
            dma((nz, 3, slots)), dma((nz, 3, slots)),
            dma((4 + 4 * nz,)),
            dma((nchip + nz,)), dma((nchip + nz + 1,)), dma((1,)),
        ],
        compiler_params=pltpu.CompilerParams(
            collective_id=2, has_side_effects=True, vmem_limit_bytes=60 * 2**20
        ),
        name="tail",
    )(dwo, dwd, dwi, dwq, part_e, vectors)


def on_device(
    nz,
    nchip,
    ncore,
    tokens,
    block_ids,
    cotangent,
    norm1_gain,
    norm1_bias,
    norm2_gain,
    norm2_bias,
    w_qkv,
    b_qkv,
    w_dense,
    b_dense,
    w_in,
    b_in,
    w_out,
    b_out,
):
    own, width = tokens.shape
    z = lax.axis_index("seq")
    chip = lax.axis_index("chip")
    core = lax.axis_index("core")
    ranks = nz * ncore
    rank = z * ncore + core
    rows = ranks * own
    ffr = w_out.shape[0] // ncore
    hc = width // ranks
    split = max(1, HD // hc)
    wrows = width // nz
    blocks = block_ids.shape[1]
    length = blocks * BLOCK
    core_at = core.reshape(1)

    parts = [norm1_gain, norm1_bias, norm2_gain, norm2_bias, b_qkv, b_dense + 0, b_in, b_out,
             block_ids.reshape(-1)]
    sizes = [p.shape[0] for p in parts]
    total = -(-sum(sizes) // 2048) * 2048
    starts = [sum(sizes[:i]) for i in range(len(sizes))]
    small = sum(
        jnp.pad(p.astype(f32), (at, total - at - p.shape[0])) for p, at in zip(parts, starts)
    )
    small = small.astype(bf16).reshape(-1, 128)
    tok, w_in_c, w_qkv_c, small = front(nz, nchip, ncore, tokens, w_in, w_qkv, small)
    tok = tok.reshape(rows, width)
    small = small.reshape(nz, total)

    def vector(i):
        return small[:, starts[i] : starts[i] + sizes[i]].astype(f32).reshape(1, -1)

    gain1, bias1, gain2, bias2 = [vector(i) for i in range(4)]
    bias_c = lax.dynamic_index_in_dim(vector(4).reshape(3, ranks, hc), rank, 1, keepdims=False)
    bias_c = bias_c.reshape(1, 3 * hc)
    bias_in = lax.dynamic_slice_in_dim(vector(6), rank * ffr, ffr, 1)
    ids = vector(8).astype(jnp.int32).reshape(nz, blocks)
    tok, cot_own = lax.optimization_barrier((tok, cotangent))
    cot = lax.all_gather(cot_own, TP, axis=0, tiled=True)

    per_chip = blocks // nchip
    ids_rows = lax.dynamic_slice_in_dim(ids, chip * per_chip, per_chip, 1).reshape(-1)
    ids_seq = lax.dynamic_index_in_dim(ids, chip, 0, keepdims=False)
    slots = jnp.arange(blocks, dtype=jnp.int32)
    order = jnp.sum(jnp.where(ids_seq[None, :] == slots[:, None], slots[None, :], 0), axis=1)
    place = (lax.rem(rank, split) == 0).astype(jnp.int32).reshape(1)
    table = jnp.asarray(turn_table(length))

    def heads_of(x):
        g = x.shape[1] // hc
        if split > 1:
            x = lax.all_gather(x.reshape(rows, g, hc), "core", axis=2, tiled=True)
        x = x.reshape(nz, rows // nz, g * HD)
        return lax.all_to_all(x, "chip", 0, 0, tiled=True).reshape(length, g * HD)

    def heads_back(x):
        g = x.shape[1] // HD
        x = x.reshape(nchip, length // nchip, g * HD)
        x = lax.all_to_all(x, "chip", 0, 0, tiled=True).reshape(rows, g * HD)
        if split > 1:
            x = lax.dynamic_slice_in_dim(x.reshape(rows, g, HD), core * hc, hc, 2)
        return x.reshape(rows, g * hc)

    tile = 256
    normed1, qkv = projections(nz, ids_rows, place, tok, w_qkv_c, bias_c, gain1, bias1, table)
    qkv = heads_of(qkv)
    normed2, active, slope = feed_forward(nz, tok, w_in_c, bias_in, gain2, bias2)
    qkv, active, slope, normed2 = lax.optimization_barrier((qkv, active, slope, normed2))
    attended, lse = attention_forward(ids_seq, order, qkv, tile)
    attended, cot = lax.optimization_barrier((attended, cot))
    mixed = heads_back(attended)

    grad_mixed = grad_of_mixed(nz, core_at, cot, w_dense, hc)
    grad_mixed, cot = lax.optimization_barrier((grad_mixed, cot))
    g = heads_of(grad_mixed)
    grad_hidden, sum_bin = grad_of_hidden(nz, core_at, cot, w_out, slope)
    dw_in = lax.dot_general(normed2, grad_hidden, TN, preferred_element_type=f32).astype(bf16)
    dw_in = dw_in.reshape(nz, nchip, wrows // nchip, ffr).transpose(1, 0, 2, 3)
    dw_in = dw_in.reshape(width, ffr)
    g, dw_in, mixed = lax.optimization_barrier((g, dw_in, mixed))
    s_in = lax.psum_scatter(dw_in, "chip", scatter_dimension=0, tiled=True)
    s_in = s_in.reshape(nz, wrows // nchip, ffr)
    dqkv = attention_backward(ids_seq, order, qkv, g, lse, table, tile)
    dqkv, mixed, active, cot, grad_hidden = lax.optimization_barrier(
        (dqkv, mixed, active, cot, grad_hidden)
    )
    grad_project = heads_back(dqkv)
    part_out = layer_out(nz, core_at, mixed, w_dense, active, w_out)
    dw_out = lax.dot_general(active, cot, TN, preferred_element_type=f32).astype(bf16)
    dw_dense = lax.dot_general(mixed, cot, TN, preferred_element_type=f32).astype(bf16)
    e2, sums2 = norm_back(nz, grad_hidden, w_in_c, tok, gain2, None, False)
    grad_project, part_out, dw_out, dw_dense, e2, s_in = lax.optimization_barrier(
        (grad_project, part_out, dw_out, dw_dense, e2, s_in)
    )
    summed_out = lax.psum_scatter(part_out, TP, scatter_dimension=0, tiled=True).astype(f32)
    dw_qkv = lax.dot_general(normed1, grad_project, TN, preferred_element_type=f32).astype(bf16)
    e_part, sums1, sum_bqkv = norm_back(nz, grad_project, w_qkv_c, tok, gain1, e2, True)

    here = jnp.arange(ranks, dtype=jnp.int32) == rank
    mine_bqkv = jnp.where(here[None, :, None], sum_bqkv.reshape(3, 1, hc), 0.0)
    mine_bin = jnp.where(here[:, None], sum_bin.reshape(1, ffr), 0.0)
    vectors = [
        sums1.reshape(-1),
        sums2.reshape(-1),
        mine_bqkv.reshape(-1),
        jnp.sum(cotangent.astype(f32), axis=0),
        mine_bin.reshape(-1),
    ]
    vectors = jnp.concatenate([v.reshape(-1, 128) for v in vectors])
    g_wout, g_wdense, g_win, g_wqkv, e, sums = tail(
        nz, nchip, ncore, dw_out, dw_dense, s_in, dw_qkv, e_part, vectors
    )
    sums = sums.reshape(-1)
    at = 0
    small_out = []
    for size in (width, width, width, width, 3 * width, width, ranks * ffr):
        small_out.append(lax.dynamic_slice_in_dim(sums, at + z * (size // nz), size // nz))
        at += size
    g_gain1, g_bias1, g_gain2, g_bias2, g_bqkv, g_bdense, g_bin = small_out

    output = (tokens.astype(f32) + summed_out + vector(5) + vector(7)).astype(bf16)
    xhat_own, inv_own = stats(tokens.astype(f32))
    terms = (
        e
        - jnp.mean(e, axis=-1, keepdims=True)
        - xhat_own * jnp.mean(e * xhat_own, axis=-1, keepdims=True)
    ) * inv_own
    grad_tokens = (cotangent.astype(f32) + terms).astype(bf16)
    g_wout, g_wdense, g_win, g_wqkv = [g.astype(f32) for g in (g_wout, g_wdense, g_win, g_wqkv)]
    return (
        output,
        grad_tokens,
        g_gain1,
        g_bias1,
        g_gain2,
        g_bias2,
        g_wqkv,
        g_bqkv,
        g_wdense,
        g_bdense,
        g_win,
        g_bin,
        g_wout,
        g_bdense,
    )


def solution(mesh):
    nz, nctx = mesh.shape["seq"], mesh.shape["ctx"]
    ncore = 2
    nchip = nctx // ncore
    fine = Mesh(mesh.devices.reshape(nz, nchip, ncore), ("seq", "chip", "core"))
    own = P(("seq", "chip", "core"), None)
    vec = P("seq")
    mat = P("seq", None)
    return jax.shard_map(
        functools.partial(on_device, nz, nchip, ncore),
        mesh=fine,
        in_specs=(own, mat, own, vec, vec, vec, vec, mat, vec, mat, vec, mat, vec, mat, vec),
        out_specs=(own, own, vec, vec, vec, vec, mat, vec, mat, vec, mat, vec, mat, vec),
        check_vma=False,
    )
```

time: 770 us -> 587 us (0.76)
  matrix products: 135 us -> 36.7 us
  local copies, waits for them, and re-layouts: 52 us -> 14.8 us
  other arithmetic: 73.9 us -> 44.5 us
  blocking collectives: 21.4 us -> 0 us
    dot_general x12 -> x4, matrix products: 135 us -> 36.7 us  [the longest x1 11.2 us: on_device(): lax.dot_general(active, cot, TN, preferred_element_type=f32).astype(bf16)]
    unnamed x1 -> x0, blocking collectives: 21.4 us -> none
    all_to_all x4, waiting for transfers between devices: 27.9 us -> 9.23 us  [the longest x2 9.22 us: heads_of(): return lax.all_to_all(x, 'chip', 0, 0, tiled=True).reshape(length, g * HD)]
    reduce_scatter x0 -> x2, waiting for transfers between devices: none -> 15.7 us  [the longest x1 15.7 us: on_device(): s_in = lax.psum_scatter(dw_in, 'chip', scatter_dimension=0, tiled=True)]
    unnamed x90 -> x41, local copies, waits for them, and re-layouts: 19 us -> 5.47 us
    another operation x2 -> x1, other arithmetic: 11.6 us -> 0.01 us  [on_device(): vector(4).reshape(3, ranks, hc)]
    slice x8 -> x0, local copies, waits for them, and re-layouts: 11.5 us -> none  [the longest x4 9.55 us: rotate(): u[..., ROT:]]
    convert_element_type x7 -> x2, other arithmetic: 8.58 us -> 0.66 us  [the longest x1 0.66 us: on_device(): p.astype(f32)]
  transfers between devices with their start and end apart: 5 -> 7, of which waited for: 2 -> 3; matrix products, arithmetic and copies ran while one was open for 13% -> 15% of each run, Pallas kernels for 1% -> 52%
where the time goes in v3:
time: 587 us; the launch traced here: 580 us
  Pallas kernels  421 us (72%)
  other arithmetic  44.5 us (8%)
  matrix products  36.7 us (6%)
  waiting for transfers between devices  32.2 us (5%)
  starting transfers between devices  16.5 us (3%)
  local copies, waits for them, and re-layouts  14.8 us (3%)
  between operations  14.5 us (2%)
    pallas_call x1, Pallas kernels, tail(): pl.pallas_call(kernel, in_specs=[anywhere] * 5 + [vmem], out_specs=[anywh...  198 us
    pallas_call x1, Pallas kernels, front(): pl.pallas_call(kernel, in_specs=[anywhere] * 4, out_specs=[anywhere] * 4,...  112 us
    convert_element_type x4, other arithmetic, on_device(): g.astype(f32)  35.5 us
    pallas_call x2, Pallas kernels, norm_back(): pl.pallas_call(kernel, grid=(nz,), in_specs=[part(cols), whole((width, co...  32 us
    pallas_call x1, Pallas kernels, feed_forward(): pl.pallas_call(kernel, grid=(nz,), in_specs=[part(width), whole((width, c...  16.3 us
    reduce_scatter x1, waiting for transfers between devices, on_device(): s_in = lax.psum_scatter(dw_in, 'chip', scatter_dimension=0, tiled=True)  15.7 us
    pallas_call x1, Pallas kernels, projections(): pl.pallas_call(kernel, grid_spec=pltpu.PrefetchScalarGridSpec(num_scalar_...  15.2 us
    pallas_call x1, Pallas kernels, layer_out(): pl.pallas_call(kernel, grid_spec=pltpu.PrefetchScalarGridSpec(num_scalar_...  13 us
  transfers between devices with their start and end apart: 7, of which 3 were waited for; matrix products, arithmetic and copies ran while one was open for 15% of the time, Pallas kernels for 52%

profile of v3, /device:TPU:0, one launch (start us, length us, event | category | flops | bytes accessed | tf_op | source)
XLA Modules:
  0.0 579.9 jit_solution(4689595028026805948)
XLA Ops:
  7.2 0.7 convert_bitcast_fusion.7
  7.9 1.4 fusion.13.sm_ref
  9.3 112.1 %front.1 = (bf16[4,2,192,2048]{3,2,1,0:T(8,128)(2,1)}, bf16[2048,1024]{1,0:T(8,128)(2,1)}, bf16[2048,768]{1,0:T(8,128)(2,1)}, bf16[4,64,128]{2,1,0:T(8,128)(2,1)}) custom-call(bf16[192,2048]{1,0:T(8,128)(2,1)} %tok_ref.1, bf16[512,8192]{1,0:T(8,128)(2,1)} %wi_ref.1, bf16[512,6144]{1,0:T(8,128)(2,1)} %wq_ref.1, bf16[64,128]{1,0:T(8,128)(2,1)} %fusion.13.sm_ref), custom_call_target="tpu_custom_call" | custom-call | tf_op jit(solution)/shard_map/front/pallas_call | solution.py:262
  121.5 0.9 copy.44
  122.4 0.6 reshape.176.ids_ref
  123.1 0.6 copy.36
  123.7 0.6 copy.37
  124.3 0.6 constant_dynamic-slice_fusion.1
  124.9 15.2 %projections.1 = (bf16[1536,2048]{1,0:T(8,128)(2,1)}, bf16[1536,768]{1,0:T(8,128)(2,1)}) custom-call(s32[16]{0:T(128)} %reshape.176.ids_ref, s32[1]{0:T(128)} %constant.62.clone.1.place_ref, bf16[1536,2048]{1,0:T(8,128)(2,1)} %bitcast.77, bf16[2048,768]{1,0:T(8,128)(2,1)} %get-tuple-element.65.w_ref.refs_1_, f32[1,768]{1,0:T(1,128)} %bitcast.111, ...), custom_call_target="tpu_custom_call" | custom-call | flops 4831838208 | bytes 15728640 | tf_op jit(solution)/shard_map/projections/pallas_call | solution.py:340
  140.1 4.3 all-to-all-start
  144.5 0.6 copy.39
  145.1 0.6 copy.40
  145.7 0.6 constant_dynamic-slice_fusion.b_ref
  146.3 0.6 select_reduce_fusion.order_ref
  146.9 16.3 %feed_forward.1 = (bf16[1536,2048]{1,0:T(8,128)(2,1)}, bf16[1536,1024]{1,0:T(8,128)(2,1)}, bf16[1536,1024]{1,0:T(8,128)(2,1)}) custom-call(bf16[1536,2048]{1,0:T(8,128)(2,1)} %bitcast.78, bf16[2048,1024]{1,0:T(8,128)(2,1)} %get-tuple-element.67.w_ref.refs_1_, f32[1,1024]{1,0:T(1,128)} %constant_dynamic-slice_fusion.b_ref, f32[1,2048]{1,0:T(1,128)} %bitcast.103, ...), custom_call_target="tpu_custom_call" | custom-call | flops 6442450944 | bytes 16777216 | tf_op jit(solution)/shard_map/feed_forward/pallas_call | solution.py:385
  163.3 9.2 %all-to-all-done = bf16[4,384,768]{2,1,0:T(8,128)(2,1)S(1)} async-done(((bf16[4,384,768]{2,1,0:T(8,128)(2,1)}), bf16[4,384,768]{2,1,0:T(8,128)(2,1)S(1)}, u32[]{:S(2)}, u32[]{:S(2)}) %all-to-all-start) | async-done | bytes 2359328 | tf_op jit(solution)/shard_map/all_to_all | solution.py:1221
  172.5 1.5 copy-done.6
  173.9 6.7 %attention_forward.1 = (bf16[1536,256]{1,0:T(8,128)(2,1)}, f32[1536,1]{1,0:T(8,128)}) custom-call(s32[16]{0:T(128)} %copy-done.13, s32[16]{0:T(128)} %select_reduce_fusion.order_ref, bf16[1536,768]{1,0:T(8,128)(2,1)} %bitcast.87), custom_call_target="tpu_custom_call" | custom-call | flops 1389153536 | bytes 3145728 | tf_op jit(solution)/shard_map/attention_forward/pallas_call | solution.py:579
  180.7 7.2 %all-gather.2.cloned.1.call-done.c_ref = bf16[1536,2048]{1,0:T(8,128)(2,1)} async-done(((bf16[192,2048]{1,0:T(8,128)(2,1)}), bf16[1536,2048]{1,0:T(8,128)(2,1)}) %all-gather.2.cloned.1.call-update) | async-done | bytes 6291472 | tf_op jit(solution)/shard_map/all_gather | solution.py:1206
  187.9 5.8 %grad_of_mixed.1 = bf16[1536,256]{1,0:T(8,128)(2,1)} custom-call(s32[1]{0:T(128)} %bitcast.7.core_ref, bf16[1536,2048]{1,0:T(8,128)(2,1)} %all-gather.2.cloned.1.call-done.c_ref, bf16[512,2048]{1,0:T(8,128)(2,1)} %wd_ref.1), custom_call_target="tpu_custom_call" | custom-call | flops 1610612736 | bytes 6291456 | tf_op jit(solution)/shard_map/grad_of_mixed/pallas_call | solution.py:439
  193.7 3.6 all-to-all-start.1
  197.4 11.5 %grad_of_hidden.1 = (bf16[1536,1024]{1,0:T(8,128)(2,1)}, f32[1,1024]{1,0:T(1,128)}) custom-call(s32[1]{0:T(128)} %bitcast.7.core_ref, bf16[1536,2048]{1,0:T(8,128)(2,1)} %all-gather.2.cloned.1.call-done.c_ref, bf16[2048,2048]{1,0:T(8,128)(2,1)} %wo_ref.1, bf16[1536,1024]{1,0:T(8,128)(2,1)} %get-tuple-element.78.d_ref), custom_call_target="tpu_custom_call" | custom-call | flops 6442450944 | bytes 10485760 | tf_op jit(solution)/shard_map/grad_of_hidden/pallas_call | solution.py:473
  208.9 4.2 all-to-all-start.2
  213.3 9.9 %convolution_convert_fusion.1 = bf16[2048,1024]{1,0:T(8,128)(2,1)S(1)} fusion(bf16[1536,2048]{1,0:T(8,128)(2,1)} %get-tuple-element.76, bf16[1536,1024]{1,0:T(8,128)(2,1)} %get-tuple-element.89.refs_0_), kind=kOutput, calls=%fused_computation.1 | convolution fusion | flops 6444548096 | bytes 13631488 | tf_op jit(solution)/shard_map/dot_general | solution.py:1244
  223.2 2.5 copy.34
  225.7 10.3 %attention_backward.1 = bf16[1536,768]{1,0:T(8,128)(2,1)} custom-call(s32[16]{0:T(128)} %copy-done.13, s32[16]{0:T(128)} %select_reduce_fusion.order_ref, bf16[1536,768]{1,0:T(8,128)(2,1)} %bitcast.88, bf16[1536,256]{1,0:T(8,128)(2,1)} %bitcast.92, f32[1536,1]{1,0:T(8,128)} %get-tuple-element.82.lse_ref, f32[3,1536,128]{2,1,0:T(8,128)} %constant.83.clone.t_ref), custom_call_target="tpu_custom_call" | custom-call | flops 3623878656 | bytes 7864320 | tf_op jit(solution)/shard_map/attention_backward/pallas_call | solution.py:643
  236.0 4.2 all-to-all-start.3
  240.2 5.8 %convolution_convert_fusion.3 = bf16[256,2048]{1,0:T(8,128)(2,1)} fusion(bf16[1536,256]{1,0:T(8,128)(2,1)S(1)} %bitcast.75, bf16[1536,2048]{1,0:T(8,128)(2,1)} %all-gather.2.cloned.1.call-done.c_ref), kind=kOutput, calls=%fused_computation.3 | convolution fusion | flops 1611137024 | bytes 8126464 | tf_op jit(solution)/shard_map/dot_general | solution.py:1257
  246.0 16.1 %norm_back.2 = (bf16[1536,2048]{1,0:T(8,128)(2,1)}, f32[2,2048]{1,0:T(2,128)}) custom-call(bf16[1536,1024]{1,0:T(8,128)(2,1)} %get-tuple-element.89.refs_0_, bf16[2048,1024]{1,0:T(8,128)(2,1)} %get-tuple-element.67.w_ref.refs_1_, bf16[1536,2048]{1,0:T(8,128)(2,1)} %bitcast.79, f32[1,2048]{1,0:T(1,128)} %bitcast.104), custom_call_target="tpu_custom_call" | custom-call | flops 6442450944 | bytes 23068672 | tf_op jit(solution)/shard_map/norm_back/pallas_call | solution.py:531
  262.1 13.0 %layer_out.1 = bf16[1536,2048]{1,0:T(8,128)(2,1)} custom-call(s32[1]{0:T(128)} %bitcast.7.core_ref, bf16[1536,256]{1,0:T(8,128)(2,1)} %bitcast.76, bf16[512,2048]{1,0:T(8,128)(2,1)} %wd_ref.1, bf16[1536,1024]{1,0:T(8,128)(2,1)} %get-tuple-element.87.a_ref, bf16[2048,2048]{1,0:T(8,128)(2,1)} %wo_ref.1), custom_call_target="tpu_custom_call" | custom-call | flops 8053063680 | bytes 16777216 | tf_op jit(solution)/shard_map/layer_out/pallas_call | solution.py:415
  275.2 11.2 %convolution_convert_fusion = bf16[1024,2048]{1,0:T(8,128)(2,1)} fusion(bf16[1536,1024]{1,0:T(8,128)(2,1)} %get-tuple-element.87.a_ref, bf16[1536,2048]{1,0:T(8,128)(2,1)} %all-gather.2.cloned.1.call-done.c_ref), kind=kOutput, calls=%fused_computation | convolution fusion | flops 6444548096 | bytes 13631488 | tf_op jit(solution)/shard_map/dot_general | solution.py:1256
  286.4 15.7 %reduce-scatter.3.cloned.1.call-done = bf16[512,1024]{1,0:T(8,128)(2,1)} async-done(((bf16[2048,1024]{1,0:T(8,128)(2,1)}), bf16[512,1024]{1,0:T(8,128)(2,1)}) %reduce-scatter.3.cloned.1.call-update) | async-done | bytes 1048592 | tf_op jit(solution)/shard_map/reduce_scatter | solution.py:1248
  302.3 1.3 convert_reduce_fusion.1
  304.2 15.9 %norm_back.3 = (bf16[1536,2048]{1,0:T(8,128)(2,1)}, f32[2,2048]{1,0:T(2,128)}, f32[1,768]{1,0:T(1,128)}) custom-call(bf16[1536,768]{1,0:T(8,128)(2,1)} %bitcast.73, bf16[2048,768]{1,0:T(8,128)(2,1)} %get-tuple-element.65.w_ref.refs_1_, bf16[1536,2048]{1,0:T(8,128)(2,1)} %bitcast.80, f32[1,2048]{1,0:T(1,128)} %bitcast.100, ...), custom_call_target="tpu_custom_call" | custom-call | flops 4831838208 | bytes 22020096 | tf_op jit(solution)/shard_map/norm_back/pallas_call | solution.py:531
  320.0 0.7 reshape_reshape.16
  320.8 0.7 reduce
  321.7 9.9 %convolution_convert_fusion.2 = bf16[2048,768]{1,0:T(8,128)(2,1)} fusion(bf16[1536,2048]{1,0:T(8,128)(2,1)} %get-tuple-element.96, bf16[1536,768]{1,0:T(8,128)(2,1)S(1)} %bitcast.74), kind=kOutput, calls=%fused_computation.2 | convolution fusion | flops 4833411072 | bytes 11796480 | tf_op jit(solution)/shard_map/dot_general | solution.py:1263
  331.6 197.6 %tail.1 = (bf16[2048,2048]{1,0:T(8,128)(2,1)}, bf16[512,2048]{1,0:T(8,128)(2,1)}, bf16[512,8192]{1,0:T(8,128)(2,1)}, bf16[512,6144]{1,0:T(8,128)(2,1)}, f32[192,2048]{1,0:T(8,128)}, /*index=5*/f32[192,128]{1,0:T(8,128)}) custom-call(bf16[4,256,2048]{2,1,0:T(8,128)(2,1)} %bitcast.83, bf16[4,64,2048]{2,1,0:T(8,128)(2,1)} %bitcast.84, ...), custom_call_target="tpu_custom_call" | custom-call | tf_op jit(solution)/shard_map/tail/pallas_call | solution.py:1106
  529.2 9.4 %convert_element_type.108 = f32[512,6144]{1,0:T(8,128)} convert(bf16[512,6144]{1,0:T(8,128)(2,1)} %get-tuple-element.106) | non-fusion elementwise | flops 3145728 | bytes 18874368 | tf_op jit(solution)/shard_map/convert_element_type | solution.py:1296
  538.5 2.5 convert_element_type.109
  541.1 11.7 %convert_element_type.110 = f32[512,8192]{1,0:T(8,128)} convert(bf16[512,8192]{1,0:T(8,128)(2,1)} %get-tuple-element.108) | non-fusion elementwise | flops 4194304 | bytes 25165824 | tf_op jit(solution)/shard_map/convert_element_type | solution.py:1296
  552.8 1.4 dynamic_slice.43
  554.2 1.3 dynamic_slice.45
  555.5 11.8 %convert_element_type.111 = f32[2048,2048]{1,0:T(8,128)} convert(bf16[2048,2048]{1,0:T(8,128)(2,1)} %get-tuple-element.109) | non-fusion elementwise | flops 4194304 | bytes 25165824 | tf_op jit(solution)/shard_map/convert_element_type | solution.py:1296
  567.3 1.4 fusion.16
  568.7 0.4 fusion.15
  569.2 3.2 fusion.8
  572.4 0.6 copy.50
  (64 shorter events, 1.4 us)
Async XLA Ops:
  7.2 180.7 %all-gather.2.cloned.1.call-start = ((), (), s32[]{:S(2)}) async-start(), calls=%async_computation.6 | async-start | bytes 7077888 | tf_op jit(solution)/shard_map/all_gather | solution.py:1206
  140.1 32.3 %all-to-all-start = ((bf16[4,384,768]{2,1,0:T(8,128)(2,1)}), bf16[4,384,768]{2,1,0:T(8,128)(2,1)S(1)}, u32[]{:S(2)}, u32[]{:S(2)}) async-start(bf16[4,384,768]{2,1,0:T(8,128)(2,1)} %bitcast.89), calls=%async_computation | async-start | bytes 4718592 | tf_op jit(solution)/shard_map/all_to_all | solution.py:1221
  145.7 17.6 %copy-start.13 = (s32[16]{0:T(128)}, s32[16]{0:T(128)S(1)}, u32[]{:S(2)}) copy-start(s32[16]{0:T(128)S(1)} %fusion.14.ids_ref) | copy-start | bytes 196
  172.5 1.5 copy-start.6
  193.7 15.2 %all-to-all-start.1 = ((bf16[4,384,256]{2,1,0:T(8,128)(2,1)}), bf16[4,384,256]{2,1,0:T(8,128)(2,1)S(1)}, u32[]{:S(2)}, u32[]{:S(2)}) async-start(bf16[4,384,256]{2,1,0:T(8,128)(2,1)} %bitcast.85), calls=%async_computation.1 | async-start | bytes 1572864 | tf_op jit(solution)/shard_map/all_to_all | solution.py:1221
  208.9 14.2 %copy-start.8 = (bf16[4,384,256]{2,1,0:T(8,128)(2,1)}, bf16[4,384,256]{2,1,0:T(8,128)(2,1)S(1)}, u32[]{:S(2)}) copy-start(bf16[4,384,256]{2,1,0:T(8,128)(2,1)S(1)} %all-to-all-done.1) | copy-start | bytes 2359300
  208.9 16.7 %all-to-all-start.2 = ((bf16[4,384,256]{2,1,0:T(8,128)(2,1)}), bf16[4,384,256]{2,1,0:T(8,128)(2,1)S(1)}, u32[]{:S(2)}, u32[]{:S(2)}) async-start(bf16[4,384,256]{2,1,0:T(8,128)(2,1)} %bitcast.13), calls=%async_computation.2 | async-start | bytes 1572864 | tf_op jit(solution)/shard_map/all_to_all | solution.py:1226
  213.1 88.9 %reduce-scatter.3.cloned.1.call-start = ((), (), s32[]{:S(2)}) async-start(), calls=%async_computation.7 | async-start | bytes 5242880 | tf_op jit(solution)/shard_map/reduce_scatter | solution.py:1248
  225.6 14.6 %copy-start.4 = (bf16[4,384,256]{2,1,0:T(8,128)(2,1)}, bf16[4,384,256]{2,1,0:T(8,128)(2,1)S(1)}, u32[]{:S(2)}) copy-start(bf16[4,384,256]{2,1,0:T(8,128)(2,1)S(1)} %all-to-all-done.2) | copy-start | bytes 2359300
  236.0 50.4 %all-to-all-start.3 = ((bf16[4,384,768]{2,1,0:T(8,128)(2,1)}), bf16[4,384,768]{2,1,0:T(8,128)(2,1)S(1)}, u32[]{:S(2)}, u32[]{:S(2)}) async-start(bf16[4,384,768]{2,1,0:T(8,128)(2,1)} %bitcast.90), calls=%async_computation.3 | async-start | bytes 4718592 | tf_op jit(solution)/shard_map/all_to_all | solution.py:1226
  240.2 329.0 %reduce-scatter.5.cloned.1.call-start = ((), (), s32[]{:S(2)}) async-start(), calls=%async_computation.8 | async-start | bytes 7077888 | tf_op jit(solution)/shard_map/reduce_scatter | solution.py:1262
  286.4 15.7 %copy-start.1 = (bf16[4,384,768]{2,1,0:T(8,128)(2,1)}, bf16[4,384,768]{2,1,0:T(8,128)(2,1)S(1)}, u32[]{:S(2)}) copy-start(bf16[4,384,768]{2,1,0:T(8,128)(2,1)S(1)} %all-to-all-done.3) | copy-start | bytes 7077892
  302.0 1.5 copy-start
  302.0 2.1 copy-start.10
  304.1 17.5 %copy-start.12 = (f32[1,1024]{1,0:T(1,128)S(1)}, f32[1,1024]{1,0:T(1,128)}, u32[]{:S(2)}) copy-start(f32[1,1024]{1,0:T(1,128)} %get-tuple-element.103) | copy-start | bytes 12292
  304.1 17.5 %copy-start.2 = (bf16[4,384,768]{2,1,0:T(8,128)(2,1)S(1)}, bf16[4,384,768]{2,1,0:T(8,128)(2,1)}, u32[]{:S(2)}) copy-start(bf16[4,384,768]{2,1,0:T(8,128)(2,1)} %copy-done.1) | copy-start | bytes 7077892
  321.7 9.9 %copy-start.9 = (f32[192,128]{1,0:T(8,128)}, f32[192,128]{1,0:T(8,128)S(1)}, u32[]{:S(2)}) copy-start(f32[192,128]{1,0:T(8,128)S(1)} %fusion.12.vec_ref) | copy-start | bytes 294916
  529.2 9.4 %copy-start.7 = (bf16[512,2048]{1,0:T(8,128)(2,1)S(1)}, bf16[512,2048]{1,0:T(8,128)(2,1)}, u32[]{:S(2)}) copy-start(bf16[512,2048]{1,0:T(8,128)(2,1)} %get-tuple-element.107) | copy-start | bytes 6291460
  555.5 13.2 %copy-start.5 = (f32[192,2048]{1,0:T(8,128)S(1)}, f32[192,2048]{1,0:T(8,128)}, u32[]{:S(2)}) copy-start(f32[192,2048]{1,0:T(8,128)} %get-tuple-element.104) | copy-start | bytes 4718596
  555.5 13.7 %copy-start.3 = (bf16[192,2048]{1,0:T(8,128)(2,1)S(1)}, bf16[192,2048]{1,0:T(8,128)(2,1)}, u32[]{:S(2)}) copy-start(bf16[192,2048]{1,0:T(8,128)(2,1)} %param.18) | copy-start | bytes 2359300
  568.7 3.7 copy-start.11
Sparse Core Ops, SparseCore 0:
  121.6 66.2 all-gather.1
  225.8 76.1 reduce-scatter.2
  304.4 105.7 reduce-scatter.4

commit v4 on v3

--- a/solution.py
+++ b/solution.py
@@ -425,6 +425,26 @@
         cost_estimate=cost(2 * rows * width * (hc + units), 4 * rows * width + 2 * width * units),
         name="layer_out",
     )(core, mixed, w_dense, active, w_out)
+
+
+def widen(x):
+    rows, cols = x.shape
+    step = min(rows, 128 if cols > 4096 else 512)
+
+    def kernel(x_ref, o_ref):
+        o_ref[...] = x_ref[...].astype(f32)
+
+    part = pl.BlockSpec((step, cols), lambda i: (i, 0))
+    return pl.pallas_call(
+        kernel,
+        grid=(rows // step,),
+        in_specs=[part],
+        out_specs=part,
+        out_shape=jax.ShapeDtypeStruct((rows, cols), f32),
+        compiler_params=BIG,
+        cost_estimate=cost(rows * cols, 6 * rows * cols),
+        name="widen",
+    )(x)
 
 
 def grad_of_mixed(nz, core, cot, w_dense, hc):
@@ -849,29 +869,31 @@
     return begin, middle, finish, last
 
 
-def tail(nz, nchip, ncore, dwo, dwd, dwi, dwq, part_e, vectors):
+def tail(nz, nchip, ncore, dwo, dwd, dwi, vectors, normed1, grad_project, grad_hidden, tok, w_qkv, w_in, gain1, gain2):
     width = dwo.shape[1]
-    ro, rd = dwo.shape[0] // nchip, dwd.shape[0] // nchip
+    ro, rd = dwo.shape[0], dwd.shape[0] // nchip
     halves = 2 if nchip == 4 else 1
     hz = nz // halves
-    ho, hd = ro // halves, rd // halves
-    ci, cq = dwi.shape[2], dwq.shape[1] // 3
+    hd = rd // halves
+    ci, cq = dwi.shape[1], grad_project.shape[1] // 3
     wrows = width // nz
     ri = wrows // nchip
-    own = part_e.shape[0] // nz // ncore
+    rows = tok.shape[0]
+    step = rows // nz
+    own = step // ncore
     vr = vectors.shape[0]
-    dwo = dwo.reshape(nchip, ro, width)
-    dwq = dwq.reshape(nz, nchip, ri, 3 * cq)
+    chunk = 512
+    dwi = dwi.reshape(nz, nchip, ri, ci)
     dwd = dwd.reshape(nchip, rd, width)
-    part_e = part_e.reshape(nz, ncore, own, width)
 
     def kernel(
-        dwo_ref, dwd_ref, dwi_ref, dwq_ref, pe_ref, vec_ref,
+        dwo_ref, dwd_ref, dwi_ref, vec_ref, n_hbm, gp_hbm, gh_hbm, tok_hbm, wq_hbm, wi_hbm, g1_ref, g2_ref,
         go_ref, gd_ref, gi_ref, gq_ref, e_ref, vsum_ref,
-        oo, fo, so, oq, fq, sq, od, fd, sd, ti, tq, se, me, ze, v1, v2, v3,
-        ro_s, ro_r, ro_l, rq_s, rq_r, rq_l, rd_s, rd_r, rd_l, x_s, x_r, x_l, ez_s, ez_r, t_s, t_r, t_l,
+        x_ref, gp_ref, gh_ref, wq_ref, wi_ref, dwq_ref, eb,
+        oi, fi, si, oq, fq, sq, od, fd, sd, ti, tq, se, ze, cs, v0, v1, v2, v3,
+        ld, ri_s, ri_r, ri_l, rq_s, rq_r, rq_l, rd_s, rd_r, rd_l, x_s, x_r, ez_s, ez_r, t_s, t_r, t_l,
         go_s, go_r, gd_s, gd_r, gi_s, gi_r, gq_s, gq_r, own_l,
-        v_s, v_r, v_l,
+        v_s, v_r,
     ):
         z = lax.axis_index("seq")
         chip = lax.axis_index("chip")
@@ -884,6 +906,14 @@
         def chip_at(d):
             return lax.rem(chip + d, nchip)
 
+        loads = [
+            pltpu.make_async_copy(a, b, ld.at[i])
+            for i, (a, b) in enumerate(
+                ((n_hbm, x_ref), (gp_hbm, gp_ref), (gh_hbm, gh_ref), (wi_hbm, wi_ref), (wq_hbm, wq_ref))
+            )
+        ]
+        for copy in loads:
+            copy.start()
         greet(
             [{"seq": z_at(d)} for d in range(1, nz)]
             + [{"chip": chip_at(d)} for d in range(1, nchip)]
@@ -906,87 +936,121 @@
         def turned_at(kind, part, turned, source):
             return remote(part, turned.at[source], t_s.at[kind, 0], t_r.at[kind, source], sibling)
 
+        sum_i = scatter_plane(
+            nchip, chip, lambda c, h: dwi_ref.at[pl.ds(h * hz, hz), c], oi, fi, si, ri_s, ri_r, ri_l
+        )
         sum_q = scatter_plane(
-            nchip, chip, lambda c, h: dwq_ref.at[pl.ds(h * hz, hz), c], oq, fq, sq, rq_s, rq_r, rq_l
-        )
-        sum_o = scatter_plane(
-            nchip, chip, lambda c, h: dwo_ref.at[c, pl.ds(h * ho, ho)], oo, fo, so, ro_s, ro_r, ro_l
+            nchip, chip, lambda c, h: dwq_ref.at[pl.ds(h * hz, hz), pl.ds(c * ri, ri)], oq, fq, sq,
+            rq_s, rq_r, rq_l,
         )
         sum_d = scatter_plane(
             nchip, chip, lambda c, h: dwd_ref.at[c, pl.ds(h * hd, hd)], od, fd, sd, rd_s, rd_r, rd_l
         )
-        turn_i = turn(0, lambda to: dwi_ref.at[to], ti)
+        sum_i[0]()
+
+        loads[0].wait()
+        loads[1].wait()
+        for b in range(nz):
+            dwq_ref[b] = lax.dot_general(
+                x_ref[:, b * wrows : (b + 1) * wrows], gp_ref[...], TN, preferred_element_type=f32
+            ).astype(bf16)
+        load_tok = pltpu.make_async_copy(tok_hbm, x_ref, ld.at[5])
+        load_tok.start()
+        sum_i[1]()
         sum_q[0]()
-
-        exchanged = [
-            remote(pe_ref.at[:, 1 - core], se, x_s.at[0], x_r.at[0], sibling),
-        ]
-        keep = [
-            pltpu.make_async_copy(pe_ref.at[:, core], me, x_l.at[0]),
-        ]
-        for copy in exchanged + keep:
+        sum_d[0]()
+
+        for copy in loads[2:] + [load_tok]:
+            copy.wait()
+        cs[...] = jnp.zeros_like(cs)
+
+        def norm_back(b):
+            at = pl.ds(b * step, step)
+            x = x_ref[at, :].astype(f32)
+            mean = jnp.mean(x, axis=-1, keepdims=True)
+            x = x - mean
+            inv = lax.rsqrt(jnp.mean(x * x, axis=-1, keepdims=True) + EPSILON)
+
+            @pl.loop(0, width // chunk)
+            def _(c):
+                cols = pl.ds(pl.multiple_of(c * chunk, chunk), chunk)
+                xhat = (x_ref[at, cols].astype(f32) - mean) * inv
+                gn = lax.dot_general(
+                    gp_ref[at, :], wq_ref[cols, :], NT, preferred_element_type=f32
+                )
+                cs[0:1, cols] += jnp.sum(gn * xhat, axis=0, keepdims=True)
+                cs[1:2, cols] += jnp.sum(gn, axis=0, keepdims=True)
+                e = gn * g1_ref[:, cols]
+                gn = lax.dot_general(
+                    gh_ref[at, :], wi_ref[cols, :], NT, preferred_element_type=f32
+                )
+                cs[2:3, cols] += jnp.sum(gn * xhat, axis=0, keepdims=True)
+                cs[3:4, cols] += jnp.sum(gn, axis=0, keepdims=True)
+                e = (e + gn * g2_ref[:, cols]).astype(bf16)
+                for k in range(ncore):
+                    eb[b, k, :, cols] = e[k * own : (k + 1) * own]
+
+            copy = remote(eb.at[b, 1 - core], se.at[b], x_s.at[b], x_r.at[b], sibling)
             copy.start()
-
-        v_own = pltpu.make_async_copy(vec_ref, v1.at[chip], v_l.at[0])
-        v_own.start()
+            return copy
+
+        exchanged = [norm_back(b) for b in range(nz)]
+        sum_i[2]()
+        turn_i = turn(0, lambda to: oi.at[to // hz, 0, lax.rem(to, hz)], ti)
+        sum_q[1]()
+
+        v0[...] = vec_ref[...]
+        lanes = width // 128
+        for k in range(4):
+            for j in range(lanes):
+                v0[k * lanes + j : k * lanes + j + 1, :] = cs[k : k + 1, j * 128 : (j + 1) * 128]
         v_chips = [
-            remote(vec_ref, v1.at[chip], v_s.at[d], v_r.at[chip], {"chip": chip_at(d)})
+            remote(v0, v1.at[chip], v_s.at[d], v_r.at[chip], {"chip": chip_at(d)})
             for d in range(1, nchip)
         ]
         for copy in v_chips:
             copy.start()
-
-        def pair_sum(which, mine, theirs):
-            exchanged[which].wait_recv()
-            keep[which].wait()
-
-            @pl.loop(0, nz)
-            def _(b):
-                @pl.loop(0, own // 16)
-                def _(i):
-                    at = pl.ds(pl.multiple_of(i * 16, 16), 16)
-                    mine[b, at, :] = (
-                        mine[b, at, :].astype(f32) + theirs[b, at, :].astype(f32)
-                    ).astype(bf16)
-
-        def z_sends(which, mine, landing):
-            return [
-                remote(
-                    mine.at[z_at(d)], landing.at[d], ez_s.at[which, d], ez_r.at[which, d],
-                    {"seq": z_at(d)},
-                )
-                for d in range(1, nz)
-            ]
-
-        def z_sum(copies, mine, landing, out):
-            for copy in copies:
-                copy.wait_recv()
+        v1[chip] = v0[...]
+
+        go_at = lambda c, k: go_ref.at[pl.ds(k * (ro * nchip) + c * ro, ro), :]
+        gd_at = lambda c, k, h: gd_ref.at[pl.ds(k * (rd * nchip) + c * rd + h * hd, hd), :]
+        gi_at = lambda c, k, s: gi_ref.at[
+            pl.ds(c * ri, ri), pl.ds((s * ncore + k) * ci, ci)
+        ]
+        gq_at = lambda c, k, s, g: gq_ref.at[
+            pl.ds(c * ri, ri), pl.ds(g * nz * ncore * cq + (s * ncore + k) * cq, cq)
+        ]
+        group = functools.partial(gather_plane, nchip, chip, core)
+        rows_o = group(dwo_ref, go_at, go_s, go_r, own_l.at[nz])
+        rows_o[0]()
+
+        for b in range(nz):
+            exchanged[b].wait_recv()
 
             @pl.loop(0, own // 16)
             def _(i):
                 at = pl.ds(pl.multiple_of(i * 16, 16), 16)
-                acc = mine[z, at, :].astype(f32)
-                for d in range(1, nz):
-                    acc = acc + landing[d, at, :].astype(f32)
-                out[at, :] = acc
-
-        pair_sum(0, me, se)
-        sum_q[1]()
-        sum_o[0]()
-        sum_d[0]()
-
-        go_at = lambda c, k, h: go_ref.at[pl.ds(k * (ro * nchip) + c * ro + h * ho, ho), :]
-        gd_at = lambda c, k, h: gd_ref.at[pl.ds(k * (rd * nchip) + c * rd + h * hd, hd), :]
-        gi_at = lambda c, k, s: gi_ref.at[
-            pl.ds(c * ri, ri), pl.ds((s * ncore + k) * ci, ci)
-        ]
-        gq_at = lambda c, k, s, g: gq_ref.at[
-            pl.ds(c * ri, ri), pl.ds(g * nz * ncore * cq + (s * ncore + k) * cq, cq)
-        ]
-        group = functools.partial(gather_plane, nchip, chip, core)
+                eb[b, core, at, :] = (
+                    eb[b, core, at, :].astype(f32) + se[b, at, :].astype(f32)
+                ).astype(bf16)
+
+        sum_q[2]()
+        turn_q = turn(1, lambda to: oq.at[to // hz, 0, lax.rem(to, hz)], tq)
+        sum_d[1]()
+
+        for d in range(1, nchip):
+            other = chip_at(d)
+            remote(v0, v1.at[other], v_s.at[d], v_r.at[other], sibling).wait_recv()
+        total = v1[0]
+        for d in range(1, nchip):
+            total = total + v1[d]
+        v2[core] = total
+        v_side = remote(v2.at[core], v2.at[core], v_s.at[nchip], v_r.at[nchip], sibling)
+        v_side.start()
+
         groups = []
         for dz in range(1, nz):
-            turned_at(0, dwi_ref.at[0], ti, z_at(dz)).wait_recv()
+            turned_at(0, oi.at[0, 0, 0], ti, z_at(dz)).wait_recv()
         turn_i[-1].wait()
         for source in range(nz):
             groups.append(
@@ -996,22 +1060,14 @@
                 )
             )
             groups[-1][0]()
-        sent_e = z_sends(0, me, ze)
+        sent_e = [
+            remote(
+                eb.at[z_at(d), core], ze.at[d], ez_s.at[d], ez_r.at[d], {"seq": z_at(d)}
+            )
+            for d in range(1, nz)
+        ]
         for copy in sent_e:
             copy.start()
-        sum_q[2]()
-        turn_q = turn(1, lambda to: oq.at[to // hz, 0, lax.rem(to, hz)], tq)
-
-        v_own.wait()
-        for d in range(1, nchip):
-            other = chip_at(d)
-            remote(vec_ref, v1.at[other], v_s.at[d], v_r.at[other], sibling).wait_recv()
-        total = v1[0]
-        for d in range(1, nchip):
-            total = total + v1[d]
-        v2[core] = total
-        v_side = remote(v2.at[core], v2.at[core], v_s.at[nchip], v_r.at[nchip], sibling)
-        v_side.start()
 
         v_side.wait_recv()
         vz = v2[0]
@@ -1024,24 +1080,16 @@
         ]
         for copy in v_zs:
             copy.start()
-
-        sum_o[1]()
-        sum_d[1]()
+        sum_d[2]()
+        rows_d = [
+            group(od.at[h, 0], functools.partial(gd_at, h=h), gd_s.at[h], gd_r.at[h], own_l.at[nz + 1 + h])
+            for h in range(halves)
+        ]
+        for first, onward, pass_on, last in rows_d:
+            first()
+        rows_o[1]()
         for first, onward, pass_on, last in groups:
             onward()
-        sum_o[2]()
-        sum_d[2]()
-        for h in range(halves):
-            for at, (buf, place, sends, recvs) in enumerate(
-                ((oo, go_at, go_s, go_r), (od, gd_at, gd_s, gd_r))
-            ):
-                groups.append(
-                    group(
-                        buf.at[h, 0], functools.partial(place, h=h), sends.at[h], recvs.at[h],
-                        own_l.at[nz + 2 * at + h],
-                    )
-                )
-                groups[-1][0]()
 
         for dz in range(1, nz):
             turned_at(1, oq.at[0, 0, 0], tq, z_at(dz)).wait_recv()
@@ -1058,13 +1106,14 @@
                 )
         for first, onward, pass_on, last in later:
             first()
-        for first, onward, pass_on, last in groups[nz:]:
+        rows_o[2]()
+        for first, onward, pass_on, last in rows_d:
             onward()
-        for first, onward, pass_on, last in groups[:nz]:
+        for first, onward, pass_on, last in groups:
             pass_on()
         for first, onward, pass_on, last in later:
             onward()
-        for first, onward, pass_on, last in groups[nz:]:
+        for first, onward, pass_on, last in rows_d:
             pass_on()
 
         for d in range(1, nz):
@@ -1075,13 +1124,23 @@
             total = total + v3[d]
         vsum_ref[...] = total
 
-        z_sum(sent_e, me, ze, e_ref)
+        for copy in sent_e:
+            copy.wait_recv()
+
+        @pl.loop(0, own // 16)
+        def _(i):
+            at = pl.ds(pl.multiple_of(i * 16, 16), 16)
+            acc = eb[z, core, at, :].astype(f32)
+            for d in range(1, nz):
+                acc = acc + ze[d, at, :].astype(f32)
+            e_ref[at, :] = acc
+
         for first, onward, pass_on, last in later:
             pass_on()
 
-        for first, onward, pass_on, last in groups + later:
+        for first, onward, pass_on, last in [rows_o] + rows_d + groups + later:
             last()
-        for begin, middle, finish, last in (sum_o, sum_q, sum_d):
+        for begin, middle, finish, last in (sum_i, sum_q, sum_d):
             last()
         for copy in exchanged + sent_e + v_chips + v_zs + [v_side]:
             copy.wait_send()
@@ -1099,51 +1158,64 @@
         jax.ShapeDtypeStruct((own, width), f32),
         jax.ShapeDtypeStruct((vr, 128), f32),
     ]
-    ranked = (nz, own, width)
     slots = max(3 * nchip, 12)
     pair = 2 if nchip == 4 else 1
     nfirst = 2 if nchip == 4 else nchip
+
+    def three(*shape):
+        return [
+            pltpu.VMEM((halves, pair) + shape, bf16),
+            pltpu.VMEM((halves, nfirst) + shape, bf16),
+            pltpu.VMEM((halves,) + shape, bf16),
+        ]
+
     return pl.pallas_call(
         kernel,
-        in_specs=[anywhere] * 5 + [vmem],
+        in_specs=[anywhere] * 3 + [vmem] + [anywhere] * 6 + [vmem] * 2,
         out_specs=[anywhere] * 4 + [vmem] * 2,
         out_shape=out_shape,
         scratch_shapes=[
-            pltpu.VMEM((halves, pair, ho, width), bf16),
-            pltpu.VMEM((halves, nfirst, ho, width), bf16),
-            pltpu.VMEM((halves, ho, width), bf16),
-            pltpu.VMEM((halves, pair, hz, ri, 3 * cq), bf16),
-            pltpu.VMEM((halves, nfirst, hz, ri, 3 * cq), bf16),
-            pltpu.VMEM((halves, hz, ri, 3 * cq), bf16),
-            pltpu.VMEM((halves, pair, hd, width), bf16),
-            pltpu.VMEM((halves, nfirst, hd, width), bf16),
-            pltpu.VMEM((halves, hd, width), bf16),
+            pltpu.VMEM((rows, width), bf16),
+            pltpu.VMEM(grad_project.shape, bf16),
+            pltpu.VMEM(grad_hidden.shape, bf16),
+            pltpu.VMEM(w_qkv.shape, bf16),
+            pltpu.VMEM(w_in.shape, bf16),
+            pltpu.VMEM((nz, wrows, 3 * cq), bf16),
+            pltpu.VMEM((nz, ncore, own, width), bf16),
+        ]
+        + three(hz, ri, ci)
+        + three(hz, ri, 3 * cq)
+        + three(hd, width)
+        + [
             pltpu.VMEM((nz, ri, ci), bf16),
             pltpu.VMEM((nz, ri, 3 * cq), bf16),
-            pltpu.VMEM(ranked, bf16),
-            pltpu.VMEM(ranked, bf16),
-            pltpu.VMEM(ranked, bf16),
+            pltpu.VMEM((nz, own, width), bf16),
+            pltpu.VMEM((nz, own, width), bf16),
+            pltpu.VMEM((8, width), f32),
+            pltpu.VMEM((vr, 128), f32),
             pltpu.VMEM((nchip, vr, 128), f32),
             pltpu.VMEM((ncore, vr, 128), f32),
             pltpu.VMEM((nz, vr, 128), f32),
+            dma((6,)),
             dma((halves, nchip)), dma((halves, nchip)), dma((halves, 2)),
             dma((halves, nchip)), dma((halves, nchip)), dma((halves, 2)),
             dma((halves, nchip)), dma((halves, nchip)), dma((halves, 2)),
-            dma((2,)), dma((2,)), dma((2,)),
-            dma((2, nz)), dma((2, nz)),
+            dma((nz,)), dma((nz,)),
+            dma((nz,)), dma((nz,)),
             dma((2, nz)), dma((2, nz)), dma((2,)),
-            dma((halves, slots)), dma((halves, slots)),
+            dma((slots,)), dma((slots,)),
             dma((halves, slots)), dma((halves, slots)),
             dma((nz, slots)), dma((nz, slots)),
             dma((nz, 3, slots)), dma((nz, 3, slots)),
             dma((4 + 4 * nz,)),
-            dma((nchip + nz,)), dma((nchip + nz + 1,)), dma((1,)),
+            dma((nchip + nz,)), dma((nchip + nz + 1,)),
         ],
         compiler_params=pltpu.CompilerParams(
-            collective_id=2, has_side_effects=True, vmem_limit_bytes=60 * 2**20
+            collective_id=2, has_side_effects=True, vmem_limit_bytes=62 * 2**20
         ),
+        cost_estimate=cost(4 * rows * width * (3 * cq + ci), 20 * rows * width),
         name="tail",
-    )(dwo, dwd, dwi, dwq, part_e, vectors)
+    )(dwo, dwd, dwi, vectors, normed1, grad_project, grad_hidden, tok, w_qkv, w_in, gain1, gain2)
 
 
 def on_device(
@@ -1240,42 +1312,37 @@
     grad_mixed = grad_of_mixed(nz, core_at, cot, w_dense, hc)
     grad_mixed, cot = lax.optimization_barrier((grad_mixed, cot))
     g = heads_of(grad_mixed)
+    dw_out = lax.dot_general(active, cot, TN, preferred_element_type=f32).astype(bf16)
+    dw_out, cot = lax.optimization_barrier((dw_out, cot))
+    s_out = lax.psum_scatter(dw_out, "chip", scatter_dimension=0, tiled=True)
     grad_hidden, sum_bin = grad_of_hidden(nz, core_at, cot, w_out, slope)
-    dw_in = lax.dot_general(normed2, grad_hidden, TN, preferred_element_type=f32).astype(bf16)
-    dw_in = dw_in.reshape(nz, nchip, wrows // nchip, ffr).transpose(1, 0, 2, 3)
-    dw_in = dw_in.reshape(width, ffr)
-    g, dw_in, mixed = lax.optimization_barrier((g, dw_in, mixed))
-    s_in = lax.psum_scatter(dw_in, "chip", scatter_dimension=0, tiled=True)
-    s_in = s_in.reshape(nz, wrows // nchip, ffr)
+    g, grad_hidden, mixed = lax.optimization_barrier((g, grad_hidden, mixed))
     dqkv = attention_backward(ids_seq, order, qkv, g, lse, table, tile)
     dqkv, mixed, active, cot, grad_hidden = lax.optimization_barrier(
         (dqkv, mixed, active, cot, grad_hidden)
     )
     grad_project = heads_back(dqkv)
     part_out = layer_out(nz, core_at, mixed, w_dense, active, w_out)
-    dw_out = lax.dot_general(active, cot, TN, preferred_element_type=f32).astype(bf16)
+    part_out, cot, mixed, grad_hidden = lax.optimization_barrier((part_out, cot, mixed, grad_hidden))
+    summed_out = lax.psum_scatter(part_out, TP, scatter_dimension=0, tiled=True).astype(f32)
+    dw_in = lax.dot_general(normed2, grad_hidden, TN, preferred_element_type=f32).astype(bf16)
     dw_dense = lax.dot_general(mixed, cot, TN, preferred_element_type=f32).astype(bf16)
-    e2, sums2 = norm_back(nz, grad_hidden, w_in_c, tok, gain2, None, False)
-    grad_project, part_out, dw_out, dw_dense, e2, s_in = lax.optimization_barrier(
-        (grad_project, part_out, dw_out, dw_dense, e2, s_in)
-    )
-    summed_out = lax.psum_scatter(part_out, TP, scatter_dimension=0, tiled=True).astype(f32)
-    dw_qkv = lax.dot_general(normed1, grad_project, TN, preferred_element_type=f32).astype(bf16)
-    e_part, sums1, sum_bqkv = norm_back(nz, grad_project, w_qkv_c, tok, gain1, e2, True)
+    grad_project, dw_in, dw_dense = lax.optimization_barrier((grad_project, dw_in, dw_dense))
+    sum_bqkv = jnp.sum(grad_project.astype(f32), axis=0)
 
     here = jnp.arange(ranks, dtype=jnp.int32) == rank
     mine_bqkv = jnp.where(here[None, :, None], sum_bqkv.reshape(3, 1, hc), 0.0)
     mine_bin = jnp.where(here[:, None], sum_bin.reshape(1, ffr), 0.0)
     vectors = [
-        sums1.reshape(-1),
-        sums2.reshape(-1),
+        jnp.zeros(4 * width, f32),
         mine_bqkv.reshape(-1),
         jnp.sum(cotangent.astype(f32), axis=0),
         mine_bin.reshape(-1),
     ]
     vectors = jnp.concatenate([v.reshape(-1, 128) for v in vectors])
     g_wout, g_wdense, g_win, g_wqkv, e, sums = tail(
-        nz, nchip, ncore, dw_out, dw_dense, s_in, dw_qkv, e_part, vectors
+        nz, nchip, ncore, s_out, dw_dense, dw_in, vectors, normed1, grad_project, grad_hidden, tok,
+        w_qkv_c, w_in_c, gain1, gain2
     )
     sums = sums.reshape(-1)
     at = 0
@@ -1293,7 +1360,7 @@
         - xhat_own * jnp.mean(e * xhat_own, axis=-1, keepdims=True)
     ) * inv_own
     grad_tokens = (cotangent.astype(f32) + terms).astype(bf16)
-    g_wout, g_wdense, g_win, g_wqkv = [g.astype(f32) for g in (g_wout, g_wdense, g_win, g_wqkv)]
+    g_wout, g_wdense, g_win, g_wqkv = [widen(g) for g in (g_wout, g_wdense, g_win, g_wqkv)]
     return (
         output,
         grad_tokens,

time: 587 us -> 549 us (0.935)
  other arithmetic: 44.5 us -> 10.4 us
  blocking collectives: 0 us -> 23.5 us
  Pallas kernels: 421 us -> 407 us
  matrix products: 36.7 us -> 27.1 us
    convert_element_type x4 -> x0, other arithmetic: 35.5 us -> none  [on_device(): g.astype(f32)]
    all_to_all x0 -> x1, blocking collectives: none -> 23.5 us  [heads_back(): x = lax.all_to_all(x, 'chip', 0, 0, tiled=True).reshape(rows, g * HD)]
    reduce_scatter x1, waiting for transfers between devices: 15.7 us -> 0.01 us  [on_device(): s_out = lax.psum_scatter(dw_out, 'chip', scatter_dimension=0, tiled=True)]
    pallas_call x3 -> x5, Pallas kernels: 230 us -> 215 us  [the longest x1 185 us: tail(): pl.pallas_call(kernel, in_specs=[anywhere] * 3 + [vmem] + [anywhere] * 6...]
    all_to_all x2 -> x1, waiting for transfers between devices: 0.01 us -> 11 us  [heads_back(): x = lax.all_to_all(x, 'chip', 0, 0, tiled=True).reshape(rows, g * HD)]
    dot_general x1 -> x0, matrix products: 9.88 us -> none  [on_device(): lax.dot_general(normed1, grad_project, TN, preferred_element_type=f32)]
    all_to_all x2, waiting for transfers between devices: 9.22 us -> 15.3 us  [heads_of(): return lax.all_to_all(x, 'chip', 0, 0, tiled=True).reshape(length, g * HD)]
  transfers between devices with their start and end apart: 7 -> 6, of which waited for: 3 -> 4; matrix products, arithmetic and copies ran while one was open for 15% -> 6% of each run, Pallas kernels for 52% -> 53%
where the time goes in v4:
time: 549 us; the launch traced here: 544 us
  Pallas kernels  407 us (74%)
  waiting for transfers between devices  34.2 us (6%)
  matrix products  27.1 us (5%)
  blocking collectives  23.5 us (4%)
  local copies, waits for them, and re-layouts  14.4 us (3%)
  between operations  14.2 us (3%)
  starting transfers between devices  13 us (2%)
  other arithmetic  10.4 us (2%)
    pallas_call x1, Pallas kernels, tail(): pl.pallas_call(kernel, in_specs=[anywhere] * 3 + [vmem] + [anywhere] * 6...  185 us
    pallas_call x1, Pallas kernels, front(): pl.pallas_call(kernel, in_specs=[anywhere] * 4, out_specs=[anywhere] * 4,...  112 us
    pallas_call x4, Pallas kernels, widen(): pl.pallas_call(kernel, grid=(rows // step,), in_specs=[part], out_specs=p...  30.9 us
    all_to_all x1, blocking collectives, heads_back(): x = lax.all_to_all(x, 'chip', 0, 0, tiled=True).reshape(rows, g * HD)  23.5 us
    pallas_call x1, Pallas kernels, feed_forward(): pl.pallas_call(kernel, grid=(nz,), in_specs=[part(width), whole((width, c...  16.4 us
    all_to_all x2, waiting for transfers between devices, heads_of(): return lax.all_to_all(x, 'chip', 0, 0, tiled=True).reshape(length, g * HD)  15.3 us
    pallas_call x1, Pallas kernels, projections(): pl.pallas_call(kernel, grid_spec=pltpu.PrefetchScalarGridSpec(num_scalar_...  15.2 us
    pallas_call x1, Pallas kernels, layer_out(): pl.pallas_call(kernel, grid_spec=pltpu.PrefetchScalarGridSpec(num_scalar_...  12.9 us
  transfers between devices with their start and end apart: 6, of which 4 were waited for; matrix products, arithmetic and copies ran while one was open for 6% of the time, Pallas kernels for 53%

profile of v4, /device:TPU:0, one launch (start us, length us, event | category | flops | bytes accessed | tf_op | source)
XLA Modules:
  0.0 543.7 jit_solution(16933792840933329420)
XLA Ops:
  7.2 0.7 convert_bitcast_fusion.7
  7.9 1.4 fusion.12.sm_ref
  9.3 112.1 %front.1 = (bf16[4,2,192,2048]{3,2,1,0:T(8,128)(2,1)}, bf16[2048,1024]{1,0:T(8,128)(2,1)}, bf16[2048,768]{1,0:T(8,128)(2,1)}, bf16[4,64,128]{2,1,0:T(8,128)(2,1)}) custom-call(bf16[192,2048]{1,0:T(8,128)(2,1)} %tok_ref.1, bf16[512,8192]{1,0:T(8,128)(2,1)} %wi_ref.1, bf16[512,6144]{1,0:T(8,128)(2,1)} %wq_ref.1, bf16[64,128]{1,0:T(8,128)(2,1)} %fusion.12.sm_ref), custom_call_target="tpu_custom_call" | custom-call | tf_op jit(solution)/shard_map/front/pallas_call | solution.py:262
  121.5 0.9 copy.40
  122.4 0.6 reshape.165.ids_ref
  123.1 0.6 copy.33
  123.7 0.6 copy.32
  124.3 0.6 constant_dynamic-slice_fusion.1
  124.9 15.2 %projections.1 = (bf16[1536,2048]{1,0:T(8,128)(2,1)}, bf16[1536,768]{1,0:T(8,128)(2,1)}) custom-call(s32[16]{0:T(128)} %reshape.165.ids_ref, s32[1]{0:T(128)} %constant.63.clone.1.place_ref, bf16[1536,2048]{1,0:T(8,128)(2,1)} %bitcast.89, bf16[2048,768]{1,0:T(8,128)(2,1)} %get-tuple-element.63.w_ref.wq_hbm, f32[1,768]{1,0:T(1,128)} %bitcast.88, ...), custom_call_target="tpu_custom_call" | custom-call | flops 4831838208 | bytes 15728640 | tf_op jit(solution)/shard_map/projections/pallas_call | solution.py:340
  140.1 3.8 all-to-all-start
  144.2 0.6 copy.36
  144.8 0.6 copy.35
  145.5 0.6 constant_dynamic-slice_fusion.b_ref
  146.1 0.6 select_reduce_fusion.order_ref
  146.7 16.4 %feed_forward.1 = (bf16[1536,2048]{1,0:T(8,128)(2,1)}, bf16[1536,1024]{1,0:T(8,128)(2,1)}, bf16[1536,1024]{1,0:T(8,128)(2,1)}) custom-call(bf16[1536,2048]{1,0:T(8,128)(2,1)} %bitcast.90, bf16[2048,1024]{1,0:T(8,128)(2,1)} %get-tuple-element.65.w_ref.wi_hbm, f32[1,1024]{1,0:T(1,128)} %constant_dynamic-slice_fusion.b_ref, f32[1,2048]{1,0:T(1,128)} %bitcast.80, ...), custom_call_target="tpu_custom_call" | custom-call | flops 6442450944 | bytes 16777216 | tf_op jit(solution)/shard_map/feed_forward/pallas_call | solution.py:385
  163.1 8.8 %all-to-all-done = bf16[4,384,768]{2,1,0:T(8,128)(2,1)S(1)} async-done(((bf16[4,384,768]{2,1,0:T(8,128)(2,1)}), bf16[4,384,768]{2,1,0:T(8,128)(2,1)S(1)}, u32[]{:S(2)}, u32[]{:S(2)}) %all-to-all-start) | async-done | bytes 2359328 | tf_op jit(solution)/shard_map/all_to_all | solution.py:1293
  171.9 1.4 copy-done.5
  173.3 6.7 %attention_forward.1 = (bf16[1536,256]{1,0:T(8,128)(2,1)}, f32[1536,1]{1,0:T(8,128)}) custom-call(s32[16]{0:T(128)} %copy-done.10, s32[16]{0:T(128)} %select_reduce_fusion.order_ref, bf16[1536,768]{1,0:T(8,128)(2,1)} %bitcast.63), custom_call_target="tpu_custom_call" | custom-call | flops 1389153536 | bytes 3145728 | tf_op jit(solution)/shard_map/attention_forward/pallas_call | solution.py:599
  180.0 7.9 %all-gather.2.cloned.1.call-done.c_ref = bf16[1536,2048]{1,0:T(8,128)(2,1)} async-done(((bf16[192,2048]{1,0:T(8,128)(2,1)}), bf16[1536,2048]{1,0:T(8,128)(2,1)}) %all-gather.2.cloned.1.call-update) | async-done | bytes 6291472 | tf_op jit(solution)/shard_map/all_gather | solution.py:1278
  187.9 6.2 %grad_of_mixed.1 = bf16[1536,256]{1,0:T(8,128)(2,1)} custom-call(s32[1]{0:T(128)} %bitcast.core_ref, bf16[1536,2048]{1,0:T(8,128)(2,1)} %all-gather.2.cloned.1.call-done.c_ref, bf16[512,2048]{1,0:T(8,128)(2,1)} %wd_ref.1), custom_call_target="tpu_custom_call" | custom-call | flops 1610612736 | bytes 6291456 | tf_op jit(solution)/shard_map/grad_of_mixed/pallas_call | solution.py:459
  194.2 10.2 %convolution_convert_fusion.1 = bf16[1024,2048]{1,0:T(8,128)(2,1)} fusion(bf16[1536,1024]{1,0:T(8,128)(2,1)} %get-tuple-element.85.a_ref, bf16[1536,2048]{1,0:T(8,128)(2,1)S(1)} %copy-done), kind=kOutput, calls=%fused_computation.2 | convolution fusion | flops 6444548096 | bytes 13631488 | tf_op jit(solution)/shard_map/dot_general | solution.py:1315
  204.4 1.1 copy-done.7
  205.5 23.5 %all_to_all.20 = bf16[4,384,256]{2,1,0:T(8,128)(2,1)} all-to-all(bf16[4,384,256]{2,1,0:T(8,128)(2,1)S(1)} %bitcast.68), channel_id=1, replica_groups=mesh['seq'=4,'chip'=4,'core'=2] {'chip'}, dimensions={0} | all-to-all | bytes 1572864 | tf_op jit(solution)/shard_map/all_to_all | solution.py:1298
  228.9 3.5 all-to-all-start.1
  232.5 0.6 reduce-scatter.3.cloned.1.call-start
  233.0 11.6 %grad_of_hidden.1 = (bf16[1536,1024]{1,0:T(8,128)(2,1)}, f32[1,1024]{1,0:T(1,128)}) custom-call(s32[1]{0:T(128)} %bitcast.core_ref, bf16[1536,2048]{1,0:T(8,128)(2,1)} %all-gather.2.cloned.1.call-done.c_ref, bf16[2048,2048]{1,0:T(8,128)(2,1)} %wo_ref.1, bf16[1536,1024]{1,0:T(8,128)(2,1)} %get-tuple-element.77.d_ref), custom_call_target="tpu_custom_call" | custom-call | flops 6442450944 | bytes 10485760 | tf_op jit(solution)/shard_map/grad_of_hidden/pallas_call | solution.py:493
  244.6 6.4 %all-to-all-done.1 = bf16[4,384,256]{2,1,0:T(8,128)(2,1)S(1)} async-done(((bf16[4,384,256]{2,1,0:T(8,128)(2,1)}), bf16[4,384,256]{2,1,0:T(8,128)(2,1)S(1)}, u32[]{:S(2)}, u32[]{:S(2)}) %all-to-all-start.1) | async-done | bytes 786464 | tf_op jit(solution)/shard_map/all_to_all | solution.py:1293
  251.0 0.9 copy-done.6
  251.9 10.2 %attention_backward.1 = bf16[1536,768]{1,0:T(8,128)(2,1)} custom-call(s32[16]{0:T(128)} %copy-done.10, s32[16]{0:T(128)} %select_reduce_fusion.order_ref, bf16[1536,768]{1,0:T(8,128)(2,1)} %bitcast.64, bf16[1536,256]{1,0:T(8,128)(2,1)} %bitcast.67, f32[1536,1]{1,0:T(8,128)} %get-tuple-element.81.lse_ref, f32[3,1536,128]{2,1,0:T(8,128)} %constant.84.clone.t_ref), custom_call_target="tpu_custom_call" | custom-call | flops 3623878656 | bytes 7864320 | tf_op jit(solution)/shard_map/attention_backward/pallas_call | solution.py:663
  262.1 12.9 %layer_out.1 = bf16[1536,2048]{1,0:T(8,128)(2,1)} custom-call(s32[1]{0:T(128)} %bitcast.core_ref, bf16[1536,256]{1,0:T(8,128)(2,1)} %bitcast.60, bf16[512,2048]{1,0:T(8,128)(2,1)} %wd_ref.1, bf16[1536,1024]{1,0:T(8,128)(2,1)} %get-tuple-element.85.a_ref, bf16[2048,2048]{1,0:T(8,128)(2,1)} %wo_ref.1), custom_call_target="tpu_custom_call" | custom-call | flops 8053063680 | bytes 16777216 | tf_op jit(solution)/shard_map/layer_out/pallas_call | solution.py:415
  275.2 0.9 copy-done.1
  277.0 4.9 all-to-all-start.3
  281.9 5.8 %convolution_convert_fusion.2 = bf16[256,2048]{1,0:T(8,128)(2,1)} fusion(bf16[1536,256]{1,0:T(8,128)(2,1)S(1)} %bitcast.61, bf16[1536,2048]{1,0:T(8,128)(2,1)} %all-gather.2.cloned.1.call-done.c_ref), kind=kOutput, calls=%fused_computation.3 | convolution fusion | flops 1611137024 | bytes 8126464 | tf_op jit(solution)/shard_map/dot_general | solution.py:1329
  287.6 11.2 %convolution_convert_fusion = bf16[2048,1024]{1,0:T(8,128)(2,1)} fusion(bf16[1536,2048]{1,0:T(8,128)(2,1)} %get-tuple-element.91, bf16[1536,1024]{1,0:T(8,128)(2,1)S(1)} %copy-done.11), kind=kOutput, calls=%fused_computation.1 | convolution fusion | flops 6444548096 | bytes 13631488 | tf_op jit(solution)/shard_map/dot_general | solution.py:1328
  298.8 11.0 %all-to-all-done.3 = bf16[4,384,768]{2,1,0:T(8,128)(2,1)} async-done(((bf16[4,384,768]{2,1,0:T(8,128)(2,1)}), bf16[4,384,768]{2,1,0:T(8,128)(2,1)}, u32[]{:S(2)}, u32[]{:S(2)}) %all-to-all-start.3) | async-done | bytes 2359328 | tf_op jit(solution)/shard_map/all_to_all | solution.py:1298
  309.8 2.1 convert_reduce_fusion
  312.0 0.6 pad_maximum_fusion.vec_ref
  312.7 184.6 %tail.1 = (bf16[2048,2048]{1,0:T(8,128)(2,1)}, bf16[512,2048]{1,0:T(8,128)(2,1)}, bf16[512,8192]{1,0:T(8,128)(2,1)}, bf16[512,6144]{1,0:T(8,128)(2,1)}, f32[192,2048]{1,0:T(8,128)}, /*index=5*/f32[192,128]{1,0:T(8,128)}) custom-call(bf16[256,2048]{1,0:T(8,128)(2,1)} %reduce-scatter.5.cloned.1.call-done.dwo_ref, bf16[4,64,2048]{2,1,0:T(8,128)(2,1)} %bitcast.66, ...), custom_call_target="tpu_custom_call" | custom-call | flops 22548578304 | bytes 62914560 | tf_op jit(solution)/shard_map/tail/pallas_call | solution.py:1172
  497.3 1.4 dynamic_slice.43
  498.7 1.3 dynamic_slice.45
  500.0 1.4 fusion.15
  501.3 3.9 widen.5
  505.2 7.8 %widen.4 = f32[512,6144]{1,0:T(8,128)} custom-call(bf16[512,6144]{1,0:T(8,128)(2,1)} %get-tuple-element.102.x_ref), custom_call_target="tpu_custom_call" | custom-call | flops 3145728 | bytes 18874368 | tf_op jit(solution)/shard_map/widen/pallas_call | solution.py:438
  513.0 9.5 %widen.6 = f32[512,8192]{1,0:T(8,128)} custom-call(bf16[512,8192]{1,0:T(8,128)(2,1)} %get-tuple-element.104.x_ref), custom_call_target="tpu_custom_call" | custom-call | flops 4194304 | bytes 25165824 | tf_op jit(solution)/shard_map/widen/pallas_call | solution.py:438
  522.6 9.6 %widen.7 = f32[2048,2048]{1,0:T(8,128)} custom-call(bf16[2048,2048]{1,0:T(8,128)(2,1)} %get-tuple-element.105.x_ref), custom_call_target="tpu_custom_call" | custom-call | flops 4194304 | bytes 25165824 | tf_op jit(solution)/shard_map/widen/pallas_call | solution.py:438
  532.2 0.4 fusion.14
  532.7 3.7 fusion.8
  536.4 0.6 copy.42
  (51 shorter events, 1.7 us)
Async XLA Ops:
  7.2 180.7 %all-gather.2.cloned.1.call-start = ((), (), s32[]{:S(2)}) async-start(), calls=%async_computation.6 | async-start | bytes 7077888 | tf_op jit(solution)/shard_map/all_gather | solution.py:1278
  140.1 31.8 %all-to-all-start = ((bf16[4,384,768]{2,1,0:T(8,128)(2,1)}), bf16[4,384,768]{2,1,0:T(8,128)(2,1)S(1)}, u32[]{:S(2)}, u32[]{:S(2)}) async-start(bf16[4,384,768]{2,1,0:T(8,128)(2,1)} %bitcast.65), calls=%async_computation | async-start | bytes 4718592 | tf_op jit(solution)/shard_map/all_to_all | solution.py:1293
  143.9 168.8 %reduce-scatter.5.cloned.1.call-start = ((), (), s32[]{:S(2)}) async-start(), calls=%async_computation.8 | async-start | bytes 5242880 | tf_op jit(solution)/shard_map/reduce_scatter | solution.py:1317
  145.5 17.6 %copy-start.10 = (s32[16]{0:T(128)}, s32[16]{0:T(128)S(1)}, u32[]{:S(2)}) copy-start(s32[16]{0:T(128)S(1)} %fusion.13.ids_ref) | copy-start | bytes 196
  171.9 1.4 copy-start.5
  187.9 6.2 %copy-start = (bf16[1536,2048]{1,0:T(8,128)(2,1)S(1)}, bf16[1536,2048]{1,0:T(8,128)(2,1)}, u32[]{:S(2)}) copy-start(bf16[1536,2048]{1,0:T(8,128)(2,1)} %all-gather.2.cloned.1.call-done.c_ref) | copy-start | bytes 18874372
  204.4 1.1 copy-start.7
  228.9 22.1 %all-to-all-start.1 = ((bf16[4,384,256]{2,1,0:T(8,128)(2,1)}), bf16[4,384,256]{2,1,0:T(8,128)(2,1)S(1)}, u32[]{:S(2)}, u32[]{:S(2)}) async-start(bf16[4,384,256]{2,1,0:T(8,128)(2,1)} %bitcast.8), calls=%async_computation.1 | async-start | bytes 1572864 | tf_op jit(solution)/shard_map/all_to_all | solution.py:1293
  232.5 300.2 %reduce-scatter.3.cloned.1.call-start = ((), (), s32[]{:S(2)}) async-start(), calls=%async_computation.7 | async-start | bytes 7077888 | tf_op jit(solution)/shard_map/reduce_scatter | solution.py:1327
  251.0 0.9 copy-start.6
  275.0 1.1 copy-start.1
  275.0 1.4 copy-start.2
  275.0 1.8 copy-start.9
  277.0 4.9 copy-start.3
  277.0 32.9 %all-to-all-start.3 = ((bf16[4,384,768]{2,1,0:T(8,128)(2,1)}), bf16[4,384,768]{2,1,0:T(8,128)(2,1)}, u32[]{:S(2)}, u32[]{:S(2)}) async-start(bf16[4,384,768]{2,1,0:T(8,128)(2,1)} %bitcast.62), calls=%async_computation.5 | async-start | bytes 4718592 | tf_op jit(solution)/shard_map/all_to_all | solution.py:1298
  281.9 5.8 %copy-start.11 = (bf16[1536,1024]{1,0:T(8,128)(2,1)S(1)}, bf16[1536,1024]{1,0:T(8,128)(2,1)}, u32[]{:S(2)}) copy-start(bf16[1536,1024]{1,0:T(8,128)(2,1)} %get-tuple-element.92.gh_hbm) | copy-start | bytes 9437188
  501.3 35.0 %copy-start.8 = (f32[512]{0:T(512)}, f32[512]{0:T(512)S(1)}, u32[]{:S(2)}) copy-start(f32[512]{0:T(512)S(1)} %get-tuple-element.150) | copy-start | bytes 6148
  522.6 9.6 %copy-start.4 = (f32[192,2048]{1,0:T(8,128)S(1)}, f32[192,2048]{1,0:T(8,128)}, u32[]{:S(2)}) copy-start(f32[192,2048]{1,0:T(8,128)} %get-tuple-element.100) | copy-start | bytes 4718596
Sparse Core Ops, SparseCore 0:
  121.6 66.2 all-gather.1
  204.5 65.8 reduce-scatter.4
  275.1 67.6 reduce-scatter.2

commit v5 on v4

--- a/solution.py
+++ b/solution.py
@@ -21,7 +21,7 @@
 MESH = pl.DeviceIdType.MESH
 NT = (((1,), (1,)), ((), ()))
 TN = (((0,), (0,)), ((), ()))
-BIG = pltpu.CompilerParams(vmem_limit_bytes=56 * 2**20)
+BIG = pltpu.CompilerParams(vmem_limit_bytes=62 * 2**20)
 
 
 def remote(src, dst, send, recv, target):
@@ -427,24 +427,38 @@
     )(core, mixed, w_dense, active, w_out)
 
 
-def widen(x):
-    rows, cols = x.shape
-    step = min(rows, 128 if cols > 4096 else 512)
-
-    def kernel(x_ref, o_ref):
-        o_ref[...] = x_ref[...].astype(f32)
-
-    part = pl.BlockSpec((step, cols), lambda i: (i, 0))
+def widen(arrays):
+    steps = [min(x.shape[0], 128 if x.shape[1] > 4096 else 512) for x in arrays]
+    counts = [x.shape[0] // step for x, step in zip(arrays, steps)]
+    starts = [sum(counts[:i]) for i in range(len(counts))]
+
+    def kernel(*refs):
+        n = len(arrays)
+        for i in range(n):
+            here = pl.program_id(0) - starts[i]
+
+            @pl.when(jnp.logical_and(here >= 0, here < counts[i]))
+            def _():
+                refs[n + i][...] = refs[i][...].astype(f32)
+
+    def part(i):
+        return pl.BlockSpec(
+            (steps[i], arrays[i].shape[1]),
+            lambda s: (jnp.clip(s - starts[i], 0, counts[i] - 1), 0),
+        )
+
+    specs = [part(i) for i in range(len(arrays))]
+    size = sum(x.size for x in arrays)
     return pl.pallas_call(
         kernel,
-        grid=(rows // step,),
-        in_specs=[part],
-        out_specs=part,
-        out_shape=jax.ShapeDtypeStruct((rows, cols), f32),
+        grid=(sum(counts),),
+        in_specs=specs,
+        out_specs=specs,
+        out_shape=[jax.ShapeDtypeStruct(x.shape, f32) for x in arrays],
         compiler_params=BIG,
-        cost_estimate=cost(rows * cols, 6 * rows * cols),
+        cost_estimate=cost(size, 6 * size),
         name="widen",
-    )(x)
+    )(*arrays)
 
 
 def grad_of_mixed(nz, core, cot, w_dense, hc):
@@ -674,6 +688,101 @@
     )(ids, order, qkv, grad, lse, table)
 
 
+def exchange_heads(nz, nchip, ncore, attended, cot, w_dense, active):
+    rows, width = cot.shape
+    step = rows // nz
+    length, hc = attended.shape
+    part = length // nchip
+    units = active.shape[1]
+    tile = 256
+
+    def kernel(att_ref, cot_hbm, w_hbm, act_hbm, mix_out, g_out, dw_out, cot_ref, w_ref, act_ref, gm_ref, dw_ref,
+               ld, m_s, m_r, g_s, g_r, own_l, dw_l):
+        chip = lax.axis_index("chip")
+        core = lax.axis_index("core")
+        loads = [
+            pltpu.make_async_copy(w_hbm.at[pl.ds(core * hc, hc), :], w_ref, ld.at[0]),
+            pltpu.make_async_copy(cot_hbm, cot_ref, ld.at[1]),
+            pltpu.make_async_copy(act_hbm, act_ref, ld.at[2]),
+        ]
+        for copy in loads:
+            copy.start()
+
+        def chip_at(d):
+            return lax.rem(chip + d, nchip)
+
+        greet([{"chip": chip_at(d)} for d in range(1, nchip)])
+        sent = [
+            remote(
+                att_ref.at[pl.ds(chip_at(d) * part, part), :],
+                mix_out.at[pl.ds(chip * step, step), :], m_s.at[d], m_r.at[d], {"chip": chip_at(d)},
+            )
+            for d in range(1, nchip)
+        ]
+        kept = [
+            pltpu.make_async_copy(
+                att_ref.at[pl.ds(chip * part, part), :], mix_out.at[pl.ds(chip * step, step), :],
+                own_l.at[0],
+            )
+        ]
+        for copy in sent + kept:
+            copy.start()
+        loads[0].wait()
+        loads[1].wait()
+        for d in range(1, nchip + 1):
+            to = chip_at(d)
+            at = pl.ds(pl.multiple_of(to * step, step), step)
+            gm_ref[at, :] = lax.dot_general(
+                cot_ref[at, :], w_ref[...], NT, preferred_element_type=f32
+            ).astype(bf16)
+            there = g_out.at[pl.ds(chip * part, part), :]
+            if d < nchip:
+                copy = remote(gm_ref.at[at, :], there, g_s.at[d], g_r.at[d], {"chip": to})
+                sent.append(copy)
+            else:
+                copy = pltpu.make_async_copy(gm_ref.at[at, :], there, own_l.at[1])
+                kept.append(copy)
+            copy.start()
+        loads[2].wait()
+        for t in range(units // tile):
+            at = pl.ds(t * tile, tile)
+            dw_ref[at, :] = lax.dot_general(
+                act_ref[:, at], cot_ref[...], TN, preferred_element_type=f32
+            ).astype(bf16)
+            copy = pltpu.make_async_copy(dw_ref.at[at, :], dw_out.at[at, :], dw_l.at[t])
+            copy.start()
+            kept.append(copy)
+        for copy in kept + sent:
+            copy.wait()
+
+    dma = pltpu.SemaphoreType.DMA
+    anywhere = pl.BlockSpec(memory_space=pl.ANY)
+    return pl.pallas_call(
+        kernel,
+        in_specs=[anywhere] * 4,
+        out_specs=[anywhere] * 3,
+        out_shape=[
+            jax.ShapeDtypeStruct((rows, hc), bf16),
+            jax.ShapeDtypeStruct((length, hc), bf16),
+            jax.ShapeDtypeStruct((units, width), bf16),
+        ],
+        scratch_shapes=[
+            pltpu.VMEM((rows, width), bf16),
+            pltpu.VMEM((hc, width), bf16),
+            pltpu.VMEM((rows, units), bf16),
+            pltpu.VMEM((rows, hc), bf16),
+            pltpu.VMEM((units, width), bf16),
+            dma((3,)), dma((nchip,)), dma((nchip,)), dma((nchip,)), dma((nchip,)), dma((2,)),
+            dma((units // tile,)),
+        ],
+        compiler_params=pltpu.CompilerParams(
+            collective_id=3, has_side_effects=True, vmem_limit_bytes=62 * 2**20
+        ),
+        cost_estimate=cost(2 * rows * width * (hc + units), 4 * rows * width),
+        name="exchange_heads",
+    )(attended, cot, w_dense, active)
+
+
 def gather_plane(nchip, chip, core, src, dst_of, send, recv, local):
     sibling = {"core": 1 - core}
     rows = src.shape[0]
@@ -1307,27 +1416,27 @@
     qkv, active, slope, normed2 = lax.optimization_barrier((qkv, active, slope, normed2))
     attended, lse = attention_forward(ids_seq, order, qkv, tile)
     attended, cot = lax.optimization_barrier((attended, cot))
-    mixed = heads_back(attended)
-
-    grad_mixed = grad_of_mixed(nz, core_at, cot, w_dense, hc)
-    grad_mixed, cot = lax.optimization_barrier((grad_mixed, cot))
-    g = heads_of(grad_mixed)
-    dw_out = lax.dot_general(active, cot, TN, preferred_element_type=f32).astype(bf16)
-    dw_out, cot = lax.optimization_barrier((dw_out, cot))
+
+    if split == 1:
+        mixed, g, dw_out = exchange_heads(nz, nchip, ncore, attended, cot, w_dense, active)
+    else:
+        mixed = heads_back(attended)
+        g = heads_of(grad_of_mixed(nz, core_at, cot, w_dense, hc))
+        dw_out = lax.dot_general(active, cot, TN, preferred_element_type=f32).astype(bf16)
+    mixed, g, dw_out, cot = lax.optimization_barrier((mixed, g, dw_out, cot))
     s_out = lax.psum_scatter(dw_out, "chip", scatter_dimension=0, tiled=True)
+    part_out = layer_out(nz, core_at, mixed, w_dense, active, w_out)
+    g, part_out = lax.optimization_barrier((g, part_out))
+    dqkv = attention_backward(ids_seq, order, qkv, g, lse, table, tile)
+    dqkv, cot, mixed, part_out = lax.optimization_barrier((dqkv, cot, mixed, part_out))
+    grad_project = heads_back(dqkv)
     grad_hidden, sum_bin = grad_of_hidden(nz, core_at, cot, w_out, slope)
-    g, grad_hidden, mixed = lax.optimization_barrier((g, grad_hidden, mixed))
-    dqkv = attention_backward(ids_seq, order, qkv, g, lse, table, tile)
-    dqkv, mixed, active, cot, grad_hidden = lax.optimization_barrier(
-        (dqkv, mixed, active, cot, grad_hidden)
-    )
-    grad_project = heads_back(dqkv)
-    part_out = layer_out(nz, core_at, mixed, w_dense, active, w_out)
-    part_out, cot, mixed, grad_hidden = lax.optimization_barrier((part_out, cot, mixed, grad_hidden))
-    summed_out = lax.psum_scatter(part_out, TP, scatter_dimension=0, tiled=True).astype(f32)
     dw_in = lax.dot_general(normed2, grad_hidden, TN, preferred_element_type=f32).astype(bf16)
     dw_dense = lax.dot_general(mixed, cot, TN, preferred_element_type=f32).astype(bf16)
-    grad_project, dw_in, dw_dense = lax.optimization_barrier((grad_project, dw_in, dw_dense))
+    grad_project, dw_in, dw_dense, s_out, part_out = lax.optimization_barrier(
+        (grad_project, dw_in, dw_dense, s_out, part_out)
+    )
+    summed_out = lax.psum_scatter(part_out, TP, scatter_dimension=0, tiled=True).astype(f32)
     sum_bqkv = jnp.sum(grad_project.astype(f32), axis=0)
 
     here = jnp.arange(ranks, dtype=jnp.int32) == rank
@@ -1360,7 +1469,7 @@
         - xhat_own * jnp.mean(e * xhat_own, axis=-1, keepdims=True)
     ) * inv_own
     grad_tokens = (cotangent.astype(f32) + terms).astype(bf16)
-    g_wout, g_wdense, g_win, g_wqkv = [widen(g) for g in (g_wout, g_wdense, g_win, g_wqkv)]
+    g_wout, g_wdense, g_win, g_wqkv = widen([g_wout, g_wdense, g_win, g_wqkv])
     return (
         output,
         grad_tokens,

time: 549 us -> 524 us (0.954)
  blocking collectives: 23.5 us -> 0 us
  Pallas kernels: 407 us -> 424 us
  matrix products: 27.1 us -> 16.8 us
    all_to_all x1 -> x0, blocking collectives: 23.5 us -> none  [heads_back(): x = lax.all_to_all(x, 'chip', 0, 0, tiled=True).reshape(rows, g * HD)]
    pallas_call x5 -> x2, Pallas kernels: 37.1 us -> 48.4 us  [the longest x1 27.1 us: widen(): pl.pallas_call(kernel, grid=(sum(counts),), in_specs=specs, out_specs=spe...]
    dot_general x1 -> x0, matrix products: 10.2 us -> none  [on_device(): lax.dot_general(active, cot, TN, preferred_element_type=f32).astype(bf16)]
    reduce_scatter x1, waiting for transfers between devices: 0.01 us -> 7.37 us  [on_device(): s_out = lax.psum_scatter(dw_out, 'chip', scatter_dimension=0, tiled=True)]
    all_to_all x2 -> x1, waiting for transfers between devices: 15.3 us -> 8.7 us  [heads_of(): return lax.all_to_all(x, 'chip', 0, 0, tiled=True).reshape(length, g * HD)]
    all_to_all x1, waiting for transfers between devices: 11 us -> 4.83 us  [heads_back(): x = lax.all_to_all(x, 'chip', 0, 0, tiled=True).reshape(rows, g * HD)]
  transfers between devices with their start and end apart: 6 -> 5, of which waited for: 4 -> 4; matrix products, arithmetic and copies ran while one was open for 6% -> 6% of each run, Pallas kernels for 53% -> 56%
where the time goes in v5:
time: 524 us; the launch traced here: 517 us
  Pallas kernels  424 us (81%)
  waiting for transfers between devices  29.4 us (6%)
  matrix products  16.8 us (3%)
  between operations  14.4 us (3%)
  other arithmetic  11.8 us (2%)
  local copies, waits for them, and re-layouts  11 us (2%)
  starting transfers between devices  9.31 us (2%)
    pallas_call x1, Pallas kernels, tail(): pl.pallas_call(kernel, in_specs=[anywhere] * 3 + [vmem] + [anywhere] * 6...  190 us
    pallas_call x1, Pallas kernels, front(): pl.pallas_call(kernel, in_specs=[anywhere] * 4, out_specs=[anywhere] * 4,...  112 us
    pallas_call x1, Pallas kernels, widen(): pl.pallas_call(kernel, grid=(sum(counts),), in_specs=specs, out_specs=spe...  27.1 us
    pallas_call x1, Pallas kernels, exchange_heads(): pl.pallas_call(kernel, in_specs=[anywhere] * 4, out_specs=[anywhere] * 3,...  21.2 us
    pallas_call x1, Pallas kernels, feed_forward(): pl.pallas_call(kernel, grid=(nz,), in_specs=[part(width), whole((width, c...  16.8 us
    pallas_call x1, Pallas kernels, projections(): pl.pallas_call(kernel, grid_spec=pltpu.PrefetchScalarGridSpec(num_scalar_...  15.3 us
    pallas_call x1, Pallas kernels, layer_out(): pl.pallas_call(kernel, grid_spec=pltpu.PrefetchScalarGridSpec(num_scalar_...  13.1 us
    pallas_call x1, Pallas kernels, grad_of_hidden(): pl.pallas_call(kernel, grid_spec=pltpu.PrefetchScalarGridSpec(num_scalar_...  11.7 us
  transfers between devices with their start and end apart: 5, of which 4 were waited for; matrix products, arithmetic and copies ran while one was open for 6% of the time, Pallas kernels for 56%

profile of v5, /device:TPU:0, one launch (start us, length us, event | category | flops | bytes accessed | tf_op | source)
XLA Modules:
  0.0 517.1 jit_solution(14091398411074833579)
XLA Ops:
  7.2 0.7 convert_bitcast_fusion.7
  7.9 1.4 fusion.12.sm_ref
  9.3 112.1 %front.1 = (bf16[4,2,192,2048]{3,2,1,0:T(8,128)(2,1)}, bf16[2048,1024]{1,0:T(8,128)(2,1)}, bf16[2048,768]{1,0:T(8,128)(2,1)}, bf16[4,64,128]{2,1,0:T(8,128)(2,1)}) custom-call(bf16[192,2048]{1,0:T(8,128)(2,1)} %tok_ref.1, bf16[512,8192]{1,0:T(8,128)(2,1)} %wi_ref.1, bf16[512,6144]{1,0:T(8,128)(2,1)} %wq_ref.1, bf16[64,128]{1,0:T(8,128)(2,1)} %fusion.12.sm_ref), custom_call_target="tpu_custom_call" | custom-call | tf_op jit(solution)/shard_map/front/pallas_call | solution.py:262
  121.5 0.9 copy.40
  122.4 0.1 constant_dynamic-slice_fusion.2
  122.4 0.6 reshape.152.ids_ref
  123.1 0.6 copy.33
  123.7 0.6 copy.32
  124.3 0.6 constant_dynamic-slice_fusion.1
  124.9 15.3 %projections.1 = (bf16[1536,2048]{1,0:T(8,128)(2,1)}, bf16[1536,768]{1,0:T(8,128)(2,1)}) custom-call(s32[16]{0:T(128)} %reshape.152.ids_ref, s32[1]{0:T(128)} %constant.63.clone.1.place_ref, bf16[1536,2048]{1,0:T(8,128)(2,1)} %bitcast.77, bf16[2048,768]{1,0:T(8,128)(2,1)} %get-tuple-element.66.w_ref.wq_hbm, f32[1,768]{1,0:T(1,128)} %bitcast.76, ...), custom_call_target="tpu_custom_call" | custom-call | flops 4831838208 | bytes 15728640 | tf_op jit(solution)/shard_map/projections/pallas_call | solution.py:340
  140.2 4.5 all-to-all-start
  144.7 0.0 reduce-scatter.3.cloned.1.call-start
  144.8 0.6 copy.36
  145.4 0.6 copy.35
  146.0 0.6 constant_dynamic-slice_fusion.b_ref
  146.6 0.6 select_reduce_fusion.order_ref
  147.2 16.8 %feed_forward.1 = (bf16[1536,2048]{1,0:T(8,128)(2,1)}, bf16[1536,1024]{1,0:T(8,128)(2,1)}, bf16[1536,1024]{1,0:T(8,128)(2,1)}) custom-call(bf16[1536,2048]{1,0:T(8,128)(2,1)} %bitcast.78, bf16[2048,1024]{1,0:T(8,128)(2,1)} %get-tuple-element.68.w_ref.wi_hbm, f32[1,1024]{1,0:T(1,128)} %constant_dynamic-slice_fusion.b_ref, f32[1,2048]{1,0:T(1,128)} %bitcast.68, ...), custom_call_target="tpu_custom_call" | custom-call | flops 6442450944 | bytes 16777216 | tf_op jit(solution)/shard_map/feed_forward/pallas_call | solution.py:385
  164.1 8.7 %all-to-all-done = bf16[4,384,768]{2,1,0:T(8,128)(2,1)} async-done(((bf16[4,384,768]{2,1,0:T(8,128)(2,1)}), bf16[4,384,768]{2,1,0:T(8,128)(2,1)}, u32[]{:S(2)}, u32[]{:S(2)}) %all-to-all-start) | async-done | bytes 2359328 | tf_op jit(solution)/shard_map/all_to_all | solution.py:1402
  172.8 6.7 %attention_forward.1 = (bf16[1536,256]{1,0:T(8,128)(2,1)}, f32[1536,1]{1,0:T(8,128)}) custom-call(s32[16]{0:T(128)} %copy-done.5, s32[16]{0:T(128)} %select_reduce_fusion.order_ref, bf16[1536,768]{1,0:T(8,128)(2,1)} %bitcast.6.x_ref), custom_call_target="tpu_custom_call" | custom-call | flops 1389153536 | bytes 3145728 | tf_op jit(solution)/shard_map/attention_forward/pallas_call | solution.py:613
  179.5 8.4 %all-gather.2.cloned.1.call-done.cot_hbm.c_ref = bf16[1536,2048]{1,0:T(8,128)(2,1)} async-done(((bf16[192,2048]{1,0:T(8,128)(2,1)}), bf16[1536,2048]{1,0:T(8,128)(2,1)}) %all-gather.2.cloned.1.call-update) | async-done | bytes 6291472 | tf_op jit(solution)/shard_map/all_gather | solution.py:1387
  187.9 21.2 %exchange_heads.1 = (bf16[1536,256]{1,0:T(8,128)(2,1)}, bf16[1536,256]{1,0:T(8,128)(2,1)}, bf16[1024,2048]{1,0:T(8,128)(2,1)}) custom-call(bf16[1536,256]{1,0:T(8,128)(2,1)} %get-tuple-element.75.att_ref, bf16[1536,2048]{1,0:T(8,128)(2,1)} %all-gather.2.cloned.1.call-done.cot_hbm.c_ref, bf16[512,2048]{1,0:T(8,128)(2,1)} %wd_ref.1, ...), custom_call_target="tpu_custom_call" | custom-call | flops 8053063680 | bytes 12582912 | tf_op jit(solution)/shard_map/exchange_heads/pallas_call | solution.py:760
  209.2 13.1 %layer_out.1 = bf16[1536,2048]{1,0:T(8,128)(2,1)} custom-call(s32[1]{0:T(128)} %bitcast.7.core_ref, bf16[1536,256]{1,0:T(8,128)(2,1)} %get-tuple-element.92.m_ref, bf16[512,2048]{1,0:T(8,128)(2,1)} %wd_ref.1, bf16[1536,1024]{1,0:T(8,128)(2,1)} %get-tuple-element.77.act_hbm.a_ref, bf16[2048,2048]{1,0:T(8,128)(2,1)} %w_ref.1), custom_call_target="tpu_custom_call" | custom-call | flops 8053063680 | bytes 16777216 | tf_op jit(solution)/shard_map/layer_out/pallas_call | solution.py:415
  222.3 10.4 %attention_backward.1 = bf16[1536,768]{1,0:T(8,128)(2,1)} custom-call(s32[16]{0:T(128)} %copy-done.5, s32[16]{0:T(128)} %select_reduce_fusion.order_ref, bf16[1536,768]{1,0:T(8,128)(2,1)} %bitcast.6.x_ref, bf16[1536,256]{1,0:T(8,128)(2,1)} %get-tuple-element.83.g_ref, f32[1536,1]{1,0:T(8,128)} %get-tuple-element.84.lse_ref, f32[3,1536,128]{2,1,0:T(8,128)} %constant.84.clone.t_ref), custom_call_target="tpu_custom_call" | custom-call | flops 3623878656 | bytes 7864320 | tf_op jit(solution)/shard_map/attention_backward/pallas_call | solution.py:677
  232.7 4.7 all-to-all-start.1
  237.4 5.6 %convolution_convert_fusion.1 = bf16[256,2048]{1,0:T(8,128)(2,1)} fusion(bf16[1536,256]{1,0:T(8,128)(2,1)S(1)} %copy-done.2, bf16[1536,2048]{1,0:T(8,128)(2,1)} %all-gather.2.cloned.1.call-done.cot_hbm.c_ref), kind=kOutput, calls=%fused_computation.2 | convolution fusion | flops 1611137024 | bytes 8126464 | tf_op jit(solution)/shard_map/dot_general | solution.py:1435
  243.1 11.7 %grad_of_hidden.1 = (bf16[1536,1024]{1,0:T(8,128)(2,1)}, f32[1,1024]{1,0:T(1,128)}) custom-call(s32[1]{0:T(128)} %bitcast.7.core_ref, bf16[1536,2048]{1,0:T(8,128)(2,1)} %all-gather.2.cloned.1.call-done.cot_hbm.c_ref, bf16[2048,2048]{1,0:T(8,128)(2,1)} %w_ref.1, bf16[1536,1024]{1,0:T(8,128)(2,1)} %get-tuple-element.90.d_ref), custom_call_target="tpu_custom_call" | custom-call | flops 6442450944 | bytes 10485760 | tf_op jit(solution)/shard_map/grad_of_hidden/pallas_call | solution.py:507
  254.8 11.2 %convolution_convert_fusion = bf16[2048,1024]{1,0:T(8,128)(2,1)} fusion(bf16[1536,2048]{1,0:T(8,128)(2,1)} %get-tuple-element.88, bf16[1536,1024]{1,0:T(8,128)(2,1)} %get-tuple-element.91.gh_hbm), kind=kOutput, calls=%fused_computation.1 | convolution fusion | flops 6444548096 | bytes 13631488 | tf_op jit(solution)/shard_map/dot_general | solution.py:1434
  265.9 4.8 all-to-all-done.1
  270.8 7.4 %reduce-scatter.3.cloned.1.call-done.dwo_ref = bf16[256,2048]{1,0:T(8,128)(2,1)} async-done(((bf16[1024,2048]{1,0:T(8,128)(2,1)}), bf16[256,2048]{1,0:T(8,128)(2,1)}) %reduce-scatter.3.cloned.1.call-update) | async-done | bytes 1048592 | tf_op jit(solution)/shard_map/reduce_scatter | solution.py:1427
  278.2 0.1 broadcast_in_dim.75
  278.3 0.1 broadcast_in_dim.76
  278.4 0.9 copy-done
  279.3 0.2 convert_reduce_fusion.1
  279.5 0.1 copy-done.1
  279.5 0.1 convert_reduce_fusion.2
  279.7 0.4 fusion.7
  280.0 0.1 bitcast_select_fusion
  280.1 2.1 convert_reduce_fusion
  282.2 0.1 broadcast_select_fusion
  282.3 0.6 pad_maximum_fusion.vec_ref
  282.9 189.9 %tail.1 = (bf16[2048,2048]{1,0:T(8,128)(2,1)}, bf16[512,2048]{1,0:T(8,128)(2,1)}, bf16[512,8192]{1,0:T(8,128)(2,1)}, bf16[512,6144]{1,0:T(8,128)(2,1)}, f32[192,2048]{1,0:T(8,128)}, /*index=5*/f32[192,128]{1,0:T(8,128)}) custom-call(bf16[256,2048]{1,0:T(8,128)(2,1)} %reduce-scatter.3.cloned.1.call-done.dwo_ref, bf16[4,64,2048]{2,1,0:T(8,128)(2,1)} %bitcast.56, ...), custom_call_target="tpu_custom_call" | custom-call | flops 22548578304 | bytes 62914560 | tf_op jit(solution)/shard_map/tail/pallas_call | solution.py:1281
  472.8 1.4 dynamic_slice.43
  474.2 1.3 dynamic_slice.45
  475.5 1.4 fusion.15
  476.9 27.1 %widen.1 = (f32[2048,2048]{1,0:T(8,128)}, f32[512,2048]{1,0:T(8,128)}, f32[512,8192]{1,0:T(8,128)}, f32[512,6144]{1,0:T(8,128)}) custom-call(bf16[2048,2048]{1,0:T(8,128)(2,1)} %get-tuple-element.104.refs_0_, bf16[512,2048]{1,0:T(8,128)(2,1)} %get-tuple-element.105.refs_1_, bf16[512,8192]{1,0:T(8,128)(2,1)} %get-tuple-element.106.refs_2_, ...), custom_call_target="tpu_custom_call" | custom-call | flops 12582912 | bytes 75497472 | tf_op jit(solution)/shard_map/widen/pallas_call | solution.py:452
  504.0 1.8 fusion.14
  505.9 3.7 fusion.8
  509.6 0.6 copy.42
  (32 shorter events, 0.3 us)
Async XLA Ops:
  7.2 180.7 %all-gather.2.cloned.1.call-start = ((), (), s32[]{:S(2)}) async-start(), calls=%async_computation.4 | async-start | bytes 7077888 | tf_op jit(solution)/shard_map/all_gather | solution.py:1387
  140.2 32.6 %all-to-all-start = ((bf16[4,384,768]{2,1,0:T(8,128)(2,1)}), bf16[4,384,768]{2,1,0:T(8,128)(2,1)}, u32[]{:S(2)}, u32[]{:S(2)}) async-start(bf16[4,384,768]{2,1,0:T(8,128)(2,1)} %bitcast.54), calls=%async_computation | async-start | bytes 4718592 | tf_op jit(solution)/shard_map/all_to_all | solution.py:1402
  144.7 133.5 %reduce-scatter.3.cloned.1.call-start = ((), (), s32[]{:S(2)}) async-start(), calls=%async_computation.5 | async-start | bytes 5242880 | tf_op jit(solution)/shard_map/reduce_scatter | solution.py:1427
  146.0 18.0 %copy-start.5 = (s32[16]{0:T(128)}, s32[16]{0:T(128)S(1)}, u32[]{:S(2)}) copy-start(s32[16]{0:T(128)S(1)} %fusion.13.ids_ref) | copy-start | bytes 196
  232.7 4.7 copy-start.2
  232.7 38.1 %all-to-all-start.1 = ((bf16[4,384,768]{2,1,0:T(8,128)(2,1)}), bf16[4,384,768]{2,1,0:T(8,128)(2,1)}, u32[]{:S(2)}, u32[]{:S(2)}) async-start(bf16[4,384,768]{2,1,0:T(8,128)(2,1)} %bitcast.55), calls=%async_computation.1 | async-start | bytes 4718592 | tf_op jit(solution)/shard_map/all_to_all | solution.py:1407
  237.4 268.5 %reduce-scatter.5.cloned.1.call-start = ((), (), s32[]{:S(2)}) async-start(), calls=%async_computation.6 | async-start | bytes 7077888 | tf_op jit(solution)/shard_map/reduce_scatter | solution.py:1439
  278.1 1.1 copy-start
  278.1 1.4 copy-start.1
  278.2 1.8 copy-start.4
  476.9 32.7 %copy-start.3 = (f32[512]{0:T(512)}, f32[512]{0:T(512)S(1)}, u32[]{:S(2)}) copy-start(f32[512]{0:T(512)S(1)} %get-tuple-element.156) | copy-start | bytes 6148
Sparse Core Ops, SparseCore 0:
  121.6 66.3 all-gather.1
  209.3 68.7 reduce-scatter.2
  280.6 91.4 reduce-scatter.4

commit v6 on v5

--- a/solution.py
+++ b/solution.py
@@ -44,12 +44,13 @@
     heads3 = w_qkv.shape[1]
     nctx = nchip * ncore
     piece = wrows // nctx
+    half = piece // 2
     zi, zq = ff // nz, heads3 // 3 // nz
     ci, cq = zi // ncore, zq // ncore
 
     def kernel(
         tok_ref, wi_ref, wq_ref, sm_ref, tok_out, wi_out, wq_out, sm_out, buf_i, buf_q,
-        up_s, up_r, dn_s, dn_r, sib_s, sib_r, zi_s, zi_r, zq_s, zq_r, pi_s, pi_r, pq_s, pq_r, loc, sm_s, sm_r,
+        up_s, up_r, dn_s, dn_r, sib_s, sib_r, zi_s, zi_r, zq_s, zq_r, p_s, p_r, r_s, loc, loc_p, sm_s, sm_r,
     ):
         z = lax.axis_index("seq")
         chip = lax.axis_index("chip")
@@ -69,44 +70,61 @@
             + [{"chip": plane_at(d)[0], "core": plane_at(d)[1]} for d in range(1, nctx)]
         )
 
-        rows = pl.ds(share * piece, piece)
-        def hop(to):
-            to = jnp.clip(to, 0, nz - 1)
-            copies = [
-                remote(
-                    wi_ref.at[rows, pl.ds(to * zi, zi)], buf_i.at[z], zi_s.at[to], zi_r.at[z],
-                    {"seq": to},
-                )
-            ]
-            for g in range(3):
-                copies.append(
-                    remote(
-                        wq_ref.at[rows, pl.ds(g * zq * nz + to * zq, zq)], buf_q.at[z, g],
-                        zq_s.at[to, g], zq_r.at[z, g], {"seq": to},
-                    )
-                )
-            return copies
-
-        def around(body):
-            for distance in range(1, nz):
+        def around(body, distances=range(1, nz)):
+            for distance in distances:
                 for other in (z + distance, z - distance):
+
                     @pl.when(jnp.logical_and(other >= 0, other < nz))
                     def _():
                         body(jnp.clip(other, 0, nz - 1))
 
+        rows = pl.ds(share * piece, piece)
+
+        def hop(to):
+            pairs = [(wi_ref.at[rows, pl.ds(to * zi, zi)], buf_i.at[z], zi_s.at[to], zi_r.at[z])]
+            for k in range(ncore):
+                for g in range(3):
+                    pairs.append(
+                        (
+                            wq_ref.at[rows, pl.ds(g * zq * nz + to * zq + k * cq, cq)],
+                            buf_q.at[z, k, :, pl.ds(g * cq, cq)],
+                            zq_s.at[to, k, g], zq_r.at[z, k, g],
+                        )
+                    )
+            return pairs
+
+        def hop_to(to):
+            return [remote(a, b, c, d, {"seq": to}) for a, b, c, d in hop(to)]
+
+        def send_hop(to):
+            for copy in hop_to(to):
+                copy.start()
+
+        def hop_left(to):
+            for copy in hop_to(to):
+                copy.wait_send()
+
+        def hop_arrival(source):
+            here = buf_i.at[source]
+            remote(here, here, zi_s.at[0], zi_r.at[source], sibling).wait_recv()
+            for k in range(ncore):
+                for g in range(3):
+                    here = buf_q.at[source, k, :, pl.ds(g * cq, cq)]
+                    remote(here, here, zq_s.at[0, 0, 0], zq_r.at[source, k, g], sibling).wait_recv()
+
         def up(s):
-            shard = z - s
-            src = tok_ref if s == 0 else tok_out.at[jnp.maximum(shard, 0), core]
+            at = jnp.maximum(z - s, 0)
+            src = tok_ref if s == 0 else tok_out.at[at, core]
             return remote(
-                src, tok_out.at[jnp.maximum(shard, 0), core], up_s.at[s], up_r.at[s],
+                src, tok_out.at[at, core], up_s.at[s], up_r.at[s],
                 {"seq": jnp.minimum(z + 1, nz - 1)},
             )
 
         def down(s):
-            shard = z + s
-            src = tok_ref if s == 0 else tok_out.at[jnp.minimum(shard, nz - 1), core]
+            at = jnp.minimum(z + s, nz - 1)
+            src = tok_ref if s == 0 else tok_out.at[at, core]
             return remote(
-                src, tok_out.at[jnp.minimum(shard, nz - 1), core], dn_s.at[s], dn_r.at[s],
+                src, tok_out.at[at, core], dn_s.at[s], dn_r.at[s],
                 {"seq": jnp.maximum(z - 1, 0)},
             )
 
@@ -114,17 +132,130 @@
             src = tok_ref if own_rows else tok_out.at[shard, core]
             return remote(src, tok_out.at[shard, core], sib_s.at[shard], sib_r.at[shard], sibling)
 
+        def token_step(s):
+            @pl.when(z - 1 - s >= 0)
+            def _():
+                shard = jnp.maximum(z - 1 - s, 0)
+                here = tok_out.at[shard, core]
+                remote(here, here, up_s.at[s], up_r.at[s], sibling).wait_recv()
+                if s + 1 < nz - 1:
+
+                    @pl.when(z + 1 < nz)
+                    def _():
+                        up(s + 1).start()
+
+                side(shard).start()
+
+            @pl.when(z + 1 + s < nz)
+            def _():
+                shard = jnp.minimum(z + 1 + s, nz - 1)
+                here = tok_out.at[shard, core]
+                remote(here, here, dn_s.at[s], dn_r.at[s], sibling).wait_recv()
+                if s + 1 < nz - 1:
+
+                    @pl.when(z > 0)
+                    def _():
+                        down(s + 1).start()
+
+                side(shard).start()
+
+        def pieces(source, k):
+            return buf_i.at[source, :, pl.ds(k * ci, ci)], buf_q.at[source, k]
+
+        def places(source, owner):
+            at = pl.ds(source * wrows + owner * piece, piece)
+            return wi_out.at[at, :], wq_out.at[at, :]
+
+        def cut(ref, h):
+            return ref if h is None else ref.at[pl.ds(h * half, half), :]
+
+        def in_place(source):
+            return [
+                pltpu.make_async_copy(a, b, loc_p.at[source, i])
+                for i, (a, b) in enumerate(zip(pieces(source, core), places(source, share)))
+            ]
+
+        if nchip == 4:
+            beside = chip + 1 - 2 * lax.rem(chip, 2)
+            below = lax.rem(chip + 2, 4)
+            across = 3 - chip
+            order = ((beside, 0), (below, 1), (beside, 1), (below, 0))
+
+            def spread(source):
+                copies = []
+                for way, (to, h) in enumerate(order):
+                    for k in range(ncore):
+                        for i, (a, b) in enumerate(zip(pieces(source, k), places(source, share))):
+                            copies.append(
+                                remote(
+                                    cut(a, h), cut(b, h), p_s.at[source, i, k, way],
+                                    p_r.at[source, i, share, h], {"chip": to, "core": k},
+                                )
+                            )
+                return copies
+
+            def relays(source):
+                copies = []
+                for h, (came, to) in enumerate(((beside, below), (below, beside))):
+                    for k in range(ncore):
+                        owner = came * ncore + k
+                        for i, ref in enumerate(places(source, owner)):
+                            part = cut(ref, h)
+                            copies.append(
+                                remote(
+                                    part, part, r_s.at[source, i, k, h],
+                                    p_r.at[source, i, owner, h], {"chip": to},
+                                )
+                            )
+                return copies
+
+            def relay(source):
+                for copy in relays(source):
+                    copy.wait_recv()
+                    copy.start()
+
+            rest = [(beside, 1), (below, 0), (across, 0), (across, 1)]
+        else:
+
+            def spread(source):
+                copies = []
+                for d in range(1, nctx):
+                    to, k = plane_at(d)
+                    for i, (a, b) in enumerate(zip(pieces(source, k), places(source, share))):
+                        copies.append(
+                            remote(
+                                a, b, p_s.at[source, i, 0, d], p_r.at[source, i, share, 0],
+                                {"chip": to, "core": k},
+                            )
+                        )
+                return copies
+
+            def relay(source):
+                pass
+
+        def to_sibling(source):
+            return [
+                remote(a, b, p_s.at[source, i, 0, 4], p_r.at[source, i, share, 0], sibling)
+                for i, (a, b) in enumerate(zip(pieces(source, 1 - core), places(source, share)))
+            ]
+
+        def hand_on(source):
+            for copy in spread(source) + in_place(source):
+                copy.start()
+            if nchip == 4:
+                for copy in to_sibling(source):
+                    copy.start()
+
+        def arrive(source):
+            hop_arrival(source)
+            hand_on(source)
+
         smalls = [
             remote(sm_ref, sm_out.at[z], sm_s.at[d], sm_r.at[z], {"seq": z_at(d)})
             for d in range(1, nz)
         ]
         for copy in smalls:
             copy.start()
-
-        def send_hop(to):
-            for copy in hop(to):
-                copy.start()
-
         around(send_hop)
 
         @pl.when(z + 1 < nz)
@@ -136,88 +267,35 @@
             down(0).start()
 
         side(z, True).start()
-        locals_ = [
+        mine = [
             pltpu.make_async_copy(tok_ref, tok_out.at[z, core], loc.at[0]),
-            pltpu.make_async_copy(wi_ref.at[rows, pl.ds(z * zi, zi)], buf_i.at[z], loc.at[1]),
-            pltpu.make_async_copy(sm_ref, sm_out.at[z], sm_s.at[0]),
-        ] + [
-            pltpu.make_async_copy(
-                wq_ref.at[rows, pl.ds(g * zq * nz + z * zq, zq)], buf_q.at[z, g], loc.at[2 + g]
-            )
-            for g in range(3)
-        ]
-        for copy in locals_:
+            pltpu.make_async_copy(sm_ref, sm_out.at[z], loc.at[1]),
+        ]
+        held = [
+            pltpu.make_async_copy(a, b, loc.at[2 + i]) for i, (a, b, c, d) in enumerate(hop(z))
+        ]
+        for copy in held + mine:
             copy.start()
-
-        def spread(source, d):
-            to_chip, to_core = plane_at(d)
-            target_rows = pl.ds(source * wrows + share * piece, piece)
-            pairs = [
-                (
-                    buf_i.at[source, :, pl.ds(to_core * ci, ci)], wi_out.at[target_rows, :],
-                    pi_s.at[source, d], pi_r.at[source, share],
-                )
-            ] + [
-                (
-                    buf_q.at[source, g, :, pl.ds(to_core * cq, cq)],
-                    wq_out.at[target_rows, pl.ds(g * cq, cq)],
-                    pq_s.at[source, d, g], pq_r.at[source, share, g],
-                )
-                for g in range(3)
-            ]
-            if d == 0:
-                return [pltpu.make_async_copy(a, b, c) for a, b, c, r in pairs]
-            return [remote(a, b, c, r, {"chip": to_chip, "core": to_core}) for a, b, c, r in pairs]
-
-        def hop_arrival(source):
-            remote(buf_i.at[source], buf_i.at[source], zi_s.at[0], zi_r.at[source], sibling).wait_recv()
-            for g in range(3):
-                remote(
-                    buf_q.at[source, g], buf_q.at[source, g], zq_s.at[0, 0], zq_r.at[source, g],
-                    sibling,
-                ).wait_recv()
-
-        for copy in locals_[1:]:
+        for copy in held:
             copy.wait()
-        for d in range(nctx):
-            for copy in spread(z, d):
-                copy.start()
-        def hand_on(source):
-            hop_arrival(source)
-            for d in range(nctx):
-                for copy in spread(source, d):
-                    copy.start()
-
-        around(hand_on)
-
+        hand_on(z)
+        for distance in range(1, nz):
+            around(arrive, [distance])
+            if distance == 1:
+                relay(z)
+            else:
+                around(relay, [distance - 1])
+            token_step(distance - 1)
+        around(relay, [nz - 1])
+
+        for copy in mine:
+            copy.wait()
+        for shard in range(nz):
+            there = tok_out.at[shard, 1 - core]
+            remote(there, there, sib_s.at[shard], sib_r.at[shard], sibling).wait_recv()
+            side(shard).wait_send()
         for s in range(nz - 1):
-            from_below = z - 1 - s
-            from_above = z + 1 + s
-
-            @pl.when(from_below >= 0)
-            def _():
-                shard = jnp.maximum(from_below, 0)
-                remote(tok_ref, tok_out.at[shard, core], up_s.at[s], up_r.at[s], sibling).wait_recv()
-                if s + 1 < nz - 1:
-                    @pl.when(z + 1 < nz)
-                    def _():
-                        up(s + 1).start()
-                side(shard).start()
-
-            @pl.when(from_above < nz)
-            def _():
-                shard = jnp.minimum(from_above, nz - 1)
-                remote(tok_ref, tok_out.at[shard, core], dn_s.at[s], dn_r.at[s], sibling).wait_recv()
-                if s + 1 < nz - 1:
-                    @pl.when(z > 0)
-                    def _():
-                        down(s + 1).start()
-                side(shard).start()
-
-        locals_[0].wait()
-        for shard in range(nz):
-            remote(tok_ref, tok_out.at[shard, 1 - core], sib_s.at[shard], sib_r.at[shard], sibling).wait()
-        for s in range(nz - 1):
+
             @pl.when(jnp.logical_and(z + 1 < nz, z - s >= 0))
             def _():
                 up(s).wait_send()
@@ -225,36 +303,31 @@
             @pl.when(jnp.logical_and(z > 0, z + s < nz))
             def _():
                 down(s).wait_send()
+
+        around(hop_left)
         for copy in smalls:
             copy.wait_send()
-
-        def hop_left(to):
-            for copy in hop(to):
+        for d in range(1, nz):
+            there = sm_out.at[z_at(d)]
+            remote(there, there, sm_s.at[d], sm_r.at[z_at(d)], sibling).wait_recv()
+        for source in range(nz):
+            for copy in in_place(source):
+                copy.wait()
+            for copy in spread(source):
                 copy.wait_send()
-
-        around(hop_left)
-        for d in range(1, nz):
-            other = z_at(d)
-            remote(sm_ref, sm_out.at[other], sm_s.at[d], sm_r.at[other], sibling).wait_recv()
-        for source in range(nz):
-            for d in range(nctx):
-                if d == 0:
-                    for copy in spread(source, d):
-                        copy.wait()
-                    continue
-                for copy in spread(source, d):
+            if nchip == 4:
+                for copy in to_sibling(source) + relays(source):
                     copy.wait_send()
-                other = lax.rem(share + d, nctx)
-                rows_there = pl.ds(source * wrows + other * piece, piece)
-                remote(
-                    wi_out.at[rows_there, :], wi_out.at[rows_there, :], pi_s.at[source, d],
-                    pi_r.at[source, other], sibling,
-                ).wait_recv()
-                for g in range(3):
-                    cols = pl.ds(g * cq, cq)
+                waits = [(chip * ncore + 1 - core, None, 0)] + [
+                    (c * ncore + k, h, h) for c, h in rest for k in range(ncore)
+                ]
+            else:
+                waits = [(lax.rem(share + d, nctx), None, 0) for d in range(1, nctx)]
+            for owner, h, slot in waits:
+                for i, ref in enumerate(places(source, owner)):
+                    part = cut(ref, h)
                     remote(
-                        wq_out.at[rows_there, cols], wq_out.at[rows_there, cols],
-                        pq_s.at[source, d, g], pq_r.at[source, other, g], sibling,
+                        part, part, p_s.at[source, i, 0, 0], p_r.at[source, i, owner, slot], sibling
                     ).wait_recv()
 
     dma = pltpu.SemaphoreType.DMA
@@ -271,14 +344,16 @@
         ],
         scratch_shapes=[
             pltpu.VMEM((nz, piece, zi), bf16),
-            pltpu.VMEM((nz, 3, piece, zq), bf16),
+            pltpu.VMEM((nz, ncore, piece, 3 * cq), bf16),
             dma((nz,)), dma((nz,)), dma((nz,)), dma((nz,)),
             dma((nz,)), dma((nz,)),
-            dma((nz,)), dma((nz,)), dma((nz, 3)), dma((nz, 3)),
-            dma((nz, nctx)), dma((nz, nctx)), dma((nz, nctx, 3)), dma((nz, nctx, 3)),
-            dma((5,)), dma((nz,)), dma((nz,)),
+            dma((nz,)), dma((nz,)), dma((nz, ncore, 3)), dma((nz, ncore, 3)),
+            dma((nz, 2, ncore, max(5, nctx))), dma((nz, 2, nctx, 2)), dma((nz, 2, ncore, 2)),
+            dma((3 + 3 * ncore,)), dma((nz, 2)), dma((nz,)), dma((nz,)),
         ],
-        compiler_params=pltpu.CompilerParams(collective_id=1, has_side_effects=True),
+        compiler_params=pltpu.CompilerParams(
+            collective_id=1, has_side_effects=True, vmem_limit_bytes=62 * 2**20
+        ),
         name="front",
     )(tokens, w_in, w_qkv, small)
 
@@ -1072,6 +1147,7 @@
         for copy in loads[2:] + [load_tok]:
             copy.wait()
         cs[...] = jnp.zeros_like(cs)
+        cs[4:5, : 3 * cq] = jnp.sum(gp_ref[...].astype(f32), axis=0, keepdims=True)
 
         def norm_back(b):
             at = pl.ds(b * step, step)
@@ -1113,6 +1189,18 @@
         for k in range(4):
             for j in range(lanes):
                 v0[k * lanes + j : k * lanes + j + 1, :] = cs[k : k + 1, j * 128 : (j + 1) * 128]
+        rank = z * ncore + core
+        deep = (3 * cq) // 128 // 3
+        for r in range(nz * ncore):
+
+            @pl.when(rank == r)
+            def _():
+                for g in range(3):
+                    for j in range(deep):
+                        row = 4 * lanes + (g * nz * ncore + r) * deep + j
+                        col = g * cq + j * 128
+                        v0[row : row + 1, :] = cs[4:5, col : col + 128]
+
         v_chips = [
             remote(v0, v1.at[chip], v_s.at[d], v_r.at[chip], {"chip": chip_at(d)})
             for d in range(1, nchip)
@@ -1437,14 +1525,11 @@
         (grad_project, dw_in, dw_dense, s_out, part_out)
     )
     summed_out = lax.psum_scatter(part_out, TP, scatter_dimension=0, tiled=True).astype(f32)
-    sum_bqkv = jnp.sum(grad_project.astype(f32), axis=0)
 
     here = jnp.arange(ranks, dtype=jnp.int32) == rank
-    mine_bqkv = jnp.where(here[None, :, None], sum_bqkv.reshape(3, 1, hc), 0.0)
     mine_bin = jnp.where(here[:, None], sum_bin.reshape(1, ffr), 0.0)
     vectors = [
-        jnp.zeros(4 * width, f32),
-        mine_bqkv.reshape(-1),
+        jnp.zeros(7 * width, f32),
         jnp.sum(cotangent.astype(f32), axis=0),
         mine_bin.reshape(-1),
     ]

time: 524 us -> 518 us (0.989)
  transfers between devices with their start and end apart: 5 -> 5, of which waited for: 4 -> 4; matrix products, arithmetic and copies ran while one was open for 6% -> 6% of each run, Pallas kernels for 56% -> 57%
where the time goes in v6:
time: 518 us; the launch traced here: 511 us
  Pallas kernels  424 us (82%)
  waiting for transfers between devices  26.1 us (5%)
  matrix products  16.8 us (3%)
  between operations  14.4 us (3%)
  local copies, waits for them, and re-layouts  11 us (2%)
  other arithmetic  9.74 us (2%)
  starting transfers between devices  9.27 us (2%)
    pallas_call x1, Pallas kernels, tail(): pl.pallas_call(kernel, in_specs=[anywhere] * 3 + [vmem] + [anywhere] * 6...  192 us
    pallas_call x1, Pallas kernels, front(): pl.pallas_call(kernel, in_specs=[anywhere] * 4, out_specs=[anywhere] * 4,...  109 us
    pallas_call x1, Pallas kernels, widen(): pl.pallas_call(kernel, grid=(sum(counts),), in_specs=specs, out_specs=spe...  27.1 us
    pallas_call x1, Pallas kernels, exchange_heads(): pl.pallas_call(kernel, in_specs=[anywhere] * 4, out_specs=[anywhere] * 3,...  21.2 us
    pallas_call x1, Pallas kernels, feed_forward(): pl.pallas_call(kernel, grid=(nz,), in_specs=[part(width), whole((width, c...  16.8 us
    pallas_call x1, Pallas kernels, projections(): pl.pallas_call(kernel, grid_spec=pltpu.PrefetchScalarGridSpec(num_scalar_...  15.8 us
    pallas_call x1, Pallas kernels, layer_out(): pl.pallas_call(kernel, grid_spec=pltpu.PrefetchScalarGridSpec(num_scalar_...  13.1 us
    pallas_call x1, Pallas kernels, grad_of_hidden(): pl.pallas_call(kernel, grid_spec=pltpu.PrefetchScalarGridSpec(num_scalar_...  11.7 us
  transfers between devices with their start and end apart: 5, of which 4 were waited for; matrix products, arithmetic and copies ran while one was open for 6% of the time, Pallas kernels for 57%

profile of v6, /device:TPU:0, one launch (start us, length us, event | category | flops | bytes accessed | tf_op | source)
XLA Modules:
  0.0 511.1 jit_solution(553938216803757317)
XLA Ops:
  7.2 0.0 all-gather.2.cloned.1.call-start
  7.2 0.7 convert_bitcast_fusion.7
  7.9 1.4 fusion.12.sm_ref
  9.3 108.9 %front.1 = (bf16[4,2,192,2048]{3,2,1,0:T(8,128)(2,1)}, bf16[2048,1024]{1,0:T(8,128)(2,1)}, bf16[2048,768]{1,0:T(8,128)(2,1)}, bf16[4,64,128]{2,1,0:T(8,128)(2,1)}) custom-call(bf16[192,2048]{1,0:T(8,128)(2,1)} %tok_ref.1, bf16[512,8192]{1,0:T(8,128)(2,1)} %wi_ref.1, bf16[512,6144]{1,0:T(8,128)(2,1)} %wq_ref.1, bf16[64,128]{1,0:T(8,128)(2,1)} %fusion.12.sm_ref), custom_call_target="tpu_custom_call" | custom-call | tf_op jit(solution)/shard_map/front/pallas_call | solution.py:335
  118.2 0.9 copy.40
  119.1 0.1 constant_dynamic-slice_fusion.2
  119.2 0.6 reshape.142.ids_ref
  119.8 0.6 copy.33
  120.4 0.6 copy.32
  121.1 0.6 constant_dynamic-slice_fusion.1
  121.6 15.8 %projections.1 = (bf16[1536,2048]{1,0:T(8,128)(2,1)}, bf16[1536,768]{1,0:T(8,128)(2,1)}) custom-call(s32[16]{0:T(128)} %reshape.142.ids_ref, s32[1]{0:T(128)} %constant.63.clone.1.place_ref, bf16[1536,2048]{1,0:T(8,128)(2,1)} %bitcast.77, bf16[2048,768]{1,0:T(8,128)(2,1)} %get-tuple-element.66.w_ref.wq_hbm, f32[1,768]{1,0:T(1,128)} %bitcast.76, ...), custom_call_target="tpu_custom_call" | custom-call | flops 4831838208 | bytes 15728640 | tf_op jit(solution)/shard_map/projections/pallas_call | solution.py:415
  137.4 4.5 all-to-all-start
  141.9 0.0 reduce-scatter.3.cloned.1.call-start
  142.1 0.6 copy.36
  142.7 0.6 copy.35
  143.3 0.6 constant_dynamic-slice_fusion.b_ref
  143.9 0.6 select_reduce_fusion.order_ref
  144.5 16.8 %feed_forward.1 = (bf16[1536,2048]{1,0:T(8,128)(2,1)}, bf16[1536,1024]{1,0:T(8,128)(2,1)}, bf16[1536,1024]{1,0:T(8,128)(2,1)}) custom-call(bf16[1536,2048]{1,0:T(8,128)(2,1)} %bitcast.78, bf16[2048,1024]{1,0:T(8,128)(2,1)} %get-tuple-element.68.w_ref.wi_hbm, f32[1,1024]{1,0:T(1,128)} %constant_dynamic-slice_fusion.b_ref, f32[1,2048]{1,0:T(1,128)} %bitcast.68, ...), custom_call_target="tpu_custom_call" | custom-call | flops 6442450944 | bytes 16777216 | tf_op jit(solution)/shard_map/feed_forward/pallas_call | solution.py:460
  161.3 6.5 %all-to-all-done = bf16[4,384,768]{2,1,0:T(8,128)(2,1)} async-done(((bf16[4,384,768]{2,1,0:T(8,128)(2,1)}), bf16[4,384,768]{2,1,0:T(8,128)(2,1)}, u32[]{:S(2)}, u32[]{:S(2)}) %all-to-all-start) | async-done | bytes 2359328 | tf_op jit(solution)/shard_map/all_to_all | solution.py:1490
  167.7 6.7 %attention_forward.1 = (bf16[1536,256]{1,0:T(8,128)(2,1)}, f32[1536,1]{1,0:T(8,128)}) custom-call(s32[16]{0:T(128)} %copy-done.5, s32[16]{0:T(128)} %select_reduce_fusion.order_ref, bf16[1536,768]{1,0:T(8,128)(2,1)} %bitcast.6.x_ref), custom_call_target="tpu_custom_call" | custom-call | flops 1389153536 | bytes 3145728 | tf_op jit(solution)/shard_map/attention_forward/pallas_call | solution.py:688
  174.5 7.4 %all-gather.2.cloned.1.call-done.cot_hbm.c_ref = bf16[1536,2048]{1,0:T(8,128)(2,1)} async-done(((bf16[192,2048]{1,0:T(8,128)(2,1)}), bf16[1536,2048]{1,0:T(8,128)(2,1)}) %all-gather.2.cloned.1.call-update) | async-done | bytes 6291472 | tf_op jit(solution)/shard_map/all_gather | solution.py:1475
  181.9 21.2 %exchange_heads.1 = (bf16[1536,256]{1,0:T(8,128)(2,1)}, bf16[1536,256]{1,0:T(8,128)(2,1)}, bf16[1024,2048]{1,0:T(8,128)(2,1)}) custom-call(bf16[1536,256]{1,0:T(8,128)(2,1)} %get-tuple-element.75.att_ref, bf16[1536,2048]{1,0:T(8,128)(2,1)} %all-gather.2.cloned.1.call-done.cot_hbm.c_ref, bf16[512,2048]{1,0:T(8,128)(2,1)} %wd_ref.1, ...), custom_call_target="tpu_custom_call" | custom-call | flops 8053063680 | bytes 12582912 | tf_op jit(solution)/shard_map/exchange_heads/pallas_call | solution.py:835
  203.1 13.1 %layer_out.1 = bf16[1536,2048]{1,0:T(8,128)(2,1)} custom-call(s32[1]{0:T(128)} %bitcast.7.core_ref, bf16[1536,256]{1,0:T(8,128)(2,1)} %get-tuple-element.92.m_ref, bf16[512,2048]{1,0:T(8,128)(2,1)} %wd_ref.1, bf16[1536,1024]{1,0:T(8,128)(2,1)} %get-tuple-element.77.act_hbm.a_ref, bf16[2048,2048]{1,0:T(8,128)(2,1)} %w_ref.1), custom_call_target="tpu_custom_call" | custom-call | flops 8053063680 | bytes 16777216 | tf_op jit(solution)/shard_map/layer_out/pallas_call | solution.py:490
  216.2 10.4 %attention_backward.1 = bf16[1536,768]{1,0:T(8,128)(2,1)} custom-call(s32[16]{0:T(128)} %copy-done.5, s32[16]{0:T(128)} %select_reduce_fusion.order_ref, bf16[1536,768]{1,0:T(8,128)(2,1)} %bitcast.6.x_ref, bf16[1536,256]{1,0:T(8,128)(2,1)} %get-tuple-element.83.g_ref, f32[1536,1]{1,0:T(8,128)} %get-tuple-element.84.lse_ref, f32[3,1536,128]{2,1,0:T(8,128)} %constant.84.clone.t_ref), custom_call_target="tpu_custom_call" | custom-call | flops 3623878656 | bytes 7864320 | tf_op jit(solution)/shard_map/attention_backward/pallas_call | solution.py:752
  226.7 4.6 all-to-all-start.1
  231.3 0.0 reduce-scatter.5.cloned.1.call-start
  231.4 5.6 %convolution_convert_fusion.1 = bf16[256,2048]{1,0:T(8,128)(2,1)} fusion(bf16[1536,256]{1,0:T(8,128)(2,1)S(1)} %copy-done.2, bf16[1536,2048]{1,0:T(8,128)(2,1)} %all-gather.2.cloned.1.call-done.cot_hbm.c_ref), kind=kOutput, calls=%fused_computation.1 | convolution fusion | flops 1611137024 | bytes 8126464 | tf_op jit(solution)/shard_map/dot_general | solution.py:1523
  237.0 11.7 %grad_of_hidden.1 = (bf16[1536,1024]{1,0:T(8,128)(2,1)}, f32[1,1024]{1,0:T(1,128)}) custom-call(s32[1]{0:T(128)} %bitcast.7.core_ref, bf16[1536,2048]{1,0:T(8,128)(2,1)} %all-gather.2.cloned.1.call-done.cot_hbm.c_ref, bf16[2048,2048]{1,0:T(8,128)(2,1)} %w_ref.1, bf16[1536,1024]{1,0:T(8,128)(2,1)} %get-tuple-element.90.d_ref), custom_call_target="tpu_custom_call" | custom-call | flops 6442450944 | bytes 10485760 | tf_op jit(solution)/shard_map/grad_of_hidden/pallas_call | solution.py:582
  248.7 11.2 %convolution_convert_fusion = bf16[2048,1024]{1,0:T(8,128)(2,1)} fusion(bf16[1536,2048]{1,0:T(8,128)(2,1)} %get-tuple-element.88, bf16[1536,1024]{1,0:T(8,128)(2,1)} %get-tuple-element.91.gh_hbm), kind=kOutput, calls=%fused_computation | convolution fusion | flops 6444548096 | bytes 13631488 | tf_op jit(solution)/shard_map/dot_general | solution.py:1522
  259.9 4.8 all-to-all-done.1
  264.7 7.4 %reduce-scatter.3.cloned.1.call-done.dwo_ref = bf16[256,2048]{1,0:T(8,128)(2,1)} async-done(((bf16[1024,2048]{1,0:T(8,128)(2,1)}), bf16[256,2048]{1,0:T(8,128)(2,1)}) %reduce-scatter.3.cloned.1.call-update) | async-done | bytes 1048592 | tf_op jit(solution)/shard_map/reduce_scatter | solution.py:1515
  272.2 0.1 broadcast_in_dim.50
  272.2 0.1 broadcast_in_dim.51
  272.4 0.9 copy-done
  273.2 0.2 convert_reduce_fusion
  273.4 0.1 copy-done.1
  273.5 0.1 convert_reduce_fusion.1
  273.6 0.4 fusion.7
  274.0 0.1 bitcast_select_fusion
  274.1 0.7 pad_maximum_fusion.vec_ref
  274.8 192.0 %tail.1 = (bf16[2048,2048]{1,0:T(8,128)(2,1)}, bf16[512,2048]{1,0:T(8,128)(2,1)}, bf16[512,8192]{1,0:T(8,128)(2,1)}, bf16[512,6144]{1,0:T(8,128)(2,1)}, f32[192,2048]{1,0:T(8,128)}, /*index=5*/f32[192,128]{1,0:T(8,128)}) custom-call(bf16[256,2048]{1,0:T(8,128)(2,1)} %reduce-scatter.3.cloned.1.call-done.dwo_ref, bf16[4,64,2048]{2,1,0:T(8,128)(2,1)} %bitcast.56, ...), custom_call_target="tpu_custom_call" | custom-call | flops 22548578304 | bytes 62914560 | tf_op jit(solution)/shard_map/tail/pallas_call | solution.py:1369
  466.8 1.4 dynamic_slice.43
  468.2 1.3 dynamic_slice.45
  469.5 1.4 fusion.15
  470.9 27.1 %widen.1 = (f32[2048,2048]{1,0:T(8,128)}, f32[512,2048]{1,0:T(8,128)}, f32[512,8192]{1,0:T(8,128)}, f32[512,6144]{1,0:T(8,128)}) custom-call(bf16[2048,2048]{1,0:T(8,128)(2,1)} %get-tuple-element.104.refs_0_, bf16[512,2048]{1,0:T(8,128)(2,1)} %get-tuple-element.105.refs_1_, bf16[512,8192]{1,0:T(8,128)(2,1)} %get-tuple-element.106.refs_2_, ...), custom_call_target="tpu_custom_call" | custom-call | flops 12582912 | bytes 75497472 | tf_op jit(solution)/shard_map/widen/pallas_call | solution.py:527
  498.0 1.8 fusion.14
  499.9 3.7 fusion.8
  503.6 0.6 copy.42
  (29 shorter events, 0.2 us)
Async XLA Ops:
  7.2 174.7 %all-gather.2.cloned.1.call-start = ((), (), s32[]{:S(2)}) async-start(), calls=%async_computation.4 | async-start | bytes 7077888 | tf_op jit(solution)/shard_map/all_gather | solution.py:1475
  137.4 30.3 %all-to-all-start = ((bf16[4,384,768]{2,1,0:T(8,128)(2,1)}), bf16[4,384,768]{2,1,0:T(8,128)(2,1)}, u32[]{:S(2)}, u32[]{:S(2)}) async-start(bf16[4,384,768]{2,1,0:T(8,128)(2,1)} %bitcast.54), calls=%async_computation | async-start | bytes 4718592 | tf_op jit(solution)/shard_map/all_to_all | solution.py:1490
  141.9 130.1 %reduce-scatter.3.cloned.1.call-start = ((), (), s32[]{:S(2)}) async-start(), calls=%async_computation.5 | async-start | bytes 5242880 | tf_op jit(solution)/shard_map/reduce_scatter | solution.py:1515
  143.3 18.0 %copy-start.5 = (s32[16]{0:T(128)}, s32[16]{0:T(128)S(1)}, u32[]{:S(2)}) copy-start(s32[16]{0:T(128)S(1)} %fusion.13.ids_ref) | copy-start | bytes 196
  226.7 4.7 copy-start.2
  226.7 38.0 %all-to-all-start.1 = ((bf16[4,384,768]{2,1,0:T(8,128)(2,1)}), bf16[4,384,768]{2,1,0:T(8,128)(2,1)}, u32[]{:S(2)}, u32[]{:S(2)}) async-start(bf16[4,384,768]{2,1,0:T(8,128)(2,1)} %bitcast.55), calls=%async_computation.1 | async-start | bytes 4718592 | tf_op jit(solution)/shard_map/all_to_all | solution.py:1495
  231.3 268.5 %reduce-scatter.5.cloned.1.call-start = ((), (), s32[]{:S(2)}) async-start(), calls=%async_computation.6 | async-start | bytes 7077888 | tf_op jit(solution)/shard_map/reduce_scatter | solution.py:1527
  272.1 1.1 copy-start
  272.1 1.4 copy-start.1
  272.1 1.8 copy-start.4
  470.9 32.7 %copy-start.3 = (f32[512]{0:T(512)}, f32[512]{0:T(512)S(1)}, u32[]{:S(2)}) copy-start(f32[512]{0:T(512)S(1)} %get-tuple-element.156) | copy-start | bytes 6148
Sparse Core Ops, SparseCore 0:
  118.3 63.5 all-gather.1
  203.3 68.7 reduce-scatter.2
  274.5 93.5 reduce-scatter.4

commit v7 on v6

--- a/solution.py
+++ b/solution.py
@@ -502,7 +502,7 @@
     )(core, mixed, w_dense, active, w_out)
 
 
-def widen(arrays):
+def widen(arrays, ranks):
     steps = [min(x.shape[0], 128 if x.shape[1] > 4096 else 512) for x in arrays]
     counts = [x.shape[0] // step for x, step in zip(arrays, steps)]
     starts = [sum(counts[:i]) for i in range(len(counts))]
@@ -514,7 +514,14 @@
 
             @pl.when(jnp.logical_and(here >= 0, here < counts[i]))
             def _():
-                refs[n + i][...] = refs[i][...].astype(f32)
+                if i < n - 1:
+                    refs[n + i][...] = refs[i][...].astype(f32)
+                else:
+                    cols = arrays[i].shape[1] // 3 // ranks
+                    for r in range(ranks):
+                        for g in range(3):
+                            to, at = (g * ranks + r) * cols, (3 * r + g) * cols
+                            refs[n + i][:, to : to + cols] = refs[i][:, at : at + cols].astype(f32)
 
     def part(i):
         return pl.BlockSpec(
@@ -1140,9 +1147,9 @@
             ).astype(bf16)
         load_tok = pltpu.make_async_copy(tok_hbm, x_ref, ld.at[5])
         load_tok.start()
-        sum_i[1]()
         sum_q[0]()
         sum_d[0]()
+        sum_i[1]()
 
         for copy in loads[2:] + [load_tok]:
             copy.wait()
@@ -1183,6 +1190,7 @@
         sum_i[2]()
         turn_i = turn(0, lambda to: oi.at[to // hz, 0, lax.rem(to, hz)], ti)
         sum_q[1]()
+        sum_d[1]()
 
         v0[...] = vec_ref[...]
         lanes = width // 128
@@ -1214,8 +1222,8 @@
         gi_at = lambda c, k, s: gi_ref.at[
             pl.ds(c * ri, ri), pl.ds((s * ncore + k) * ci, ci)
         ]
-        gq_at = lambda c, k, s, g: gq_ref.at[
-            pl.ds(c * ri, ri), pl.ds(g * nz * ncore * cq + (s * ncore + k) * cq, cq)
+        gq_at = lambda c, k, s: gq_ref.at[
+            pl.ds(c * ri, ri), pl.ds((s * ncore + k) * 3 * cq, 3 * cq)
         ]
         group = functools.partial(gather_plane, nchip, chip, core)
         rows_o = group(dwo_ref, go_at, go_s, go_r, own_l.at[nz])
@@ -1233,7 +1241,13 @@
 
         sum_q[2]()
         turn_q = turn(1, lambda to: oq.at[to // hz, 0, lax.rem(to, hz)], tq)
-        sum_d[1]()
+        sum_d[2]()
+        rows_d = [
+            group(od.at[h, 0], functools.partial(gd_at, h=h), gd_s.at[h], gd_r.at[h], own_l.at[nz + 1 + h])
+            for h in range(halves)
+        ]
+        for first, onward, pass_on, last in rows_d:
+            first()
 
         for d in range(1, nchip):
             other = chip_at(d)
@@ -1244,6 +1258,10 @@
         v2[core] = total
         v_side = remote(v2.at[core], v2.at[core], v_s.at[nchip], v_r.at[nchip], sibling)
         v_side.start()
+
+        rows_o[1]()
+        for first, onward, pass_on, last in rows_d:
+            onward()
 
         groups = []
         for dz in range(1, nz):
@@ -1277,14 +1295,6 @@
         ]
         for copy in v_zs:
             copy.start()
-        sum_d[2]()
-        rows_d = [
-            group(od.at[h, 0], functools.partial(gd_at, h=h), gd_s.at[h], gd_r.at[h], own_l.at[nz + 1 + h])
-            for h in range(halves)
-        ]
-        for first, onward, pass_on, last in rows_d:
-            first()
-        rows_o[1]()
         for first, onward, pass_on, last in groups:
             onward()
 
@@ -1293,19 +1303,15 @@
         turn_q[-1].wait()
         later = []
         for source in range(nz):
-            for g in range(3):
-                later.append(
-                    group(
-                        tq.at[source, :, pl.ds(g * cq, cq)],
-                        functools.partial(gq_at, s=source, g=g),
-                        gq_s.at[source, g], gq_r.at[source, g], own_l.at[4 + nz + 3 * source + g],
-                    )
+            later.append(
+                group(
+                    tq.at[source], functools.partial(gq_at, s=source), gq_s.at[source],
+                    gq_r.at[source], own_l.at[4 + nz + source],
                 )
+            )
         for first, onward, pass_on, last in later:
             first()
         rows_o[2]()
-        for first, onward, pass_on, last in rows_d:
-            onward()
         for first, onward, pass_on, last in groups:
             pass_on()
         for first, onward, pass_on, last in later:
@@ -1403,8 +1409,8 @@
             dma((slots,)), dma((slots,)),
             dma((halves, slots)), dma((halves, slots)),
             dma((nz, slots)), dma((nz, slots)),
-            dma((nz, 3, slots)), dma((nz, 3, slots)),
-            dma((4 + 4 * nz,)),
+            dma((nz, slots)), dma((nz, slots)),
+            dma((4 + 2 * nz,)),
             dma((nchip + nz,)), dma((nchip + nz + 1,)),
         ],
         compiler_params=pltpu.CompilerParams(
@@ -1554,7 +1560,7 @@
         - xhat_own * jnp.mean(e * xhat_own, axis=-1, keepdims=True)
     ) * inv_own
     grad_tokens = (cotangent.astype(f32) + terms).astype(bf16)
-    g_wout, g_wdense, g_win, g_wqkv = widen([g_wout, g_wdense, g_win, g_wqkv])
+    g_wout, g_wdense, g_win, g_wqkv = widen([g_wout, g_wdense, g_win, g_wqkv], ranks)
     return (
         output,
         grad_tokens,

time: 518 us -> 516 us (level)
  no operation moved by 1% of the time
where the time goes in v7:
time: 516 us; the launch traced here: 510 us
  Pallas kernels  422 us (82%)
  waiting for transfers between devices  26.1 us (5%)
  matrix products  16.8 us (3%)
  between operations  14.4 us (3%)
  local copies, waits for them, and re-layouts  11 us (2%)
  other arithmetic  9.74 us (2%)
  starting transfers between devices  9.27 us (2%)
    pallas_call x1, Pallas kernels, tail(): pl.pallas_call(kernel, in_specs=[anywhere] * 3 + [vmem] + [anywhere] * 6...  191 us
    pallas_call x1, Pallas kernels, front(): pl.pallas_call(kernel, in_specs=[anywhere] * 4, out_specs=[anywhere] * 4,...  109 us
    pallas_call x1, Pallas kernels, widen(): pl.pallas_call(kernel, grid=(sum(counts),), in_specs=specs, out_specs=spe...  27.1 us
    pallas_call x1, Pallas kernels, exchange_heads(): pl.pallas_call(kernel, in_specs=[anywhere] * 4, out_specs=[anywhere] * 3,...  21.2 us
    pallas_call x1, Pallas kernels, feed_forward(): pl.pallas_call(kernel, grid=(nz,), in_specs=[part(width), whole((width, c...  16.8 us
    pallas_call x1, Pallas kernels, projections(): pl.pallas_call(kernel, grid_spec=pltpu.PrefetchScalarGridSpec(num_scalar_...  15.8 us
    pallas_call x1, Pallas kernels, layer_out(): pl.pallas_call(kernel, grid_spec=pltpu.PrefetchScalarGridSpec(num_scalar_...  13.1 us
    pallas_call x1, Pallas kernels, grad_of_hidden(): pl.pallas_call(kernel, grid_spec=pltpu.PrefetchScalarGridSpec(num_scalar_...  11.7 us
  transfers between devices with their start and end apart: 5, of which 4 were waited for; matrix products, arithmetic and copies ran while one was open for 6% of the time, Pallas kernels for 57%

profile of v7, /device:TPU:0, one launch (start us, length us, event | category | flops | bytes accessed | tf_op | source)
XLA Modules:
  0.0 509.7 jit_solution(6124777504388565513)
XLA Ops:
  7.2 0.0 all-gather.2.cloned.1.call-start
  7.2 0.7 convert_bitcast_fusion.7
  7.9 1.4 fusion.12.sm_ref
  9.3 108.9 %front.1 = (bf16[4,2,192,2048]{3,2,1,0:T(8,128)(2,1)}, bf16[2048,1024]{1,0:T(8,128)(2,1)}, bf16[2048,768]{1,0:T(8,128)(2,1)}, bf16[4,64,128]{2,1,0:T(8,128)(2,1)}) custom-call(bf16[192,2048]{1,0:T(8,128)(2,1)} %tok_ref.1, bf16[512,8192]{1,0:T(8,128)(2,1)} %wi_ref.1, bf16[512,6144]{1,0:T(8,128)(2,1)} %wq_ref.1, bf16[64,128]{1,0:T(8,128)(2,1)} %fusion.12.sm_ref), custom_call_target="tpu_custom_call" | custom-call | tf_op jit(solution)/shard_map/front/pallas_call | solution.py:335
  118.2 0.9 copy.40
  119.1 0.1 constant_dynamic-slice_fusion.2
  119.2 0.6 reshape.142.ids_ref
  119.8 0.6 copy.33
  120.4 0.6 copy.32
  121.1 0.6 constant_dynamic-slice_fusion.1
  121.6 15.8 %projections.1 = (bf16[1536,2048]{1,0:T(8,128)(2,1)}, bf16[1536,768]{1,0:T(8,128)(2,1)}) custom-call(s32[16]{0:T(128)} %reshape.142.ids_ref, s32[1]{0:T(128)} %constant.63.clone.1.place_ref, bf16[1536,2048]{1,0:T(8,128)(2,1)} %bitcast.77, bf16[2048,768]{1,0:T(8,128)(2,1)} %get-tuple-element.66.w_ref.wq_hbm, f32[1,768]{1,0:T(1,128)} %bitcast.76, ...), custom_call_target="tpu_custom_call" | custom-call | flops 4831838208 | bytes 15728640 | tf_op jit(solution)/shard_map/projections/pallas_call | solution.py:415
  137.4 4.5 all-to-all-start
  141.9 0.0 reduce-scatter.3.cloned.1.call-start
  142.1 0.6 copy.36
  142.7 0.6 copy.35
  143.3 0.6 constant_dynamic-slice_fusion.b_ref
  143.9 0.6 select_reduce_fusion.order_ref
  144.5 16.8 %feed_forward.1 = (bf16[1536,2048]{1,0:T(8,128)(2,1)}, bf16[1536,1024]{1,0:T(8,128)(2,1)}, bf16[1536,1024]{1,0:T(8,128)(2,1)}) custom-call(bf16[1536,2048]{1,0:T(8,128)(2,1)} %bitcast.78, bf16[2048,1024]{1,0:T(8,128)(2,1)} %get-tuple-element.68.w_ref.wi_hbm, f32[1,1024]{1,0:T(1,128)} %constant_dynamic-slice_fusion.b_ref, f32[1,2048]{1,0:T(1,128)} %bitcast.68, ...), custom_call_target="tpu_custom_call" | custom-call | flops 6442450944 | bytes 16777216 | tf_op jit(solution)/shard_map/feed_forward/pallas_call | solution.py:460
  161.3 6.5 %all-to-all-done = bf16[4,384,768]{2,1,0:T(8,128)(2,1)} async-done(((bf16[4,384,768]{2,1,0:T(8,128)(2,1)}), bf16[4,384,768]{2,1,0:T(8,128)(2,1)}, u32[]{:S(2)}, u32[]{:S(2)}) %all-to-all-start) | async-done | bytes 2359328 | tf_op jit(solution)/shard_map/all_to_all | solution.py:1496
  167.7 6.7 %attention_forward.1 = (bf16[1536,256]{1,0:T(8,128)(2,1)}, f32[1536,1]{1,0:T(8,128)}) custom-call(s32[16]{0:T(128)} %copy-done.5, s32[16]{0:T(128)} %select_reduce_fusion.order_ref, bf16[1536,768]{1,0:T(8,128)(2,1)} %bitcast.6.x_ref), custom_call_target="tpu_custom_call" | custom-call | flops 1389153536 | bytes 3145728 | tf_op jit(solution)/shard_map/attention_forward/pallas_call | solution.py:695
  174.5 7.4 %all-gather.2.cloned.1.call-done.cot_hbm.c_ref = bf16[1536,2048]{1,0:T(8,128)(2,1)} async-done(((bf16[192,2048]{1,0:T(8,128)(2,1)}), bf16[1536,2048]{1,0:T(8,128)(2,1)}) %all-gather.2.cloned.1.call-update) | async-done | bytes 6291472 | tf_op jit(solution)/shard_map/all_gather | solution.py:1481
  181.9 21.2 %exchange_heads.1 = (bf16[1536,256]{1,0:T(8,128)(2,1)}, bf16[1536,256]{1,0:T(8,128)(2,1)}, bf16[1024,2048]{1,0:T(8,128)(2,1)}) custom-call(bf16[1536,256]{1,0:T(8,128)(2,1)} %get-tuple-element.75.att_ref, bf16[1536,2048]{1,0:T(8,128)(2,1)} %all-gather.2.cloned.1.call-done.cot_hbm.c_ref, bf16[512,2048]{1,0:T(8,128)(2,1)} %wd_ref.1, ...), custom_call_target="tpu_custom_call" | custom-call | flops 8053063680 | bytes 12582912 | tf_op jit(solution)/shard_map/exchange_heads/pallas_call | solution.py:842
  203.1 13.1 %layer_out.1 = bf16[1536,2048]{1,0:T(8,128)(2,1)} custom-call(s32[1]{0:T(128)} %bitcast.7.core_ref, bf16[1536,256]{1,0:T(8,128)(2,1)} %get-tuple-element.92.m_ref, bf16[512,2048]{1,0:T(8,128)(2,1)} %wd_ref.1, bf16[1536,1024]{1,0:T(8,128)(2,1)} %get-tuple-element.77.act_hbm.a_ref, bf16[2048,2048]{1,0:T(8,128)(2,1)} %w_ref.1), custom_call_target="tpu_custom_call" | custom-call | flops 8053063680 | bytes 16777216 | tf_op jit(solution)/shard_map/layer_out/pallas_call | solution.py:490
  216.2 10.4 %attention_backward.1 = bf16[1536,768]{1,0:T(8,128)(2,1)} custom-call(s32[16]{0:T(128)} %copy-done.5, s32[16]{0:T(128)} %select_reduce_fusion.order_ref, bf16[1536,768]{1,0:T(8,128)(2,1)} %bitcast.6.x_ref, bf16[1536,256]{1,0:T(8,128)(2,1)} %get-tuple-element.83.g_ref, f32[1536,1]{1,0:T(8,128)} %get-tuple-element.84.lse_ref, f32[3,1536,128]{2,1,0:T(8,128)} %constant.84.clone.t_ref), custom_call_target="tpu_custom_call" | custom-call | flops 3623878656 | bytes 7864320 | tf_op jit(solution)/shard_map/attention_backward/pallas_call | solution.py:759
  226.7 4.6 all-to-all-start.1
  231.3 0.0 reduce-scatter.5.cloned.1.call-start
  231.4 5.6 %convolution_convert_fusion.1 = bf16[256,2048]{1,0:T(8,128)(2,1)} fusion(bf16[1536,256]{1,0:T(8,128)(2,1)S(1)} %copy-done.2, bf16[1536,2048]{1,0:T(8,128)(2,1)} %all-gather.2.cloned.1.call-done.cot_hbm.c_ref), kind=kOutput, calls=%fused_computation.1 | convolution fusion | flops 1611137024 | bytes 8126464 | tf_op jit(solution)/shard_map/dot_general | solution.py:1529
  237.0 11.7 %grad_of_hidden.1 = (bf16[1536,1024]{1,0:T(8,128)(2,1)}, f32[1,1024]{1,0:T(1,128)}) custom-call(s32[1]{0:T(128)} %bitcast.7.core_ref, bf16[1536,2048]{1,0:T(8,128)(2,1)} %all-gather.2.cloned.1.call-done.cot_hbm.c_ref, bf16[2048,2048]{1,0:T(8,128)(2,1)} %w_ref.1, bf16[1536,1024]{1,0:T(8,128)(2,1)} %get-tuple-element.90.d_ref), custom_call_target="tpu_custom_call" | custom-call | flops 6442450944 | bytes 10485760 | tf_op jit(solution)/shard_map/grad_of_hidden/pallas_call | solution.py:589
  248.7 11.2 %convolution_convert_fusion = bf16[2048,1024]{1,0:T(8,128)(2,1)} fusion(bf16[1536,2048]{1,0:T(8,128)(2,1)} %get-tuple-element.88, bf16[1536,1024]{1,0:T(8,128)(2,1)} %get-tuple-element.91.gh_hbm), kind=kOutput, calls=%fused_computation | convolution fusion | flops 6444548096 | bytes 13631488 | tf_op jit(solution)/shard_map/dot_general | solution.py:1528
  259.9 4.8 all-to-all-done.1
  264.7 7.4 %reduce-scatter.3.cloned.1.call-done.dwo_ref = bf16[256,2048]{1,0:T(8,128)(2,1)} async-done(((bf16[1024,2048]{1,0:T(8,128)(2,1)}), bf16[256,2048]{1,0:T(8,128)(2,1)}) %reduce-scatter.3.cloned.1.call-update) | async-done | bytes 1048592 | tf_op jit(solution)/shard_map/reduce_scatter | solution.py:1521
  272.2 0.1 broadcast_in_dim.50
  272.2 0.1 broadcast_in_dim.51
  272.4 0.9 copy-done
  273.2 0.2 convert_reduce_fusion
  273.4 0.1 copy-done.1
  273.5 0.1 convert_reduce_fusion.1
  273.6 0.4 fusion.7
  274.0 0.1 bitcast_select_fusion
  274.1 0.7 pad_maximum_fusion.vec_ref
  274.8 190.6 %tail.1 = (bf16[2048,2048]{1,0:T(8,128)(2,1)}, bf16[512,2048]{1,0:T(8,128)(2,1)}, bf16[512,8192]{1,0:T(8,128)(2,1)}, bf16[512,6144]{1,0:T(8,128)(2,1)}, f32[192,2048]{1,0:T(8,128)}, /*index=5*/f32[192,128]{1,0:T(8,128)}) custom-call(bf16[256,2048]{1,0:T(8,128)(2,1)} %reduce-scatter.3.cloned.1.call-done.dwo_ref, bf16[4,64,2048]{2,1,0:T(8,128)(2,1)} %bitcast.56, ...), custom_call_target="tpu_custom_call" | custom-call | flops 22548578304 | bytes 62914560 | tf_op jit(solution)/shard_map/tail/pallas_call | solution.py:1375
  465.4 1.4 dynamic_slice.43
  466.8 1.3 dynamic_slice.45
  468.0 1.4 fusion.15
  469.4 27.1 %widen.1 = (f32[2048,2048]{1,0:T(8,128)}, f32[512,2048]{1,0:T(8,128)}, f32[512,8192]{1,0:T(8,128)}, f32[512,6144]{1,0:T(8,128)}) custom-call(bf16[2048,2048]{1,0:T(8,128)(2,1)} %get-tuple-element.104.refs_0_, bf16[512,2048]{1,0:T(8,128)(2,1)} %get-tuple-element.105.refs_1_, bf16[512,8192]{1,0:T(8,128)(2,1)} %get-tuple-element.106.refs_2_, ...), custom_call_target="tpu_custom_call" | custom-call | flops 12582912 | bytes 75497472 | tf_op jit(solution)/shard_map/widen/pallas_call | solution.py:534
  496.5 1.8 fusion.14
  498.4 3.7 fusion.8
  502.1 0.6 copy.42
  (29 shorter events, 0.2 us)
Async XLA Ops:
  7.2 174.7 %all-gather.2.cloned.1.call-start = ((), (), s32[]{:S(2)}) async-start(), calls=%async_computation.4 | async-start | bytes 7077888 | tf_op jit(solution)/shard_map/all_gather | solution.py:1481
  137.4 30.3 %all-to-all-start = ((bf16[4,384,768]{2,1,0:T(8,128)(2,1)}), bf16[4,384,768]{2,1,0:T(8,128)(2,1)}, u32[]{:S(2)}, u32[]{:S(2)}) async-start(bf16[4,384,768]{2,1,0:T(8,128)(2,1)} %bitcast.54), calls=%async_computation | async-start | bytes 4718592 | tf_op jit(solution)/shard_map/all_to_all | solution.py:1496
  141.9 130.1 %reduce-scatter.3.cloned.1.call-start = ((), (), s32[]{:S(2)}) async-start(), calls=%async_computation.5 | async-start | bytes 5242880 | tf_op jit(solution)/shard_map/reduce_scatter | solution.py:1521
  143.3 18.0 %copy-start.5 = (s32[16]{0:T(128)}, s32[16]{0:T(128)S(1)}, u32[]{:S(2)}) copy-start(s32[16]{0:T(128)S(1)} %fusion.13.ids_ref) | copy-start | bytes 196
  226.7 4.7 copy-start.2
  226.7 38.0 %all-to-all-start.1 = ((bf16[4,384,768]{2,1,0:T(8,128)(2,1)}), bf16[4,384,768]{2,1,0:T(8,128)(2,1)}, u32[]{:S(2)}, u32[]{:S(2)}) async-start(bf16[4,384,768]{2,1,0:T(8,128)(2,1)} %bitcast.55), calls=%async_computation.1 | async-start | bytes 4718592 | tf_op jit(solution)/shard_map/all_to_all | solution.py:1501
  231.3 267.1 %reduce-scatter.5.cloned.1.call-start = ((), (), s32[]{:S(2)}) async-start(), calls=%async_computation.6 | async-start | bytes 7077888 | tf_op jit(solution)/shard_map/reduce_scatter | solution.py:1533
  272.1 1.1 copy-start
  272.1 1.4 copy-start.1
  272.1 1.8 copy-start.4
  469.4 32.7 %copy-start.3 = (f32[512]{0:T(512)}, f32[512]{0:T(512)S(1)}, u32[]{:S(2)}) copy-start(f32[512]{0:T(512)S(1)} %get-tuple-element.156) | copy-start | bytes 6148
Sparse Core Ops, SparseCore 0:
  118.3 63.5 all-gather.1
  203.3 68.7 reduce-scatter.2
  274.5 71.4 reduce-scatter.4

commit v8 on v7

--- a/solution.py
+++ b/solution.py
@@ -784,14 +784,23 @@
         core = lax.axis_index("core")
         loads = [
             pltpu.make_async_copy(w_hbm.at[pl.ds(core * hc, hc), :], w_ref, ld.at[0]),
-            pltpu.make_async_copy(cot_hbm, cot_ref, ld.at[1]),
-            pltpu.make_async_copy(act_hbm, act_ref, ld.at[2]),
-        ]
-        for copy in loads:
-            copy.start()
+            pltpu.make_async_copy(act_hbm, act_ref, ld.at[1]),
+        ]
 
         def chip_at(d):
             return lax.rem(chip + d, nchip)
+
+        def rows_of(to):
+            return pl.ds(pl.multiple_of(to * step, step), step)
+
+        blocks = [
+            pltpu.make_async_copy(
+                cot_hbm.at[rows_of(chip_at(d)), :], cot_ref.at[rows_of(chip_at(d)), :], ld.at[1 + d]
+            )
+            for d in range(1, nchip + 1)
+        ]
+        for copy in loads[:1] + blocks + loads[1:]:
+            copy.start()
 
         greet([{"chip": chip_at(d)} for d in range(1, nchip)])
         sent = [
@@ -810,10 +819,10 @@
         for copy in sent + kept:
             copy.start()
         loads[0].wait()
-        loads[1].wait()
         for d in range(1, nchip + 1):
             to = chip_at(d)
-            at = pl.ds(pl.multiple_of(to * step, step), step)
+            at = rows_of(to)
+            blocks[d - 1].wait()
             gm_ref[at, :] = lax.dot_general(
                 cot_ref[at, :], w_ref[...], NT, preferred_element_type=f32
             ).astype(bf16)
@@ -825,7 +834,7 @@
                 copy = pltpu.make_async_copy(gm_ref.at[at, :], there, own_l.at[1])
                 kept.append(copy)
             copy.start()
-        loads[2].wait()
+        loads[1].wait()
         for t in range(units // tile):
             at = pl.ds(t * tile, tile)
             dw_ref[at, :] = lax.dot_general(
@@ -854,7 +863,7 @@
             pltpu.VMEM((rows, units), bf16),
             pltpu.VMEM((rows, hc), bf16),
             pltpu.VMEM((units, width), bf16),
-            dma((3,)), dma((nchip,)), dma((nchip,)), dma((nchip,)), dma((nchip,)), dma((2,)),
+            dma((2 + nchip,)), dma((nchip,)), dma((nchip,)), dma((nchip,)), dma((nchip,)), dma((2,)),
             dma((units // tile,)),
         ],
         compiler_params=pltpu.CompilerParams(

time: 516 us -> 516 us (level)
  no operation moved by 1% of the time
where the time goes in v8:
time: 516 us; the launch traced here: 510 us
  Pallas kernels  422 us (82%)
  waiting for transfers between devices  26.1 us (5%)
  matrix products  16.8 us (3%)
  between operations  14.4 us (3%)
  local copies, waits for them, and re-layouts  11 us (2%)
  other arithmetic  9.74 us (2%)
  starting transfers between devices  9.27 us (2%)
    pallas_call x1, Pallas kernels, tail(): pl.pallas_call(kernel, in_specs=[anywhere] * 3 + [vmem] + [anywhere] * 6...  191 us
    pallas_call x1, Pallas kernels, front(): pl.pallas_call(kernel, in_specs=[anywhere] * 4, out_specs=[anywhere] * 4,...  109 us
    pallas_call x1, Pallas kernels, widen(): pl.pallas_call(kernel, grid=(sum(counts),), in_specs=specs, out_specs=spe...  27.1 us
    pallas_call x1, Pallas kernels, exchange_heads(): pl.pallas_call(kernel, in_specs=[anywhere] * 4, out_specs=[anywhere] * 3,...  21.3 us
    pallas_call x1, Pallas kernels, feed_forward(): pl.pallas_call(kernel, grid=(nz,), in_specs=[part(width), whole((width, c...  16.8 us
    pallas_call x1, Pallas kernels, projections(): pl.pallas_call(kernel, grid_spec=pltpu.PrefetchScalarGridSpec(num_scalar_...  15.8 us
    pallas_call x1, Pallas kernels, layer_out(): pl.pallas_call(kernel, grid_spec=pltpu.PrefetchScalarGridSpec(num_scalar_...  13.1 us
    pallas_call x1, Pallas kernels, grad_of_hidden(): pl.pallas_call(kernel, grid_spec=pltpu.PrefetchScalarGridSpec(num_scalar_...  11.7 us
  transfers between devices with their start and end apart: 5, of which 4 were waited for; matrix products, arithmetic and copies ran while one was open for 6% of the time, Pallas kernels for 57%

profile of v8, /device:TPU:0, one launch (start us, length us, event | category | flops | bytes accessed | tf_op | source)
XLA Modules:
  0.0 509.7 jit_solution(3536746363075335275)
XLA Ops:
  7.2 0.0 all-gather.2.cloned.1.call-start
  7.2 0.7 convert_bitcast_fusion.7
  7.9 1.4 fusion.12.sm_ref
  9.3 108.9 %front.1 = (bf16[4,2,192,2048]{3,2,1,0:T(8,128)(2,1)}, bf16[2048,1024]{1,0:T(8,128)(2,1)}, bf16[2048,768]{1,0:T(8,128)(2,1)}, bf16[4,64,128]{2,1,0:T(8,128)(2,1)}) custom-call(bf16[192,2048]{1,0:T(8,128)(2,1)} %tok_ref.1, bf16[512,8192]{1,0:T(8,128)(2,1)} %wi_ref.1, bf16[512,6144]{1,0:T(8,128)(2,1)} %wq_ref.1, bf16[64,128]{1,0:T(8,128)(2,1)} %fusion.12.sm_ref), custom_call_target="tpu_custom_call" | custom-call | tf_op jit(solution)/shard_map/front/pallas_call | solution.py:335
  118.2 0.9 copy.40
  119.1 0.1 constant_dynamic-slice_fusion.2
  119.2 0.6 reshape.142.ids_ref
  119.8 0.6 copy.33
  120.4 0.6 copy.32
  121.1 0.6 constant_dynamic-slice_fusion.1
  121.6 15.8 %projections.1 = (bf16[1536,2048]{1,0:T(8,128)(2,1)}, bf16[1536,768]{1,0:T(8,128)(2,1)}) custom-call(s32[16]{0:T(128)} %reshape.142.ids_ref, s32[1]{0:T(128)} %constant.63.clone.1.place_ref, bf16[1536,2048]{1,0:T(8,128)(2,1)} %bitcast.77, bf16[2048,768]{1,0:T(8,128)(2,1)} %get-tuple-element.66.w_ref.wq_hbm, f32[1,768]{1,0:T(1,128)} %bitcast.76, ...), custom_call_target="tpu_custom_call" | custom-call | flops 4831838208 | bytes 15728640 | tf_op jit(solution)/shard_map/projections/pallas_call | solution.py:415
  137.4 4.5 all-to-all-start
  141.9 0.0 reduce-scatter.3.cloned.1.call-start
  142.1 0.6 copy.36
  142.7 0.6 copy.35
  143.3 0.6 constant_dynamic-slice_fusion.b_ref
  143.9 0.6 select_reduce_fusion.order_ref
  144.5 16.8 %feed_forward.1 = (bf16[1536,2048]{1,0:T(8,128)(2,1)}, bf16[1536,1024]{1,0:T(8,128)(2,1)}, bf16[1536,1024]{1,0:T(8,128)(2,1)}) custom-call(bf16[1536,2048]{1,0:T(8,128)(2,1)} %bitcast.78, bf16[2048,1024]{1,0:T(8,128)(2,1)} %get-tuple-element.68.w_ref.wi_hbm, f32[1,1024]{1,0:T(1,128)} %constant_dynamic-slice_fusion.b_ref, f32[1,2048]{1,0:T(1,128)} %bitcast.68, ...), custom_call_target="tpu_custom_call" | custom-call | flops 6442450944 | bytes 16777216 | tf_op jit(solution)/shard_map/feed_forward/pallas_call | solution.py:460
  161.3 6.5 %all-to-all-done = bf16[4,384,768]{2,1,0:T(8,128)(2,1)} async-done(((bf16[4,384,768]{2,1,0:T(8,128)(2,1)}), bf16[4,384,768]{2,1,0:T(8,128)(2,1)}, u32[]{:S(2)}, u32[]{:S(2)}) %all-to-all-start) | async-done | bytes 2359328 | tf_op jit(solution)/shard_map/all_to_all | solution.py:1505
  167.7 6.7 %attention_forward.1 = (bf16[1536,256]{1,0:T(8,128)(2,1)}, f32[1536,1]{1,0:T(8,128)}) custom-call(s32[16]{0:T(128)} %copy-done.5, s32[16]{0:T(128)} %select_reduce_fusion.order_ref, bf16[1536,768]{1,0:T(8,128)(2,1)} %bitcast.6.x_ref), custom_call_target="tpu_custom_call" | custom-call | flops 1389153536 | bytes 3145728 | tf_op jit(solution)/shard_map/attention_forward/pallas_call | solution.py:695
  174.5 7.4 %all-gather.2.cloned.1.call-done.cot_hbm.c_ref = bf16[1536,2048]{1,0:T(8,128)(2,1)} async-done(((bf16[192,2048]{1,0:T(8,128)(2,1)}), bf16[1536,2048]{1,0:T(8,128)(2,1)}) %all-gather.2.cloned.1.call-update) | async-done | bytes 6291472 | tf_op jit(solution)/shard_map/all_gather | solution.py:1490
  181.9 21.3 %exchange_heads.1 = (bf16[1536,256]{1,0:T(8,128)(2,1)}, bf16[1536,256]{1,0:T(8,128)(2,1)}, bf16[1024,2048]{1,0:T(8,128)(2,1)}) custom-call(bf16[1536,256]{1,0:T(8,128)(2,1)} %get-tuple-element.75.att_ref, bf16[1536,2048]{1,0:T(8,128)(2,1)} %all-gather.2.cloned.1.call-done.cot_hbm.c_ref, bf16[512,2048]{1,0:T(8,128)(2,1)} %wd_ref.1, ...), custom_call_target="tpu_custom_call" | custom-call | flops 8053063680 | bytes 12582912 | tf_op jit(solution)/shard_map/exchange_heads/pallas_call | solution.py:851
  203.2 13.1 %layer_out.1 = bf16[1536,2048]{1,0:T(8,128)(2,1)} custom-call(s32[1]{0:T(128)} %bitcast.7.core_ref, bf16[1536,256]{1,0:T(8,128)(2,1)} %get-tuple-element.92.m_ref, bf16[512,2048]{1,0:T(8,128)(2,1)} %wd_ref.1, bf16[1536,1024]{1,0:T(8,128)(2,1)} %get-tuple-element.77.act_hbm.a_ref, bf16[2048,2048]{1,0:T(8,128)(2,1)} %w_ref.1), custom_call_target="tpu_custom_call" | custom-call | flops 8053063680 | bytes 16777216 | tf_op jit(solution)/shard_map/layer_out/pallas_call | solution.py:490
  216.3 10.4 %attention_backward.1 = bf16[1536,768]{1,0:T(8,128)(2,1)} custom-call(s32[16]{0:T(128)} %copy-done.5, s32[16]{0:T(128)} %select_reduce_fusion.order_ref, bf16[1536,768]{1,0:T(8,128)(2,1)} %bitcast.6.x_ref, bf16[1536,256]{1,0:T(8,128)(2,1)} %get-tuple-element.83.g_ref, f32[1536,1]{1,0:T(8,128)} %get-tuple-element.84.lse_ref, f32[3,1536,128]{2,1,0:T(8,128)} %constant.84.clone.t_ref), custom_call_target="tpu_custom_call" | custom-call | flops 3623878656 | bytes 7864320 | tf_op jit(solution)/shard_map/attention_backward/pallas_call | solution.py:759
  226.7 4.6 all-to-all-start.1
  231.4 0.0 reduce-scatter.5.cloned.1.call-start
  231.4 5.6 %convolution_convert_fusion.1 = bf16[256,2048]{1,0:T(8,128)(2,1)} fusion(bf16[1536,256]{1,0:T(8,128)(2,1)S(1)} %copy-done.2, bf16[1536,2048]{1,0:T(8,128)(2,1)} %all-gather.2.cloned.1.call-done.cot_hbm.c_ref), kind=kOutput, calls=%fused_computation.1 | convolution fusion | flops 1611137024 | bytes 8126464 | tf_op jit(solution)/shard_map/dot_general | solution.py:1538
  237.0 11.7 %grad_of_hidden.1 = (bf16[1536,1024]{1,0:T(8,128)(2,1)}, f32[1,1024]{1,0:T(1,128)}) custom-call(s32[1]{0:T(128)} %bitcast.7.core_ref, bf16[1536,2048]{1,0:T(8,128)(2,1)} %all-gather.2.cloned.1.call-done.cot_hbm.c_ref, bf16[2048,2048]{1,0:T(8,128)(2,1)} %w_ref.1, bf16[1536,1024]{1,0:T(8,128)(2,1)} %get-tuple-element.90.d_ref), custom_call_target="tpu_custom_call" | custom-call | flops 6442450944 | bytes 10485760 | tf_op jit(solution)/shard_map/grad_of_hidden/pallas_call | solution.py:589
  248.8 11.2 %convolution_convert_fusion = bf16[2048,1024]{1,0:T(8,128)(2,1)} fusion(bf16[1536,2048]{1,0:T(8,128)(2,1)} %get-tuple-element.88, bf16[1536,1024]{1,0:T(8,128)(2,1)} %get-tuple-element.91.gh_hbm), kind=kOutput, calls=%fused_computation | convolution fusion | flops 6444548096 | bytes 13631488 | tf_op jit(solution)/shard_map/dot_general | solution.py:1537
  259.9 4.8 all-to-all-done.1
  264.7 7.4 %reduce-scatter.3.cloned.1.call-done.dwo_ref = bf16[256,2048]{1,0:T(8,128)(2,1)} async-done(((bf16[1024,2048]{1,0:T(8,128)(2,1)}), bf16[256,2048]{1,0:T(8,128)(2,1)}) %reduce-scatter.3.cloned.1.call-update) | async-done | bytes 1048592 | tf_op jit(solution)/shard_map/reduce_scatter | solution.py:1530
  272.2 0.1 broadcast_in_dim.50
  272.3 0.1 broadcast_in_dim.51
  272.4 0.9 copy-done
  273.3 0.2 convert_reduce_fusion
  273.4 0.1 copy-done.1
  273.5 0.1 convert_reduce_fusion.1
  273.6 0.4 fusion.7
  274.0 0.1 bitcast_select_fusion
  274.1 0.7 pad_maximum_fusion.vec_ref
  274.8 190.6 %tail.1 = (bf16[2048,2048]{1,0:T(8,128)(2,1)}, bf16[512,2048]{1,0:T(8,128)(2,1)}, bf16[512,8192]{1,0:T(8,128)(2,1)}, bf16[512,6144]{1,0:T(8,128)(2,1)}, f32[192,2048]{1,0:T(8,128)}, /*index=5*/f32[192,128]{1,0:T(8,128)}) custom-call(bf16[256,2048]{1,0:T(8,128)(2,1)} %reduce-scatter.3.cloned.1.call-done.dwo_ref, bf16[4,64,2048]{2,1,0:T(8,128)(2,1)} %bitcast.56, ...), custom_call_target="tpu_custom_call" | custom-call | flops 22548578304 | bytes 62914560 | tf_op jit(solution)/shard_map/tail/pallas_call | solution.py:1384
  465.4 1.4 dynamic_slice.43
  466.8 1.3 dynamic_slice.45
  468.1 1.4 fusion.15
  469.4 27.1 %widen.1 = (f32[2048,2048]{1,0:T(8,128)}, f32[512,2048]{1,0:T(8,128)}, f32[512,8192]{1,0:T(8,128)}, f32[512,6144]{1,0:T(8,128)}) custom-call(bf16[2048,2048]{1,0:T(8,128)(2,1)} %get-tuple-element.104.refs_0_, bf16[512,2048]{1,0:T(8,128)(2,1)} %get-tuple-element.105.refs_1_, bf16[512,8192]{1,0:T(8,128)(2,1)} %get-tuple-element.106.refs_2_, ...), custom_call_target="tpu_custom_call" | custom-call | flops 12582912 | bytes 75497472 | tf_op jit(solution)/shard_map/widen/pallas_call | solution.py:534
  496.6 1.8 fusion.14
  498.4 3.7 fusion.8
  502.1 0.6 copy.42
  (29 shorter events, 0.2 us)
Async XLA Ops:
  7.2 174.7 %all-gather.2.cloned.1.call-start = ((), (), s32[]{:S(2)}) async-start(), calls=%async_computation.4 | async-start | bytes 7077888 | tf_op jit(solution)/shard_map/all_gather | solution.py:1490
  137.4 30.3 %all-to-all-start = ((bf16[4,384,768]{2,1,0:T(8,128)(2,1)}), bf16[4,384,768]{2,1,0:T(8,128)(2,1)}, u32[]{:S(2)}, u32[]{:S(2)}) async-start(bf16[4,384,768]{2,1,0:T(8,128)(2,1)} %bitcast.54), calls=%async_computation | async-start | bytes 4718592 | tf_op jit(solution)/shard_map/all_to_all | solution.py:1505
  141.9 130.2 %reduce-scatter.3.cloned.1.call-start = ((), (), s32[]{:S(2)}) async-start(), calls=%async_computation.5 | async-start | bytes 5242880 | tf_op jit(solution)/shard_map/reduce_scatter | solution.py:1530
  143.3 18.0 %copy-start.5 = (s32[16]{0:T(128)}, s32[16]{0:T(128)S(1)}, u32[]{:S(2)}) copy-start(s32[16]{0:T(128)S(1)} %fusion.13.ids_ref) | copy-start | bytes 196
  226.7 4.7 copy-start.2
  226.7 38.0 %all-to-all-start.1 = ((bf16[4,384,768]{2,1,0:T(8,128)(2,1)}), bf16[4,384,768]{2,1,0:T(8,128)(2,1)}, u32[]{:S(2)}, u32[]{:S(2)}) async-start(bf16[4,384,768]{2,1,0:T(8,128)(2,1)} %bitcast.55), calls=%async_computation.1 | async-start | bytes 4718592 | tf_op jit(solution)/shard_map/all_to_all | solution.py:1510
  231.4 267.1 %reduce-scatter.5.cloned.1.call-start = ((), (), s32[]{:S(2)}) async-start(), calls=%async_computation.6 | async-start | bytes 7077888 | tf_op jit(solution)/shard_map/reduce_scatter | solution.py:1542
  272.1 1.1 copy-start
  272.1 1.4 copy-start.1
  272.2 1.8 copy-start.4
  469.4 32.7 %copy-start.3 = (f32[512]{0:T(512)}, f32[512]{0:T(512)S(1)}, u32[]{:S(2)}) copy-start(f32[512]{0:T(512)S(1)} %get-tuple-element.156) | copy-start | bytes 6148
Sparse Core Ops, SparseCore 0:
  118.3 63.5 all-gather.1
  203.3 68.7 reduce-scatter.2
  274.5 71.4 reduce-scatter.4
